TPU v7x, 512 devices: a whole 4x4x16 slice. The times are simulated.
512 devices in a mesh: dp: 64 (over y, z_lo, core), span: 8 (over x, z_hi).
Axes of the slice: x: 4, y: 4, z: 16 (z_hi: 2, z_lo: 8; z = z_hi * 8 + z_lo), core: 2. Of those that a mesh axis runs over, the one named last changes fastest.
Arguments:
- visual_tower_outputs: bfloat16 [131072, 1152], P(('dp', 'span')), may hold values from -6 to 6
- language_tower_outputs: bfloat16 [131072, 1152], P(('dp', 'span')), may hold values from -24 to 24
- visual_mapping_frozen: bfloat16 [1152, 768], replicated, may hold values from -0.1875 to 0.1875
- language_mapping_learnable: bfloat16 [1152, 768], replicated, may hold values from -0.1875 to 0.1875
- sigmoid_sharpness_array: float32 [1], replicated, may hold values from 30 to 100
- sigmoid_offset_array: float32 [1], replicated, may hold values from -8 to -2
Outputs:
- text_grad: bfloat16 [131072, 1152], P(('dp', 'span'))
- head_grad: float32 [1152, 768], P('dp', 'span')
All inputs are finite; a program needn't handle non-finite values.
Results may differ from a plain program's by a relative error of at most 0.012.
Values may be sent and summed in bfloat16 or wider, within the bound.
No kernel may reach another device: no remote copies, remote signals or barrier semaphores. Data moves between devices by JAX's collectives and lax.ppermute only.
A program may use at most 64 MiB of HBM per device.

v0:
```python
import jax
import jax.numpy as jnp
from jax import lax
from jax.sharding import PartitionSpec as P

EPSILON = 1e-06


def embed(feats, head):
    raw = jnp.dot(feats, head, preferred_element_type=jnp.float32)
    inverse = lax.rsqrt(jnp.sum(raw * raw, axis=-1, keepdims=True) + EPSILON)
    return (raw * inverse, inverse)


def local(
    visual_tower_outputs,
    language_tower_outputs,
    visual_mapping_frozen,
    language_mapping_learnable,
    sigmoid_sharpness_array,
    sigmoid_offset_array,
):
    local_rows = language_tower_outputs.shape[0]
    members = lax.axis_size("span")
    devices = lax.axis_size("dp") * members
    position = lax.axis_index("span")
    video_unit, unused_inv = embed(visual_tower_outputs, visual_mapping_frozen)
    video_emb = video_unit.astype(jnp.bfloat16)
    text_unit, text_inv = embed(language_tower_outputs, language_mapping_learnable)
    text_emb = text_unit.astype(jnp.bfloat16)
    reciprocal_sharpness = sigmoid_sharpness_array[0]
    sigmoid_additive_offset = sigmoid_offset_array[0]
    text_index = position * local_rows + jnp.arange(local_rows, dtype=jnp.int32)
    shard_portion = lax.all_gather(video_emb, "span", axis=0, tiled=True)
    similarity_matrix = (
        reciprocal_sharpness
        * lax.dot_general(
            text_emb, shard_portion, (((1,), (1,)), ((), ())), preferred_element_type=jnp.float32
        )
        + sigmoid_additive_offset
    )
    video_index = jnp.arange(shard_portion.shape[0], dtype=jnp.int32)
    target_sign = jnp.where(text_index[:, None] == video_index[None, :], 1.0, -1.0).astype(
        jnp.float32
    )
    mapping_matrix = (-target_sign * jax.nn.sigmoid(-target_sign * similarity_matrix)).astype(
        jnp.bfloat16
    )
    caption_vector_derivative_matrix = reciprocal_sharpness * jnp.dot(
        mapping_matrix, shard_portion, preferred_element_type=jnp.float32
    )
    inner = jnp.sum(text_unit * caption_vector_derivative_matrix, axis=-1, keepdims=True)
    raw_grad = (text_inv * (caption_vector_derivative_matrix - text_unit * inner)).astype(
        jnp.bfloat16
    )
    text_grad = lax.dot_general(
        raw_grad,
        language_mapping_learnable,
        (((1,), (1,)), ((), ())),
        preferred_element_type=jnp.float32,
    ).astype(jnp.bfloat16)
    local_term = lax.dot_general(
        language_tower_outputs,
        raw_grad,
        (((0,), (0,)), ((), ())),
        preferred_element_type=jnp.float32,
    )
    partial_sum = lax.psum_scatter(local_term, "dp", scatter_dimension=0, tiled=True)
    head_total = lax.psum_scatter(
        partial_sum.astype(jnp.bfloat16), "span", scatter_dimension=1, tiled=True
    ).astype(jnp.float32)
    head_grad = head_total / jnp.float32(devices)
    return (text_grad, head_grad)


def solution(mesh):
    return jax.shard_map(
        local,
        mesh=mesh,
        in_specs=(P(("dp", "span"), None), P(("dp", "span"), None), P(), P(), P(), P()),
        out_specs=(P(("dp", "span"), None), P("dp", "span")),
        check_vma=False,
    )
```

profile of v0, /device:TPU:8, one launch (start us, length us, event | category | flops | bytes accessed | tf_op | source)
XLA Modules:
  0.0 749.4 jit_solution(2722322874617577542)
XLA Ops:
  7.2 0.0 copy-start
  7.2 0.0 copy-start.1
  7.2 0.0 all-gather.2.cloned.1.call-start
  7.2 2.6 multiply_reduce_fusion.1
  9.8 0.9 multiply_convert_fusion.1
  10.7 0.0 all-gather.2.cloned.1.call-update
  10.7 0.0 reduce-scatter.3.cloned.1.call-start
  12.0 1.3 dynamic-slice
  14.0 0.0 copy-done
  14.0 0.0 copy-done.1
  14.0 0.8 multiply_reduce_fusion.2
  14.8 142.9 %all-gather.2.cloned.1.call-done = bf16[2048,768]{1,0:T(8,128)(2,1)} async-done(((bf16[256,768]{1,0:T(8,128)(2,1)}), bf16[2048,768]{1,0:T(8,128)(2,1)}) %all-gather.2.cloned.1.call-update) | async-done | bytes 3145744 | tf_op jit(solution)/shard_map/all_gather | solution.py:34
  157.7 5.8 multiply_reduce_fusion
  163.5 2.1 multiply_convert_fusion
  165.6 3.5 convolution_bitcast_fusion
  169.0 428.8 %all-reduce.2 = bf16[1152,768]{0,1:T(8,128)(2,1)S(1)} all-reduce(f32[1152,768]{0,1:T(8,128)} %convolution_bitcast_fusion), channel_id=2, replica_groups=mesh['dp'=64,'span'=8] {'dp'}, use_global_device_ids=true, to_apply=%region_3.4.clone | all-reduce | flops 884736 | bytes 5308416
  597.9 0.8 dynamic-slice_convert_fusion
  598.7 0.0 reduce-scatter.3.cloned.1.call-update
  598.7 2.5 convolution_convert_fusion
  601.2 139.9 %reduce-scatter.3.cloned.1.call-done = bf16[18,96]{0,1:T(8,128)(2,1)} async-done(((bf16[18,768]{0,1:T(8,128)(2,1)}), bf16[18,96]{0,1:T(8,128)(2,1)}) %reduce-scatter.3.cloned.1.call-update) | async-done | bytes 3472 | tf_op jit(solution)/shard_map/reduce_scatter | solution.py:69
  741.1 0.7 convert_multiply_fusion
  741.9 0.7 copy.9
  (3 shorter events, 0.0 us)
Async XLA Ops:
  7.2 6.8 copy-start
  7.2 6.8 copy-start.1
  7.2 150.5 %all-gather.2.cloned.1.call-start = ((), (), s32[]{:S(2)}) async-start(), calls=%async_computation.1 | async-start | bytes 3538944 | tf_op jit(solution)/shard_map/all_gather | solution.py:34
  10.7 730.4 %reduce-scatter.3.cloned.1.call-start = ((), (), s32[]{:S(2)}) async-start(), calls=%async_computation.2 | async-start | bytes 221184 | tf_op jit(solution)/shard_map/reduce_scatter | solution.py:69
Sparse Core Ops, SparseCore 0:
  11.8 145.8 all-gather.1
  598.8 142.2 reduce-scatter.2
where the time goes:
time: 750 us; the launch traced here: 749 us
  blocking collectives  429 us (57%)
  waiting for transfers between devices  283 us (38%)
  between operations  16 us (2%)
  matrix products  15.1 us (2%)
    unnamed x1, blocking collectives  429 us
    all_gather x1, waiting for transfers between devices, local(): shard_portion = lax.all_gather(video_emb, 'span', axis=0, tiled=True)  143 us
    reduce_scatter x1, waiting for transfers between devices, local(): lax.psum_scatter(partial_sum.astype(jnp.bfloat16), 'span', scatter_dimens...  140 us
  transfers between devices with their start and end apart: 2, of which 2 were waited for; matrix products, arithmetic and copies ran while one was open for 1% of the time, Pallas kernels for 0%

commit v1 on v0

v1 whole, which is shorter than its diff:
```python
import jax
import jax.numpy as jnp
from jax import lax
from jax.sharding import Mesh, PartitionSpec as P

EPSILON = 1e-06
AXES = ("y", "zl", "c", "x", "zh")
SIZES = (4, 8, 2, 4, 2)


def ring(n, step):
    return [(i, (i + step) % n) for i in range(n)]


def embed(feats, head):
    raw = jnp.dot(feats, head, preferred_element_type=jnp.float32)
    inverse = lax.rsqrt(jnp.sum(raw * raw, axis=-1, keepdims=True) + EPSILON)
    return (raw * inverse, inverse)


def local(
    visual_tower_outputs,
    language_tower_outputs,
    visual_mapping_frozen,
    language_mapping_learnable,
    sigmoid_sharpness_array,
    sigmoid_offset_array,
):
    rows, feat = language_tower_outputs.shape
    width = visual_mapping_frozen.shape[1]
    ny, nzl, nc, nx, nzh = SIZES
    devices = ny * nzl * nc * nx * nzh
    piece_r = feat // (ny * nzl * nc)
    piece_c = width // (nx * nzh)
    sharp = sigmoid_sharpness_array[0]
    offset = sigmoid_offset_array[0]
    core = lax.axis_index("c")

    video_unit, unused_inv = embed(visual_tower_outputs, visual_mapping_frozen)
    video_emb = video_unit.astype(jnp.bfloat16)
    across = lax.ppermute(video_emb, "zh", ring(2, 1))
    near = [video_emb] + [lax.ppermute(video_emb, "x", ring(nx, k)) for k in (1, 3, 2)]
    far = [across] + [lax.ppermute(across, "x", ring(nx, k)) for k in (1, 3, 2)]

    text_unit, text_inv = embed(language_tower_outputs, language_mapping_learnable)
    text_emb = text_unit.astype(jnp.bfloat16)

    half = feat // 2
    place = lax.broadcasted_iota(jnp.int32, (half, feat), 0)
    source = lax.broadcasted_iota(jnp.int32, (half, feat), 1)
    start = (place // piece_r) * (2 * piece_r) + place % piece_r

    def columns_of(which):
        pick = (source == start + which * piece_r).astype(jnp.bfloat16)
        return lax.dot_general(
            pick, language_tower_outputs, (((1,), (1,)), ((), ())), preferred_element_type=jnp.float32
        ).astype(jnp.bfloat16)

    mine = columns_of(core)
    theirs = lax.ppermute(columns_of(1 - core), "c", ring(2, 1))

    def part(block, with_diagonal):
        scores = sharp * lax.dot_general(
            text_emb, block, (((1,), (1,)), ((), ())), preferred_element_type=jnp.float32
        ) + offset
        if with_diagonal:
            row = lax.broadcasted_iota(jnp.int32, scores.shape, 0)
            col = lax.broadcasted_iota(jnp.int32, scores.shape, 1)
            sign = jnp.where(row == col, 1.0, -1.0).astype(jnp.float32)
            weight = -sign * jax.nn.sigmoid(-sign * scores)
        else:
            weight = jax.nn.sigmoid(scores)
        return jnp.dot(weight.astype(jnp.bfloat16), block, preferred_element_type=jnp.float32)

    emb_grad = part(jnp.concatenate(near), True)
    emb_grad = sharp * (emb_grad + part(jnp.concatenate(far), False))
    inner = jnp.sum(text_unit * emb_grad, axis=-1, keepdims=True)
    raw_grad = (text_inv * (emb_grad - text_unit * inner)).astype(jnp.bfloat16)

    other = lax.ppermute(raw_grad, "c", ring(2, 1))
    text_grad = lax.dot_general(
        raw_grad, language_mapping_learnable, (((1,), (1,)), ((), ())), preferred_element_type=jnp.float32
    ).astype(jnp.bfloat16)

    term = jnp.dot(mine, raw_grad, preferred_element_type=jnp.float32) + jnp.dot(
        theirs, other, preferred_element_type=jnp.float32
    )
    block_r, block_c = nzl * piece_r, nzh * piece_c
    term = term.astype(jnp.bfloat16).reshape(ny, block_r, nx, block_c).transpose(0, 2, 1, 3)
    term = term.reshape(ny * nx, block_r, block_c)
    term = lax.all_to_all(term, ("y", "x"), 0, 0, tiled=True)
    term = jnp.sum(term.astype(jnp.float32), axis=0).astype(jnp.bfloat16)
    term = term.reshape(nzl, piece_r, nzh, piece_c).transpose(0, 2, 1, 3)
    term = term.reshape(nzl * nzh, piece_r, piece_c)
    term = lax.all_to_all(term, ("zl", "zh"), 0, 0, tiled=True)
    head_grad = jnp.sum(term.astype(jnp.float32), axis=0) / jnp.float32(devices)
    return (text_grad, head_grad)


def solution(mesh):
    fine = Mesh(mesh.devices.reshape(SIZES), AXES)
    pairs = P(("y", "zl", "c", "x", "zh"), None)
    return jax.shard_map(
        local,
        mesh=fine,
        in_specs=(pairs, pairs, P(), P(), P(), P()),
        out_specs=(pairs, P(("y", "zl", "c"), ("x", "zh"))),
        check_vma=False,
    )
```

time: 750 us -> 152 us (0.20)
  the two profiles are of different devices: /device:TPU:8 before, /device:TPU:32 now
where the time goes in v1:
time: 152 us; the launch traced here: 151 us
  starting transfers between devices  52.7 us (35%)
  waiting for transfers between devices  36.9 us (24%)
  blocking collectives  26.2 us (17%)
  matrix products  20.6 us (14%)
  local copies, waits for them, and re-layouts  8.98 us (6%)
  other arithmetic  3.86 us (3%)
  between operations  2.23 us (1%)
    all_to_all x1, blocking collectives, local(): term = lax.all_to_all(term, ('y', 'x'), 0, 0, tiled=True)  26.2 us
    ppermute x1, waiting for transfers between devices, local(): across = lax.ppermute(video_emb, 'zh', ring(2, 1))  20.8 us
    ppermute x1, starting transfers between devices, local(): across = lax.ppermute(video_emb, 'zh', ring(2, 1))  14.8 us
    all_to_all x1, starting transfers between devices, local(): term = lax.all_to_all(term, ('zl', 'zh'), 0, 0, tiled=True)  12 us
    ppermute x3, starting transfers between devices, local(): lax.ppermute(video_emb, 'x', ring(nx, k))  10.8 us
    ppermute x3, starting transfers between devices, local(): far = [across] + [lax.ppermute(across, 'x', ring(nx, k)) for k in (1, 3, 2)]  10.8 us
    all_to_all x1, waiting for transfers between devices, local(): term = lax.all_to_all(term, ('zl', 'zh'), 0, 0, tiled=True)  10.6 us
    dot_general x2, matrix products, part(): jnp.dot(weight.astype(jnp.bfloat16), block, preferred_element_type=jnp.fl...  7.41 us
  transfers between devices with their start and end apart: 10, of which 3 were waited for; matrix products, arithmetic and copies ran while one was open for 11% of the time, Pallas kernels for 0%

profile of v1, /device:TPU:32, one launch (start us, length us, event | category | flops | bytes accessed | tf_op | source)
XLA Modules:
  0.0 151.4 jit_solution(17976911698514323180)
XLA Ops:
  0.7 2.6 %multiply_reduce_fusion.1 = (f32[256]{0:T(256)S(1)}, f32[256,768]{1,0:T(8,128)S(1)}) fusion(bf16[256,1152]{1,0:T(8,128)(2,1)} %param.6, bf16[1152,768]{1,0:T(8,128)(2,1)} %param.8), kind=kOutput, calls=%fused_computation.52 | convolution fusion | flops 453377792 | bytes 3146752 | tf_op jit(solution)/shard_map/dot_general | solution.py:16
  3.2 0.9 multiply_convert_fusion.1
  4.1 14.8 %collective-permute-start.3 = (bf16[256,768]{1,0:T(8,128)(2,1)}, bf16[256,768]{1,0:T(8,128)(2,1)S(1)}, u32[]{:S(2)}, u32[]{:S(2)}) collective-permute-start(bf16[256,768]{1,0:T(8,128)(2,1)} %multiply_convert_fusion.1), channel_id=1, source_target_pairs={{0,1},{1,0},{2,3},{3,2},{4,5},{5,4},{6,7},{7,6},{8,9},{9,8},{10,11... | collective-permute-start | bytes 1179656 | tf_op jit(solution)/shard_map/ppermute | solution.py:41
  18.9 3.4 %collective-permute-start = (bf16[256,768]{1,0:T(8,128)(2,1)}, bf16[256,768]{1,0:T(8,128)(2,1)}, u32[]{:S(2)}, u32[]{:S(2)}) collective-permute-start(bf16[256,768]{1,0:T(8,128)(2,1)} %multiply_convert_fusion.1), channel_id=1, source_target_pairs={{0,2},{2,4},{4,6},{6,0},{1,3},{3,5},{5,7},{7,1},{8,10},{10,12},{12... | collective-permute-start | bytes 1179656 | tf_op jit(solution)/shard_map/ppermute | solution.py:42
  22.3 3.7 %collective-permute-start.1 = (bf16[256,768]{1,0:T(8,128)(2,1)}, bf16[256,768]{1,0:T(8,128)(2,1)}, u32[]{:S(2)}, u32[]{:S(2)}) collective-permute-start(bf16[256,768]{1,0:T(8,128)(2,1)} %multiply_convert_fusion.1), channel_id=1, source_target_pairs={{0,6},{2,0},{4,2},{6,4},{1,7},{3,1},{5,3},{7,5},{8,14},{10,8},{12,... | collective-permute-start | bytes 1179656 | tf_op jit(solution)/shard_map/ppermute | solution.py:42
  26.0 3.7 %collective-permute-start.2 = (bf16[256,768]{1,0:T(8,128)(2,1)}, bf16[256,768]{1,0:T(8,128)(2,1)}, u32[]{:S(2)}, u32[]{:S(2)}) collective-permute-start(bf16[256,768]{1,0:T(8,128)(2,1)} %multiply_convert_fusion.1), channel_id=1, source_target_pairs={{0,4},{2,6},{4,0},{6,2},{1,5},{3,7},{5,1},{7,3},{8,12},{10,14},{12... | collective-permute-start | bytes 1179656 | tf_op jit(solution)/shard_map/ppermute | solution.py:42
  31.0 0.8 multiply_reduce_fusion.2
  32.4 0.6 iota_divide_fusion
  33.0 20.8 %collective-permute-done.3 = bf16[256,768]{1,0:T(8,128)(2,1)S(1)} collective-permute-done((bf16[256,768]{1,0:T(8,128)(2,1)}, bf16[256,768]{1,0:T(8,128)(2,1)S(1)}, u32[]{:S(2)}, u32[]{:S(2)}) %collective-permute-start.3) | collective-permute-done | bytes 393248 | tf_op jit(solution)/shard_map/ppermute | solution.py:41
  53.8 3.4 %collective-permute-start.4 = (bf16[256,768]{1,0:T(8,128)(2,1)S(1)}, bf16[256,768]{1,0:T(8,128)(2,1)}, u32[]{:S(2)}, u32[]{:S(2)}) collective-permute-start(bf16[256,768]{1,0:T(8,128)(2,1)S(1)} %collective-permute-done.3), channel_id=1, source_target_pairs={{0,2},{2,4},{4,6},{6,0},{1,3},{3,5},{5,7},{7,1},{8,10},{10,12},{12... | collective-permute-start | bytes 1179656 | tf_op jit(solution)/shard_map/ppermute | solution.py:43
  57.2 3.7 %collective-permute-start.5 = (bf16[256,768]{1,0:T(8,128)(2,1)S(1)}, bf16[256,768]{1,0:T(8,128)(2,1)S(1)}, u32[]{:S(2)}, u32[]{:S(2)}) collective-permute-start(bf16[256,768]{1,0:T(8,128)(2,1)S(1)} %collective-permute-done.3), channel_id=1, source_target_pairs={{0,6},{2,0},{4,2},{6,4},{1,7},{3,1},{5,3},{7,5},{8,14},{10,8},{12,... | collective-permute-start | bytes 1179656 | tf_op jit(solution)/shard_map/ppermute | solution.py:43
  60.9 3.7 %collective-permute-start.6 = (bf16[256,768]{1,0:T(8,128)(2,1)S(1)}, bf16[256,768]{1,0:T(8,128)(2,1)}, u32[]{:S(2)}, u32[]{:S(2)}) collective-permute-start(bf16[256,768]{1,0:T(8,128)(2,1)S(1)} %collective-permute-done.3), channel_id=1, source_target_pairs={{0,4},{2,6},{4,0},{6,2},{1,5},{3,7},{5,1},{7,3},{8,12},{10,14},{12... | collective-permute-start | bytes 1179656 | tf_op jit(solution)/shard_map/ppermute | solution.py:43
  64.6 4.0 %fusion.36 = f32[256,768]{1,0:T(8,128)} fusion(bf16[256,768]{1,0:T(8,128)(2,1)} %collective-permute-done.2, bf16[256,768]{1,0:T(8,128)(2,1)} %collective-permute-done.1, bf16[256,768]{1,0:T(8,128)(2,1)} %collective-permute-done, bf16[256,768]{1,0:T(8,128)(2,1)} %multiply_convert_fusion.1, f32[]{:T(128)} %bitcast.22, f32[]{:T(128)} %bitcast.21, ...), kind=kOutput, calls=%fused_computation.45 | convolution fusion | flops 821166080 | bytes 3146760 | tf_op jit(solution)/shard_map/dot_general | solution.py:73
  68.6 0.8 constant_dynamic-update-slice_fusion.3
  69.4 1.8 %constant_dynamic-update-slice_fusion.2 = bf16[1024,768]{1,0:T(8,128)(2,1)} fusion(bf16[1024,768]{1,0:T(8,128)(2,1)} %constant_dynamic-update-slice_fusion.3, bf16[256,768]{1,0:T(8,128)(2,1)} %collective-permute-done.4), kind=kLoop, calls=%fused_computation.65 | loop fusion | bytes 786432
  71.2 5.4 %collective-permute-done.5 = bf16[256,768]{1,0:T(8,128)(2,1)S(1)} collective-permute-done((bf16[256,768]{1,0:T(8,128)(2,1)S(1)}, bf16[256,768]{1,0:T(8,128)(2,1)S(1)}, u32[]{:S(2)}, u32[]{:S(2)}) %collective-permute-start.5) | collective-permute-done | bytes 393248 | tf_op jit(solution)/shard_map/ppermute | solution.py:43
  76.6 0.8 constant_dynamic-update-slice_fusion.1
  77.4 1.8 %constant_dynamic-update-slice_fusion = bf16[1024,768]{1,0:T(8,128)(2,1)} fusion(bf16[1024,768]{1,0:T(8,128)(2,1)} %constant_dynamic-update-slice_fusion.1, bf16[256,768]{1,0:T(8,128)(2,1)} %collective-permute-done.6), kind=kLoop, calls=%fused_computation.63 | loop fusion | bytes 786432 | tf_op jit(solution)/shard_map/concatenate | solution.py:76
  79.2 3.4 %multiply_reduce_fusion = (f32[256]{0:T(256)S(1)}, f32[256,768]{1,0:T(8,128)S(1)}) fusion(f32[256,768]{1,0:T(8,128)S(1)} %get-tuple-element.5, f32[256]{0:T(256)S(1)} %add_rsqrt_fusion.1, f32[256,768]{1,0:T(8,128)} %fusion.36, bf16[1024,768]{1,0:T(8,128)(2,1)} %constant_dynamic-update-slice_fusion, f32[]{:T(128)} %bitcast.23, f32[]{:T(128)} %bitcast.20), kind=kOutput, calls=%fused_computation.50 | convolution fusion | flops 808255232 | bytes 3934216 | tf_op jit(solution)/shard_map/dot_general | solution.py:73
  82.7 0.9 multiply_convert_fusion
  83.6 1.9 %collective-permute-start.8 = (bf16[256,768]{1,0:T(8,128)(2,1)}, bf16[256,768]{1,0:T(8,128)(2,1)}, u32[]{:S(2)}, u32[]{:S(2)}) collective-permute-start(bf16[256,768]{1,0:T(8,128)(2,1)} %multiply_convert_fusion), channel_id=1, source_target_pairs={{0,8},{8,0},{1,9},{9,1},{2,10},{10,2},{3,11},{11,3},{4,12},{12,4},... | collective-permute-start | bytes 1179656 | tf_op jit(solution)/shard_map/ppermute | solution.py:80
  85.6 2.2 %fusion.33 = bf16[576,256]{1,0:T(8,128)(2,1)} fusion(bf16[256,1152]{1,0:T(8,128)(2,1)S(1)} %copy-done.2, s32[]{:T(128)S(6)} %mul.95, s32[576]{0:T(1024)S(1)} %copy-done.4, s32[576]{0:T(1024)S(1)} %get-tuple-element.10, s32[576]{0:T(1024)S(1)} %copy-done.3, s32[576]{0:T(1024)S(1)} %get-tuple-element.11, pred[576]{0:T(1024)(128)(4,1)S(1)} %copy-done.6, ...), kind=kOutput, calls=%fused_computation.42 | convolution fusion | flops 343867392 | bytes 895108 | tf_op jit(solution)/shard_map/dot_general | solution.py:55
  87.8 2.4 %collective-permute-start.7 = (bf16[576,256]{1,0:T(8,128)(2,1)}, bf16[576,256]{1,0:T(8,128)(2,1)}, u32[]{:S(2)}, u32[]{:S(2)}) collective-permute-start(bf16[576,256]{1,0:T(8,128)(2,1)} %fusion.33), channel_id=1, source_target_pairs={{0,8},{8,0},{1,9},{9,1},{2,10},{10,2},{3,11},{11,3},{4,12},{12,4},... | collective-permute-start | bytes 884744 | tf_op jit(solution)/shard_map/ppermute | solution.py:60
  90.2 2.7 %fusion.35 = f32[576,768]{1,0:T(8,128)S(1)} fusion(bf16[256,768]{1,0:T(8,128)(2,1)} %multiply_convert_fusion, bf16[256,1152]{1,0:T(8,128)(2,1)} %param.7, s32[]{:T(128)S(6)} %mul.94, s32[576]{0:T(1024)S(1)} %copy-done.5, s32[576]{0:T(1024)S(1)} %get-tuple-element.10, s32[576]{0:T(1024)S(1)} %copy-done.3, s32[576]{0:T(1024)S(1)} %get-tuple-element.11, ...), kind=kOutput, calls=%fused_computation.44 | convolution fusion | flops 570359808 | bytes 2762884 | tf_op jit(solution)/shard_map/dot_general | solution.py:85
  92.9 2.4 %add_convert_fusion = bf16[576,768]{1,0:T(8,128)(2,1)} fusion(f32[576,768]{1,0:T(8,128)S(1)} %fusion.35, bf16[576,256]{1,0:T(8,128)(2,1)} %collective-permute-done.7, bf16[256,768]{1,0:T(8,128)(2,1)} %collective-permute-done.8), kind=kOutput, calls=%fused_computation.6 | convolution fusion | flops 227377152 | bytes 3342336 | tf_op jit(solution)/shard_map/dot_general | solution.py:85
  95.4 2.9 %reshape.29 = bf16[4,144,4,192]{3,2,1,0:T(4,128)(2,1)S(1)} reshape(bf16[576,768]{1,0:T(8,128)(2,1)} %add_convert_fusion) | data formatting | bytes 1769472 | tf_op jit(solution)/shard_map/reshape | solution.py:89
  98.4 26.2 %all_to_all.10 = bf16[16,144,192]{2,1,0:T(8,128)(2,1)S(1)} all-to-all(bf16[16,144,192]{2,1,0:T(8,128)(2,1)S(1)} %bitcast.24), channel_id=1, replica_groups=mesh['y'=4,'zl'=8,'c'=2,'x'=4,'zh'=2] {'y','x'}, dimensions={0} | all-to-all | bytes 1769472 | tf_op jit(solution)/shard_map/all_to_all | solution.py:91
  124.9 0.7 copy.13
  125.6 12.0 %all-to-all-start.1 = ((bf16[16,18,96]{2,1,0:T(8,128)(2,1)}), bf16[16,18,96]{2,1,0:T(8,128)(2,1)S(1)}, u32[]{:S(2)}, u32[]{:S(2)}) async-start(bf16[16,18,96]{2,1,0:T(8,128)(2,1)} %copy.13), calls=%async_computation.1 | async-start | bytes 196608 | tf_op jit(solution)/shard_map/all_to_all | solution.py:95
  137.6 2.5 %convolution_convert_fusion = bf16[256,1152]{1,0:T(8,128)(2,1)} fusion(bf16[256,768]{1,0:T(8,128)(2,1)} %multiply_convert_fusion, bf16[1152,768]{1,0:T(8,128)(2,1)S(1)} %copy-done), kind=kOutput, calls=%fused_computation.5 | convolution fusion | flops 453279744 | bytes 2752512 | tf_op jit(solution)/shard_map/dot_general | solution.py:81
  140.1 10.6 %all-to-all-done.1 = bf16[16,18,96]{2,1,0:T(8,128)(2,1)S(1)} async-done(((bf16[16,18,96]{2,1,0:T(8,128)(2,1)}), bf16[16,18,96]{2,1,0:T(8,128)(2,1)S(1)}, u32[]{:S(2)}, u32[]{:S(2)}) %all-to-all-start.1) | async-done | bytes 55328 | tf_op jit(solution)/shard_map/all_to_all | solution.py:95
  150.8 0.6 broadcast_multiply_fusion
  (32 shorter events, 1.2 us)
Async XLA Ops:
  0.6 30.4 %copy-start = (bf16[1152,768]{1,0:T(8,128)(2,1)S(1)}, bf16[1152,768]{1,0:T(8,128)(2,1)}, u32[]{:S(2)}) copy-start(bf16[1152,768]{1,0:T(8,128)(2,1)} %param.9) | copy-start | bytes 5308420
  0.6 30.4 %copy-start.1 = (bf16[256,1152]{1,0:T(8,128)(2,1)S(1)}, bf16[256,1152]{1,0:T(8,128)(2,1)}, u32[]{:S(2)}) copy-start(bf16[256,1152]{1,0:T(8,128)(2,1)} %param.7) | copy-start | bytes 1769476
  4.1 49.7 %collective-permute-start.3 = (bf16[256,768]{1,0:T(8,128)(2,1)}, bf16[256,768]{1,0:T(8,128)(2,1)S(1)}, u32[]{:S(2)}, u32[]{:S(2)}) collective-permute-start(bf16[256,768]{1,0:T(8,128)(2,1)} %multiply_convert_fusion.1), channel_id=1, source_target_pairs={{0,1},{1,0},{2,3},{3,2},{4,5},{5,4},{6,7},{7,6},{8,9},{9,8},{10,11... | collective-permute-start | bytes 1179656 | tf_op jit(solution)/shard_map/ppermute | solution.py:41
  18.9 42.0 %collective-permute-start = (bf16[256,768]{1,0:T(8,128)(2,1)}, bf16[256,768]{1,0:T(8,128)(2,1)}, u32[]{:S(2)}, u32[]{:S(2)}) collective-permute-start(bf16[256,768]{1,0:T(8,128)(2,1)} %multiply_convert_fusion.1), channel_id=1, source_target_pairs={{0,2},{2,4},{4,6},{6,0},{1,3},{3,5},{5,7},{7,1},{8,10},{10,12},{12... | collective-permute-start | bytes 1179656 | tf_op jit(solution)/shard_map/ppermute | solution.py:42
  22.3 42.3 %collective-permute-start.1 = (bf16[256,768]{1,0:T(8,128)(2,1)}, bf16[256,768]{1,0:T(8,128)(2,1)}, u32[]{:S(2)}, u32[]{:S(2)}) collective-permute-start(bf16[256,768]{1,0:T(8,128)(2,1)} %multiply_convert_fusion.1), channel_id=1, source_target_pairs={{0,6},{2,0},{4,2},{6,4},{1,7},{3,1},{5,3},{7,5},{8,14},{10,8},{12,... | collective-permute-start | bytes 1179656 | tf_op jit(solution)/shard_map/ppermute | solution.py:42
  26.0 38.6 %collective-permute-start.2 = (bf16[256,768]{1,0:T(8,128)(2,1)}, bf16[256,768]{1,0:T(8,128)(2,1)}, u32[]{:S(2)}, u32[]{:S(2)}) collective-permute-start(bf16[256,768]{1,0:T(8,128)(2,1)} %multiply_convert_fusion.1), channel_id=1, source_target_pairs={{0,4},{2,6},{4,0},{6,2},{1,5},{3,7},{5,1},{7,3},{8,12},{10,14},{12... | collective-permute-start | bytes 1179656 | tf_op jit(solution)/shard_map/ppermute | solution.py:42
  53.8 15.6 %collective-permute-start.4 = (bf16[256,768]{1,0:T(8,128)(2,1)S(1)}, bf16[256,768]{1,0:T(8,128)(2,1)}, u32[]{:S(2)}, u32[]{:S(2)}) collective-permute-start(bf16[256,768]{1,0:T(8,128)(2,1)S(1)} %collective-permute-done.3), channel_id=1, source_target_pairs={{0,2},{2,4},{4,6},{6,0},{1,3},{3,5},{5,7},{7,1},{8,10},{10,12},{12... | collective-permute-start | bytes 1179656 | tf_op jit(solution)/shard_map/ppermute | solution.py:43
  57.2 19.4 %collective-permute-start.5 = (bf16[256,768]{1,0:T(8,128)(2,1)S(1)}, bf16[256,768]{1,0:T(8,128)(2,1)S(1)}, u32[]{:S(2)}, u32[]{:S(2)}) collective-permute-start(bf16[256,768]{1,0:T(8,128)(2,1)S(1)} %collective-permute-done.3), channel_id=1, source_target_pairs={{0,6},{2,0},{4,2},{6,4},{1,7},{3,1},{5,3},{7,5},{8,14},{10,8},{12,... | collective-permute-start | bytes 1179656 | tf_op jit(solution)/shard_map/ppermute | solution.py:43
  60.9 16.5 %collective-permute-start.6 = (bf16[256,768]{1,0:T(8,128)(2,1)S(1)}, bf16[256,768]{1,0:T(8,128)(2,1)}, u32[]{:S(2)}, u32[]{:S(2)}) collective-permute-start(bf16[256,768]{1,0:T(8,128)(2,1)S(1)} %collective-permute-done.3), channel_id=1, source_target_pairs={{0,4},{2,6},{4,0},{6,2},{1,5},{3,7},{5,1},{7,3},{8,12},{10,14},{12... | collective-permute-start | bytes 1179656 | tf_op jit(solution)/shard_map/ppermute | solution.py:43
  82.6 2.9 %copy-start.2 = (bf16[256,1152]{1,0:T(8,128)(2,1)S(1)}, bf16[256,1152]{1,0:T(8,128)(2,1)}, u32[]{:S(2)}) copy-start(bf16[256,1152]{1,0:T(8,128)(2,1)} %param.7) | copy-start | bytes 1769476
  82.6 2.9 %copy-start.3 = (s32[576]{0:T(1024)S(1)}, s32[576]{0:T(1024)}, u32[]{:S(2)}) copy-start(s32[576]{0:T(1024)} %get-tuple-element.8) | copy-start | bytes 6916
  82.6 2.9 %copy-start.4 = (s32[576]{0:T(1024)S(1)}, s32[576]{0:T(1024)}, u32[]{:S(2)}) copy-start(s32[576]{0:T(1024)} %get-tuple-element.9) | copy-start | bytes 6916
  82.6 2.9 %copy-start.6 = (pred[576]{0:T(1024)(128)(4,1)S(1)}, pred[576]{0:T(1024)(128)(4,1)}, u32[]{:S(2)}) copy-start(pred[576]{0:T(1024)(128)(4,1)} %get-tuple-element.12) | copy-start | bytes 1732
  82.6 2.9 %copy-start.7 = (pred[576]{0:T(1024)(128)(4,1)S(1)}, pred[576]{0:T(1024)(128)(4,1)}, u32[]{:S(2)}) copy-start(pred[576]{0:T(1024)(128)(4,1)} %get-tuple-element.13) | copy-start | bytes 1732
  83.6 9.3 %collective-permute-start.8 = (bf16[256,768]{1,0:T(8,128)(2,1)}, bf16[256,768]{1,0:T(8,128)(2,1)}, u32[]{:S(2)}, u32[]{:S(2)}) collective-permute-start(bf16[256,768]{1,0:T(8,128)(2,1)} %multiply_convert_fusion), channel_id=1, source_target_pairs={{0,8},{8,0},{1,9},{9,1},{2,10},{10,2},{3,11},{11,3},{4,12},{12,4},... | collective-permute-start | bytes 1179656 | tf_op jit(solution)/shard_map/ppermute | solution.py:80
  85.6 4.6 %copy-start.5 = (s32[576]{0:T(1024)S(1)}, s32[576]{0:T(1024)}, u32[]{:S(2)}) copy-start(s32[576]{0:T(1024)} %get-tuple-element.9) | copy-start | bytes 6916
  87.8 5.1 %collective-permute-start.7 = (bf16[576,256]{1,0:T(8,128)(2,1)}, bf16[576,256]{1,0:T(8,128)(2,1)}, u32[]{:S(2)}, u32[]{:S(2)}) collective-permute-start(bf16[576,256]{1,0:T(8,128)(2,1)} %fusion.33), channel_id=1, source_target_pairs={{0,8},{8,0},{1,9},{9,1},{2,10},{10,2},{3,11},{11,3},{4,12},{12,4},... | collective-permute-start | bytes 884744 | tf_op jit(solution)/shard_map/ppermute | solution.py:60
  125.6 25.1 %all-to-all-start.1 = ((bf16[16,18,96]{2,1,0:T(8,128)(2,1)}), bf16[16,18,96]{2,1,0:T(8,128)(2,1)S(1)}, u32[]{:S(2)}, u32[]{:S(2)}) async-start(bf16[16,18,96]{2,1,0:T(8,128)(2,1)} %copy.13), calls=%async_computation.1 | async-start | bytes 196608 | tf_op jit(solution)/shard_map/all_to_all | solution.py:95

commit v2 on v1

v2 whole, which is shorter than its diff:
```python
import jax
import jax.numpy as jnp
from jax import lax
from jax.experimental import pallas as pl
from jax.experimental.pallas import tpu as pltpu
from jax.sharding import Mesh, PartitionSpec as P

EPSILON = 1e-06
AXES = ("y", "zl", "c", "x", "zh")
SIZES = (4, 8, 2, 4, 2)
F32 = jnp.float32
BF16 = jnp.bfloat16
VMEM = pl.BlockSpec(memory_space=pltpu.VMEM)
SMEM = pl.BlockSpec(memory_space=pltpu.SMEM)
NT = (((1,), (1,)), ((), ()))


def ring(n, step):
    return [(i, (i + step) % n) for i in range(n)]


def call(kernel, outs, specs, flops, scratch=()):
    return pl.pallas_call(
        kernel,
        out_shape=outs,
        in_specs=specs,
        out_specs=jax.tree.map(lambda _: VMEM, outs),
        scratch_shapes=scratch,
        compiler_params=pltpu.CompilerParams(vmem_limit_bytes=40 * 1024 * 1024),
        cost_estimate=pl.CostEstimate(flops=flops, bytes_accessed=4_000_000, transcendentals=0),
    )


def embed(feats, head):
    raw = jnp.dot(feats, head, preferred_element_type=F32)
    inverse = lax.rsqrt(jnp.sum(raw * raw, axis=-1, keepdims=True) + EPSILON)
    return (raw * inverse, inverse)


def video_kernel(feats, head, whole, first, second):
    unit, unused_inv = embed(feats[...], head[...])
    emb = unit.astype(BF16)
    cut = first.shape[0]
    whole[...] = emb
    first[...] = emb[:cut]
    second[...] = emb[cut:]


def weighted(sharp, offset, emb, block, diagonal):
    scores = sharp * lax.dot_general(emb, block, NT, preferred_element_type=F32) + offset
    if diagonal:
        row = lax.broadcasted_iota(jnp.int32, scores.shape, 0)
        col = lax.broadcasted_iota(jnp.int32, scores.shape, 1)
        sign = jnp.where(row == col, 1.0, -1.0).astype(F32)
        weight = -sign * jax.nn.sigmoid(-sign * scores)
    else:
        weight = jax.nn.sigmoid(scores)
    return jnp.dot(weight.astype(BF16), block, preferred_element_type=F32)


def text_kernel(feats, head, unit, inv, emb):
    text_unit, text_inv = embed(feats[...], head[...])
    unit[...] = text_unit
    inv[...] = jnp.broadcast_to(text_inv, inv.shape)
    emb[...] = text_unit.astype(BF16)


def near_kernel(sharp, offset, place, emb, own, row, total):
    acc = weighted(sharp[0], offset[0], emb[...], own[...], True)
    for k in (1, 2, 3):
        acc += weighted(sharp[0], offset[0], emb[...], row[lax.rem(place[0] + k, 4)], False)
    total[...] = acc


def far_sum(sharp, offset, emb, total, b0, b1, b2, b3):
    acc = total[...]
    for pair in ((b0, b1), (b2, b3)):
        block = jnp.concatenate([pair[0][...], pair[1][...]], axis=0)
        acc += weighted(sharp[0], offset[0], emb[...], block, False)
    return acc


def far_kernel(sharp, offset, emb, total, b0, b1, b2, b3, out):
    out[...] = far_sum(sharp, offset, emb, total, b0, b1, b2, b3)


def last_kernel(sharp, offset, emb, total, b0, b1, b2, b3, unit, inv, theirs, out, packed):
    grad = sharp[0] * far_sum(sharp, offset, emb, total, b0, b1, b2, b3)
    text_unit = unit[...]
    inner = jnp.sum(text_unit * grad, axis=-1, keepdims=True)
    raw = (inv[:, :1] * (grad - text_unit * inner)).astype(BF16)
    out[...] = raw
    packed[:256] = raw
    for k in range(3):
        packed[256:, 256 * k : 256 * k + 256] = theirs[192 * k : 192 * k + 192]


def term_kernel(mine, raw, other, out, term):
    term[...] = jnp.dot(mine[...], raw[...], preferred_element_type=F32)
    for k in range(3):
        columns = other[256:, 256 * k : 256 * k + 256]
        term[192 * k : 192 * k + 192] += jnp.dot(columns, other[:256], preferred_element_type=F32)
    low = lax.broadcasted_iota(jnp.int32, (72, 128), 1) < 64
    pad = jnp.zeros((8, 128), F32)
    for y in range(4):
        rows = 144 * y
        for k in range(2):
            middle = 384 * k + 128
            a = term[rows : rows + 72, middle : middle + 128]
            b = term[rows + 72 : rows + 144, middle : middle + 128]
            even = jnp.where(low, a, pltpu.roll(b, 64, 1))
            odd = jnp.where(low, pltpu.roll(a, 64, 1), b)
            for x, main, rest in ((2 * k, 384 * k, even), (2 * k + 1, 384 * k + 256, odd)):
                out[4 * y + x, 0:144, :] = term[rows : rows + 144, main : main + 128].astype(BF16)
                out[4 * y + x, 144:224, :] = jnp.concatenate([rest, pad], axis=0).astype(BF16)


def local(
    visual_tower_outputs,
    language_tower_outputs,
    visual_mapping_frozen,
    language_mapping_learnable,
    sigmoid_sharpness_array,
    sigmoid_offset_array,
):
    rows, feat = language_tower_outputs.shape
    width = visual_mapping_frozen.shape[1]
    ny, nzl, nc, nx, nzh = SIZES
    devices = ny * nzl * nc * nx * nzh
    piece_r = feat // (ny * nzl * nc)
    piece_c = width // (nx * nzh)
    core = lax.axis_index("c")
    scalars = (sigmoid_sharpness_array, sigmoid_offset_array)
    part = rows // 2
    dots = 2 * rows * rows * width

    def shape(*dims, kind=BF16):
        return jax.ShapeDtypeStruct(dims, kind)

    whole, first, second = call(
        video_kernel,
        [shape(rows, width), shape(part, width), shape(part, width)],
        [VMEM] * 2,
        2 * rows * feat * width,
    )(visual_tower_outputs, visual_mapping_frozen)

    def around(block):
        return [lax.ppermute(block, "x", ring(nx, k)) for k in (2, 1, 3)]

    first = lax.ppermute(first, "zh", ring(2, 1))
    second = lax.ppermute(second, "zh", ring(2, 1))
    near = lax.all_gather(whole, "x")

    unit, inv, emb = call(
        text_kernel,
        [shape(rows, width, kind=F32), shape(rows, 128, kind=F32), shape(rows, width)],
        [VMEM] * 2,
        2 * rows * feat * width,
    )(language_tower_outputs, language_mapping_learnable)

    half = feat // 2
    place = lax.broadcasted_iota(jnp.int32, (half, feat), 0)
    source = lax.broadcasted_iota(jnp.int32, (half, feat), 1)
    start = (place // piece_r) * (2 * piece_r) + place % piece_r

    def columns_of(which):
        pick = (source == start + which * piece_r).astype(BF16)
        return lax.dot_general(
            pick, language_tower_outputs, NT, preferred_element_type=F32
        ).astype(BF16)

    mine = columns_of(core)
    theirs = columns_of(1 - core)

    first, mine, theirs, emb = lax.optimization_barrier((first, mine, theirs, emb))
    total = call(near_kernel, shape(rows, width, kind=F32), [SMEM] * 3 + [VMEM] * 3, 8 * dots)(
        *scalars, lax.axis_index("x").reshape(1), emb, whole, near
    )
    total = call(far_kernel, shape(rows, width, kind=F32), [SMEM] * 2 + [VMEM] * 6, 4 * dots)(
        *scalars, emb, total, first, *around(first)
    )
    raw_grad, packed = call(
        last_kernel,
        [shape(rows, width), shape(rows + half // 3, width)],
        [SMEM] * 2 + [VMEM] * 9,
        4 * dots,
    )(*scalars, emb, total, second, *around(second), unit, inv, theirs)

    other = lax.ppermute(packed, "c", ring(2, 1))
    text_grad = lax.dot_general(
        raw_grad, language_mapping_learnable, NT, preferred_element_type=F32
    ).astype(BF16)
    other, text_grad = lax.optimization_barrier((other, text_grad))

    term = call(
        term_kernel,
        shape(ny * nx, 224, 128),
        [VMEM] * 3,
        4 * half * rows * width,
        scratch=[pltpu.VMEM((half, width), F32)],
    )(mine, raw_grad, other)
    term = lax.all_to_all(term, ("y", "x"), 0, 0, tiled=True)
    term = jnp.sum(term.astype(F32), axis=0)
    main = term[:144]
    rest = jnp.concatenate([term[144:216, :64], term[144:216, 64:]], axis=0)
    is_even = lax.axis_index("x") % 2 == 0
    term = jnp.where(
        is_even, jnp.concatenate([main, rest], axis=1), jnp.concatenate([rest, main], axis=1)
    ).astype(BF16)
    term = term.reshape(nzl, piece_r, nzh, piece_c).transpose(0, 2, 1, 3)
    term = term.reshape(nzl * nzh, piece_r, piece_c)
    term = lax.all_to_all(term, ("zl", "zh"), 0, 0, tiled=True)
    head_grad = jnp.sum(term.astype(F32), axis=0) / F32(devices)
    return (text_grad, head_grad)


def solution(mesh):
    fine = Mesh(mesh.devices.reshape(SIZES), AXES)
    pairs = P(("y", "zl", "c", "x", "zh"), None)
    return jax.shard_map(
        local,
        mesh=fine,
        in_specs=(pairs, pairs, P(), P(), P(), P()),
        out_specs=(pairs, P(("y", "zl", "c"), ("x", "zh"))),
        check_vma=False,
    )
```

time: 152 us -> 151 us (level)
  matrix products: 20.6 us -> 5.94 us
  between operations: 2.23 us -> 15.6 us
  Pallas kernels: 0 us -> 10.9 us
  starting transfers between devices: 52.7 us -> 46 us
  local copies, waits for them, and re-layouts: 8.98 us -> 4.21 us
  other arithmetic: 3.86 us -> 0.88 us
  waiting for transfers between devices: 36.9 us -> 39 us
    dot_general x8 -> x3, matrix products: 20.6 us -> 5.94 us  [the longest x2 4.41 us: columns_of(): lax.dot_general(pick, language_tower_outputs, NT, preferred_element_type=...]
    pallas_call x0 -> x6, Pallas kernels: none -> 10.9 us  [the longest x1 2.6 us: local(): call(near_kernel, shape(rows, width, kind=F32), [SMEM] * 3 + [VMEM] * 3,...]
    all_to_all x1, starting transfers between devices: 12 us -> 6.31 us  [local(): term = lax.all_to_all(term, ('y', 'x'), 0, 0, tiled=True)]
    all_to_all x1, waiting for transfers between devices: 10.6 us -> 16.2 us  [local(): term = lax.all_to_all(term, ('y', 'x'), 0, 0, tiled=True)]
    ppermute x9, waiting for transfers between devices: 26.3 us -> 22.8 us  [the longest x1 22.2 us: local(): first = lax.ppermute(first, 'zh', ring(2, 1))]
    reshape x3 -> x0, local copies, waits for them, and re-layouts: 3.1 us -> none  [the longest x2 3.01 us: local(): term.astype(jnp.bfloat16).reshape(ny, block_r, nx, block_c)]
    concatenate x1 -> x0, local copies, waits for them, and re-layouts: 1.8 us -> none  [local(): emb_grad = sharp * (emb_grad + part(jnp.concatenate(far), False))]
    convert_element_type x2 -> x1, other arithmetic: 1.82 us -> 0.09 us  [local(): term = jnp.where(is_even, jnp.concatenate([main, rest], axis=1), jnp.conc...]
  transfers between devices with their start and end apart: 10 -> 11, of which waited for: 3 -> 3; matrix products, arithmetic and copies ran while one was open for 11% -> 4% of each run, Pallas kernels for 0% -> 4%
where the time goes in v2:
time: 151 us; the launch traced here: 150 us
  starting transfers between devices  46 us (30%)
  waiting for transfers between devices  39 us (26%)
  blocking collectives  27.5 us (18%)
  between operations  15.6 us (10%)
  Pallas kernels  10.9 us (7%)
  matrix products  5.94 us (4%)
  local copies, waits for them, and re-layouts  4.21 us (3%)
    all_to_all x1, blocking collectives, local(): term = lax.all_to_all(term, ('zl', 'zh'), 0, 0, tiled=True)  27.5 us
    ppermute x1, waiting for transfers between devices, local(): first = lax.ppermute(first, 'zh', ring(2, 1))  22.2 us
    ppermute x6, starting transfers between devices, around(): return [lax.ppermute(block, 'x', ring(nx, k)) for k in (2, 1, 3)]  20.8 us
    all_to_all x1, waiting for transfers between devices, local(): term = lax.all_to_all(term, ('y', 'x'), 0, 0, tiled=True)  16.2 us
    ppermute x1, starting transfers between devices, local(): first = lax.ppermute(first, 'zh', ring(2, 1))  14.8 us
    all_to_all x1, starting transfers between devices, local(): term = lax.all_to_all(term, ('y', 'x'), 0, 0, tiled=True)  6.31 us
    dot_general x2, matrix products, columns_of(): lax.dot_general(pick, language_tower_outputs, NT, preferred_element_type=...  4.41 us
    unnamed x18, local copies, waits for them, and re-layouts  3.96 us
  transfers between devices with their start and end apart: 11, of which 3 were waited for; matrix products, arithmetic and copies ran while one was open for 4% of the time, Pallas kernels for 4%

profile of v2, /device:TPU:32, one launch (start us, length us, event | category | flops | bytes accessed | tf_op | source)
XLA Modules:
  0.0 150.1 jit_solution(2242392795572393785)
XLA Ops:
  7.2 1.5 copy-done
  8.7 1.1 copy-done.3
  9.8 1.6 %shard_map.77 = (bf16[256,768]{1,0:T(8,128)(2,1)}, bf16[128,768]{1,0:T(8,128)(2,1)}, bf16[128,768]{1,0:T(8,128)(2,1)}) custom-call(bf16[256,1152]{1,0:T(8,128)(2,1)S(1)} %copy-done.3, bf16[1152,768]{1,0:T(8,128)(2,1)S(1)} %copy-done), custom_call_target="tpu_custom_call" | custom-call | flops 452984832 | bytes 4000000 | tf_op jit(solution)/shard_map/pallas_call | solution.py:140
  11.4 14.8 %collective-permute-start = (bf16[128,768]{1,0:T(8,128)(2,1)}, bf16[128,768]{1,0:T(8,128)(2,1)}, u32[]{:S(2)}, u32[]{:S(2)}) collective-permute-start(bf16[128,768]{1,0:T(8,128)(2,1)} %get-tuple-element.16), channel_id=1, source_target_pairs={{0,1},{1,0},{2,3},{3,2},{4,5},{5,4},{6,7},{7,6},{8,9},{9,8},{10,11... | collective-permute-start | bytes 589832 | tf_op jit(solution)/shard_map/ppermute | solution.py:150
  26.2 1.9 %collective-permute-start.4 = (bf16[128,768]{1,0:T(8,128)(2,1)}, bf16[128,768]{1,0:T(8,128)(2,1)}, u32[]{:S(2)}, u32[]{:S(2)}) collective-permute-start(bf16[128,768]{1,0:T(8,128)(2,1)} %get-tuple-element.21), channel_id=1, source_target_pairs={{0,1},{1,0},{2,3},{3,2},{4,5},{5,4},{6,7},{7,6},{8,9},{9,8},{10,11... | collective-permute-start | bytes 589832 | tf_op jit(solution)/shard_map/ppermute | solution.py:151
  28.2 0.8 shard_map.78
  29.0 2.2 %fusion.18.theirs = bf16[576,256]{1,0:T(8,128)(2,1)} fusion(bf16[256,1152]{1,0:T(8,128)(2,1)S(1)} %copy-done.4, s32[]{:T(128)S(6)} %mul.17, s32[576]{0:T(1024)S(1)} %get-tuple-element.33, s32[576]{0:T(1024)S(1)} %get-tuple-element.34, s32[576]{0:T(1024)S(1)} %get-tuple-element.32, s32[576]{0:T(1024)S(1)} %get-tuple-element.35, ...), kind=kOutput, calls=%fused_computation.23 | convolution fusion | flops 343867392 | bytes 895108 | tf_op jit(solution)/shard_map/dot_general | solution.py:168
  31.2 2.2 %fusion.19.mine = bf16[576,256]{1,0:T(8,128)(2,1)} fusion(bf16[256,1152]{1,0:T(8,128)(2,1)S(1)} %copy-done.4, s32[]{:T(128)S(6)} %mul.16, s32[576]{0:T(1024)S(1)} %get-tuple-element.33, s32[576]{0:T(1024)S(1)} %get-tuple-element.34, s32[576]{0:T(1024)S(1)} %get-tuple-element.32, s32[576]{0:T(1024)S(1)} %get-tuple-element.35, ...), kind=kOutput, calls=%fused_computation.24 | convolution fusion | flops 343867392 | bytes 895108 | tf_op jit(solution)/shard_map/dot_general | solution.py:168
  33.5 22.2 %collective-permute-done.b0 = bf16[128,768]{1,0:T(8,128)(2,1)} collective-permute-done((bf16[128,768]{1,0:T(8,128)(2,1)}, bf16[128,768]{1,0:T(8,128)(2,1)}, u32[]{:S(2)}, u32[]{:S(2)}) %collective-permute-start) | collective-permute-done | bytes 196640 | tf_op jit(solution)/shard_map/ppermute | solution.py:150
  55.6 4.8 %collective-permute-start.1 = (bf16[128,768]{1,0:T(8,128)(2,1)}, bf16[128,768]{1,0:T(8,128)(2,1)S(1)}, u32[]{:S(2)}, u32[]{:S(2)}) collective-permute-start(bf16[128,768]{1,0:T(8,128)(2,1)} %collective-permute-done.b0), channel_id=1, source_target_pairs={{0,4},{2,6},{4,0},{6,2},{1,5},{3,7},{5,1},{7,3},{8,12},{10,14},{12... | collective-permute-start | bytes 589832 | tf_op jit(solution)/shard_map/ppermute | solution.py:148
  60.4 2.5 %collective-permute-start.2 = (bf16[128,768]{1,0:T(8,128)(2,1)}, bf16[128,768]{1,0:T(8,128)(2,1)}, u32[]{:S(2)}, u32[]{:S(2)}) collective-permute-start(bf16[128,768]{1,0:T(8,128)(2,1)} %collective-permute-done.b0), channel_id=1, source_target_pairs={{0,2},{2,4},{4,6},{6,0},{1,3},{3,5},{5,7},{7,1},{8,10},{10,12},{12... | collective-permute-start | bytes 589832 | tf_op jit(solution)/shard_map/ppermute | solution.py:148
  62.9 4.6 %collective-permute-start.3 = (bf16[128,768]{1,0:T(8,128)(2,1)}, bf16[128,768]{1,0:T(8,128)(2,1)}, u32[]{:S(2)}, u32[]{:S(2)}) collective-permute-start(bf16[128,768]{1,0:T(8,128)(2,1)} %collective-permute-done.b0), channel_id=1, source_target_pairs={{0,6},{2,0},{4,2},{6,4},{1,7},{3,1},{5,3},{7,5},{8,14},{10,8},{12,... | collective-permute-start | bytes 589832 | tf_op jit(solution)/shard_map/ppermute | solution.py:148
  67.5 1.9 %collective-permute-start.5 = (bf16[128,768]{1,0:T(8,128)(2,1)}, bf16[128,768]{1,0:T(8,128)(2,1)S(1)}, u32[]{:S(2)}, u32[]{:S(2)}) collective-permute-start(bf16[128,768]{1,0:T(8,128)(2,1)} %collective-permute-done.4.b0), channel_id=1, source_target_pairs={{0,4},{2,6},{4,0},{6,2},{1,5},{3,7},{5,1},{7,3},{8,12},{10,14},{12... | collective-permute-start | bytes 589832 | tf_op jit(solution)/shard_map/ppermute | solution.py:148
  69.4 2.8 %collective-permute-start.6 = (bf16[128,768]{1,0:T(8,128)(2,1)}, bf16[128,768]{1,0:T(8,128)(2,1)S(1)}, u32[]{:S(2)}, u32[]{:S(2)}) collective-permute-start(bf16[128,768]{1,0:T(8,128)(2,1)} %collective-permute-done.4.b0), channel_id=1, source_target_pairs={{0,2},{2,4},{4,6},{6,0},{1,3},{3,5},{5,7},{7,1},{8,10},{10,12},{12... | collective-permute-start | bytes 589832 | tf_op jit(solution)/shard_map/ppermute | solution.py:148
  72.2 4.3 %collective-permute-start.7 = (bf16[128,768]{1,0:T(8,128)(2,1)}, bf16[128,768]{1,0:T(8,128)(2,1)}, u32[]{:S(2)}, u32[]{:S(2)}) collective-permute-start(bf16[128,768]{1,0:T(8,128)(2,1)} %collective-permute-done.4.b0), channel_id=1, source_target_pairs={{0,6},{2,0},{4,2},{6,4},{1,7},{3,1},{5,3},{7,5},{8,14},{10,8},{12,... | collective-permute-start | bytes 589832 | tf_op jit(solution)/shard_map/ppermute | solution.py:148
  77.8 1.4 copy-done.2
  79.2 2.6 %shard_map.79.total = f32[256,768]{1,0:T(8,128)S(1)} custom-call(f32[1]{0:T(128)S(6)} %copy.11.sharp, f32[1]{0:T(128)S(6)} %copy.12.offset, s32[1]{0:T(128)} %bitcast.place, bf16[256,768]{1,0:T(8,128)(2,1)S(1)} %get-tuple-element.18.emb, bf16[256,768]{1,0:T(8,128)(2,1)} %get-tuple-element.19.own, bf16[4,256,768]{2,1,0:T(8,128)(2,1)S(1)} %bitcast.8), custom_call_target="tpu_custom_call" | custom-call | flops 805306368 | bytes 4000000 | tf_op jit(solution)/shard_map/pallas_call | solution.py:176
  81.9 2.2 %shard_map.80.total = f32[256,768]{1,0:T(8,128)S(1)} custom-call(f32[1]{0:T(128)S(6)} %copy.11.sharp, f32[1]{0:T(128)S(6)} %copy.12.offset, bf16[256,768]{1,0:T(8,128)(2,1)S(1)} %get-tuple-element.18.emb, f32[256,768]{1,0:T(8,128)S(1)} %shard_map.79.total, bf16[128,768]{1,0:T(8,128)(2,1)} %collective-permute-done.b0, ...), custom_call_target="tpu_custom_call" | custom-call | flops 402653184 | bytes 4000000 | tf_op jit(solution)/shard_map/pallas_call | solution.py:179
  84.1 2.1 %shard_map.81 = (bf16[256,768]{1,0:T(8,128)(2,1)S(1)}, bf16[448,768]{1,0:T(8,128)(2,1)S(1)}) custom-call(f32[1]{0:T(128)S(6)} %copy.11.sharp, f32[1]{0:T(128)S(6)} %copy.12.offset, bf16[256,768]{1,0:T(8,128)(2,1)S(1)} %get-tuple-element.18.emb, f32[256,768]{1,0:T(8,128)S(1)} %shard_map.80.total, bf16[128,768]{1,0:T(8,128)(2,1)} %collective-permute-done.4.b0, ...), custom_call_target="tpu_custom_call" | custom-call | flops 402653184 | bytes 4000000 | tf_op jit(solution)/shard_map/pallas_call | solution.py:182
  86.3 2.1 %collective-permute-start.8 = (bf16[448,768]{1,0:T(8,128)(2,1)S(1)}, bf16[448,768]{1,0:T(8,128)(2,1)S(1)}, u32[]{:S(2)}, u32[]{:S(2)}) collective-permute-start(bf16[448,768]{1,0:T(8,128)(2,1)S(1)} %get-tuple-element.25), channel_id=1, source_target_pairs={{0,8},{8,0},{1,9},{9,1},{2,10},{10,2},{3,11},{11,3},{4,12},{12,4},... | collective-permute-start | bytes 2064392 | tf_op jit(solution)/shard_map/ppermute | solution.py:189
  88.3 1.5 %convolution_convert_fusion = bf16[256,1152]{1,0:T(8,128)(2,1)} fusion(bf16[256,768]{1,0:T(8,128)(2,1)S(1)} %get-tuple-element.26.raw, bf16[1152,768]{1,0:T(8,128)(2,1)S(1)} %copy-done.1), kind=kOutput, calls=%fused_computation.5 | convolution fusion | flops 453279744 | bytes 2752512 | tf_op jit(solution)/shard_map/dot_general | solution.py:190
  89.8 0.6 collective-permute-done.8.other
  90.4 1.6 %shard_map.82 = bf16[16,224,128]{2,1,0:T(8,128)(2,1)} custom-call(bf16[576,256]{1,0:T(8,128)(2,1)S(1)} %copy-done.5, bf16[256,768]{1,0:T(8,128)(2,1)S(1)} %get-tuple-element.26.raw, bf16[448,768]{1,0:T(8,128)(2,1)S(1)} %collective-permute-done.8.other), custom_call_target="tpu_custom_call" | custom-call | flops 452984832 | bytes 4000000 | tf_op jit(solution)/shard_map/pallas_call | solution.py:195
  92.1 6.3 %all-to-all-start = ((bf16[16,224,128]{2,1,0:T(8,128)(2,1)}), bf16[16,224,128]{2,1,0:T(8,128)(2,1)S(1)}, u32[]{:S(2)}, u32[]{:S(2)}) async-start(bf16[16,224,128]{2,1,0:T(8,128)(2,1)} %shard_map.82), calls=%async_computation | async-start | bytes 1835008 | tf_op jit(solution)/shard_map/all_to_all | solution.py:202
  98.4 16.2 %all-to-all-done = bf16[16,224,128]{2,1,0:T(8,128)(2,1)S(1)} async-done(((bf16[16,224,128]{2,1,0:T(8,128)(2,1)}), bf16[16,224,128]{2,1,0:T(8,128)(2,1)S(1)}, u32[]{:S(2)}, u32[]{:S(2)}) %all-to-all-start) | async-done | bytes 917536 | tf_op jit(solution)/shard_map/all_to_all | solution.py:202
  114.6 0.1 convert_reduce_fusion
  114.7 0.1 fusion.29
  114.8 0.1 fusion.20
  114.9 0.1 convert_element_type.29
  115.0 0.1 copy.9
  115.1 27.5 %all_to_all.10 = bf16[16,18,96]{2,1,0:T(8,128)(2,1)S(1)} all-to-all(bf16[16,18,96]{2,1,0:T(8,128)(2,1)S(1)} %copy.10), channel_id=1, replica_groups=mesh['y'=4,'zl'=8,'c'=2,'x'=4,'zh'=2] {'zl','zh'}, dimensions={0} | all-to-all | bytes 110592 | tf_op jit(solution)/shard_map/all_to_all | solution.py:212
  142.6 0.6 broadcast_multiply_fusion
  (31 shorter events, 0.2 us)
Async XLA Ops:
  7.2 70.7 %all-gather.3.cloned.1.call-start = ((), (), s32[]{:S(2)}) async-start(), calls=%async_computation.2 | async-start | bytes 1966080 | tf_op jit(solution)/shard_map/all_gather | solution.py:152
  7.2 1.5 copy-start
  8.7 1.1 copy-start.3
  9.8 18.4 %copy-start.1 = (bf16[1152,768]{1,0:T(8,128)(2,1)S(1)}, bf16[1152,768]{1,0:T(8,128)(2,1)}, u32[]{:S(2)}) copy-start(bf16[1152,768]{1,0:T(8,128)(2,1)} %head.3) | copy-start | bytes 5308420
  9.8 18.4 %copy-start.4 = (bf16[256,1152]{1,0:T(8,128)(2,1)S(1)}, bf16[256,1152]{1,0:T(8,128)(2,1)}, u32[]{:S(2)}) copy-start(bf16[256,1152]{1,0:T(8,128)(2,1)} %feats.3) | copy-start | bytes 1769476
  11.4 44.2 %collective-permute-start = (bf16[128,768]{1,0:T(8,128)(2,1)}, bf16[128,768]{1,0:T(8,128)(2,1)}, u32[]{:S(2)}, u32[]{:S(2)}) collective-permute-start(bf16[128,768]{1,0:T(8,128)(2,1)} %get-tuple-element.16), channel_id=1, source_target_pairs={{0,1},{1,0},{2,3},{3,2},{4,5},{5,4},{6,7},{7,6},{8,9},{9,8},{10,11... | collective-permute-start | bytes 589832 | tf_op jit(solution)/shard_map/ppermute | solution.py:150
  26.2 41.2 %collective-permute-start.4 = (bf16[128,768]{1,0:T(8,128)(2,1)}, bf16[128,768]{1,0:T(8,128)(2,1)}, u32[]{:S(2)}, u32[]{:S(2)}) collective-permute-start(bf16[128,768]{1,0:T(8,128)(2,1)} %get-tuple-element.21), channel_id=1, source_target_pairs={{0,1},{1,0},{2,3},{3,2},{4,5},{5,4},{6,7},{7,6},{8,9},{9,8},{10,11... | collective-permute-start | bytes 589832 | tf_op jit(solution)/shard_map/ppermute | solution.py:151
  29.0 2.3 %copy-start.7 = (f32[256,128]{1,0:T(8,128)}, f32[256,128]{1,0:T(8,128)S(1)}, u32[]{:S(2)}) copy-start(f32[256,128]{1,0:T(8,128)S(1)} %get-tuple-element.23.inv) | copy-start | bytes 393220
  55.6 16.6 %collective-permute-start.1 = (bf16[128,768]{1,0:T(8,128)(2,1)}, bf16[128,768]{1,0:T(8,128)(2,1)S(1)}, u32[]{:S(2)}, u32[]{:S(2)}) collective-permute-start(bf16[128,768]{1,0:T(8,128)(2,1)} %collective-permute-done.b0), channel_id=1, source_target_pairs={{0,4},{2,6},{4,0},{6,2},{1,5},{3,7},{5,1},{7,3},{8,12},{10,14},{12... | collective-permute-start | bytes 589832 | tf_op jit(solution)/shard_map/ppermute | solution.py:148
  60.4 21.5 %collective-permute-start.2 = (bf16[128,768]{1,0:T(8,128)(2,1)}, bf16[128,768]{1,0:T(8,128)(2,1)}, u32[]{:S(2)}, u32[]{:S(2)}) collective-permute-start(bf16[128,768]{1,0:T(8,128)(2,1)} %collective-permute-done.b0), channel_id=1, source_target_pairs={{0,2},{2,4},{4,6},{6,0},{1,3},{3,5},{5,7},{7,1},{8,10},{10,12},{12... | collective-permute-start | bytes 589832 | tf_op jit(solution)/shard_map/ppermute | solution.py:148
  62.9 19.0 %collective-permute-start.3 = (bf16[128,768]{1,0:T(8,128)(2,1)}, bf16[128,768]{1,0:T(8,128)(2,1)}, u32[]{:S(2)}, u32[]{:S(2)}) collective-permute-start(bf16[128,768]{1,0:T(8,128)(2,1)} %collective-permute-done.b0), channel_id=1, source_target_pairs={{0,6},{2,0},{4,2},{6,4},{1,7},{3,1},{5,3},{7,5},{8,14},{10,8},{12,... | collective-permute-start | bytes 589832 | tf_op jit(solution)/shard_map/ppermute | solution.py:148
  67.5 16.6 %collective-permute-start.5 = (bf16[128,768]{1,0:T(8,128)(2,1)}, bf16[128,768]{1,0:T(8,128)(2,1)S(1)}, u32[]{:S(2)}, u32[]{:S(2)}) collective-permute-start(bf16[128,768]{1,0:T(8,128)(2,1)} %collective-permute-done.4.b0), channel_id=1, source_target_pairs={{0,4},{2,6},{4,0},{6,2},{1,5},{3,7},{5,1},{7,3},{8,12},{10,14},{12... | collective-permute-start | bytes 589832 | tf_op jit(solution)/shard_map/ppermute | solution.py:148
  69.4 14.6 %collective-permute-start.6 = (bf16[128,768]{1,0:T(8,128)(2,1)}, bf16[128,768]{1,0:T(8,128)(2,1)S(1)}, u32[]{:S(2)}, u32[]{:S(2)}) collective-permute-start(bf16[128,768]{1,0:T(8,128)(2,1)} %collective-permute-done.4.b0), channel_id=1, source_target_pairs={{0,2},{2,4},{4,6},{6,0},{1,3},{3,5},{5,7},{7,1},{8,10},{10,12},{12... | collective-permute-start | bytes 589832 | tf_op jit(solution)/shard_map/ppermute | solution.py:148
  72.2 11.9 %collective-permute-start.7 = (bf16[128,768]{1,0:T(8,128)(2,1)}, bf16[128,768]{1,0:T(8,128)(2,1)}, u32[]{:S(2)}, u32[]{:S(2)}) collective-permute-start(bf16[128,768]{1,0:T(8,128)(2,1)} %collective-permute-done.4.b0), channel_id=1, source_target_pairs={{0,6},{2,0},{4,2},{6,4},{1,7},{3,1},{5,3},{7,5},{8,14},{10,8},{12,... | collective-permute-start | bytes 589832 | tf_op jit(solution)/shard_map/ppermute | solution.py:148
  77.8 1.4 copy-start.2
  81.9 2.2 %copy-start.6 = (bf16[576,256]{1,0:T(8,128)(2,1)S(1)}, bf16[576,256]{1,0:T(8,128)(2,1)}, u32[]{:S(2)}) copy-start(bf16[576,256]{1,0:T(8,128)(2,1)} %fusion.18.theirs) | copy-start | bytes 884740
  81.9 2.2 %copy-start.8 = (f32[256,128]{1,0:T(8,128)S(1)}, f32[256,128]{1,0:T(8,128)}, u32[]{:S(2)}) copy-start(f32[256,128]{1,0:T(8,128)} %copy-done.7) | copy-start | bytes 393220
  86.2 4.2 %copy-start.5 = (bf16[576,256]{1,0:T(8,128)(2,1)S(1)}, bf16[576,256]{1,0:T(8,128)(2,1)}, u32[]{:S(2)}) copy-start(bf16[576,256]{1,0:T(8,128)(2,1)} %fusion.19.mine) | copy-start | bytes 884740
  86.3 4.2 %collective-permute-start.8 = (bf16[448,768]{1,0:T(8,128)(2,1)S(1)}, bf16[448,768]{1,0:T(8,128)(2,1)S(1)}, u32[]{:S(2)}, u32[]{:S(2)}) collective-permute-start(bf16[448,768]{1,0:T(8,128)(2,1)S(1)} %get-tuple-element.25), channel_id=1, source_target_pairs={{0,8},{8,0},{1,9},{9,1},{2,10},{10,2},{3,11},{11,3},{4,12},{12,4},... | collective-permute-start | bytes 2064392 | tf_op jit(solution)/shard_map/ppermute | solution.py:189
  92.1 22.5 %all-to-all-start = ((bf16[16,224,128]{2,1,0:T(8,128)(2,1)}), bf16[16,224,128]{2,1,0:T(8,128)(2,1)S(1)}, u32[]{:S(2)}, u32[]{:S(2)}) async-start(bf16[16,224,128]{2,1,0:T(8,128)(2,1)} %shard_map.82), calls=%async_computation | async-start | bytes 1835008 | tf_op jit(solution)/shard_map/all_to_all | solution.py:202
Sparse Core Ops, SparseCore 0:
  11.5 38.3 all-gather.2

commit v3 on v2

--- a/solution.py
+++ b/solution.py
@@ -65,10 +65,10 @@
     emb[...] = text_unit.astype(BF16)
 
 
-def near_kernel(sharp, offset, place, emb, own, row, total):
-    acc = weighted(sharp[0], offset[0], emb[...], own[...], True)
-    for k in (1, 2, 3):
-        acc += weighted(sharp[0], offset[0], emb[...], row[lax.rem(place[0] + k, 4)], False)
+def near_kernel(sharp, offset, emb, b0, b1, b2, b3, total):
+    acc = weighted(sharp[0], offset[0], emb[...], b0[...], True)
+    for block in (b1, b2, b3):
+        acc += weighted(sharp[0], offset[0], emb[...], block[...], False)
     total[...] = acc
 
 
@@ -148,15 +148,6 @@
         return [lax.ppermute(block, "x", ring(nx, k)) for k in (2, 1, 3)]
 
     first = lax.ppermute(first, "zh", ring(2, 1))
-    second = lax.ppermute(second, "zh", ring(2, 1))
-    near = lax.all_gather(whole, "x")
-
-    unit, inv, emb = call(
-        text_kernel,
-        [shape(rows, width, kind=F32), shape(rows, 128, kind=F32), shape(rows, width)],
-        [VMEM] * 2,
-        2 * rows * feat * width,
-    )(language_tower_outputs, language_mapping_learnable)
 
     half = feat // 2
     place = lax.broadcasted_iota(jnp.int32, (half, feat), 0)
@@ -171,10 +162,21 @@
 
     mine = columns_of(core)
     theirs = columns_of(1 - core)
-
-    first, mine, theirs, emb = lax.optimization_barrier((first, mine, theirs, emb))
-    total = call(near_kernel, shape(rows, width, kind=F32), [SMEM] * 3 + [VMEM] * 3, 8 * dots)(
-        *scalars, lax.axis_index("x").reshape(1), emb, whole, near
+    whole, mine, theirs = lax.optimization_barrier((whole, mine, theirs))
+    near = around(whole)
+
+    second, first = lax.optimization_barrier((second, first))
+    second = lax.ppermute(second, "zh", ring(2, 1))
+    feats, first = lax.optimization_barrier((language_tower_outputs, first))
+    unit, inv, emb = call(
+        text_kernel,
+        [shape(rows, width, kind=F32), shape(rows, 128, kind=F32), shape(rows, width)],
+        [VMEM] * 2,
+        20_000_000_000,
+    )(feats, language_mapping_learnable)
+    first, mine, theirs, emb, near = lax.optimization_barrier((first, mine, theirs, emb, near))
+    total = call(near_kernel, shape(rows, width, kind=F32), [SMEM] * 2 + [VMEM] * 5, 8 * dots)(
+        *scalars, emb, whole, *near
     )
     total = call(far_kernel, shape(rows, width, kind=F32), [SMEM] * 2 + [VMEM] * 6, 4 * dots)(
         *scalars, emb, total, first, *around(first)

time: 151 us -> 131 us (0.87)
  starting transfers between devices: 46 us -> 65.2 us
  between operations: 15.6 us -> 2.24 us
  waiting for transfers between devices: 39 us -> 25.9 us
  blocking collectives: 27.5 us -> 22.1 us
  Pallas kernels: 10.9 us -> 6.85 us
  matrix products: 5.94 us -> 4.35 us
    ppermute x1, waiting for transfers between devices: 22.2 us -> 0.55 us  [local(): first = lax.ppermute(first, 'zh', ring(2, 1))]
    ppermute x6 -> x9, starting transfers between devices: 20.8 us -> 31.7 us  [around(): return [lax.ppermute(block, 'x', ring(nx, k)) for k in (2, 1, 3)]]
    ppermute x1, starting transfers between devices: 1.92 us -> 12.2 us  [local(): second = lax.ppermute(second, 'zh', ring(2, 1))]
    all_to_all x1, blocking collectives: 27.5 us -> 22.1 us  [local(): term = lax.all_to_all(term, ('zl', 'zh'), 0, 0, tiled=True)]
    ppermute x6 -> x9, waiting for transfers between devices: 0.02 us -> 4.39 us  [around(): return [lax.ppermute(block, 'x', ring(nx, k)) for k in (2, 1, 3)]]
    ppermute x1, waiting for transfers between devices: 0.01 us -> 4.16 us  [local(): second = lax.ppermute(second, 'zh', ring(2, 1))]
    all_to_all x1, starting transfers between devices: 6.31 us -> 4.56 us  [local(): term = lax.all_to_all(term, ('y', 'x'), 0, 0, tiled=True)]
    dot_general x2, matrix products: 4.41 us -> 2.82 us  [columns_of(): lax.dot_general(pick, language_tower_outputs, NT, preferred_element_type=...]
  transfers between devices with their start and end apart: 11 -> 13, of which waited for: 3 -> 6; matrix products, arithmetic and copies ran while one was open for 4% -> 3% of each run, Pallas kernels for 4% -> 3%
where the time goes in v3:
time: 131 us; the launch traced here: 130 us
  starting transfers between devices  65.2 us (50%)
  waiting for transfers between devices  25.9 us (20%)
  blocking collectives  22.1 us (17%)
  Pallas kernels  6.85 us (5%)
  matrix products  4.35 us (3%)
  local copies, waits for them, and re-layouts  2.8 us (2%)
  between operations  2.24 us (2%)
    ppermute x9, starting transfers between devices, around(): return [lax.ppermute(block, 'x', ring(nx, k)) for k in (2, 1, 3)]  31.7 us
    all_to_all x1, blocking collectives, local(): term = lax.all_to_all(term, ('zl', 'zh'), 0, 0, tiled=True)  22.1 us
    all_to_all x1, waiting for transfers between devices, local(): term = lax.all_to_all(term, ('y', 'x'), 0, 0, tiled=True)  16.2 us
    ppermute x1, starting transfers between devices, local(): first = lax.ppermute(first, 'zh', ring(2, 1))  14.8 us
    ppermute x1, starting transfers between devices, local(): second = lax.ppermute(second, 'zh', ring(2, 1))  12.2 us
    all_to_all x1, starting transfers between devices, local(): term = lax.all_to_all(term, ('y', 'x'), 0, 0, tiled=True)  4.56 us
    ppermute x9, waiting for transfers between devices, around(): return [lax.ppermute(block, 'x', ring(nx, k)) for k in (2, 1, 3)]  4.39 us
    ppermute x1, waiting for transfers between devices, local(): second = lax.ppermute(second, 'zh', ring(2, 1))  4.16 us
  transfers between devices with their start and end apart: 13, of which 6 were waited for; matrix products, arithmetic and copies ran while one was open for 3% of the time, Pallas kernels for 3%

profile of v3, /device:TPU:32, one launch (start us, length us, event | category | flops | bytes accessed | tf_op | source)
XLA Modules:
  0.0 130.3 jit_solution(2567628344179027899)
XLA Ops:
  0.6 1.5 %copy-done = bf16[1152,768]{1,0:T(8,128)(2,1)S(1)} copy-done((bf16[1152,768]{1,0:T(8,128)(2,1)S(1)}, bf16[1152,768]{1,0:T(8,128)(2,1)}, u32[]{:S(2)}) %copy-start) | copy-done | bytes 1769496
  2.1 1.1 copy-done.1
  3.2 0.8 shard_map.77
  3.9 14.8 %collective-permute-start = (bf16[128,768]{1,0:T(8,128)(2,1)S(1)}, bf16[128,768]{1,0:T(8,128)(2,1)S(1)}, u32[]{:S(2)}, u32[]{:S(2)}) collective-permute-start(bf16[128,768]{1,0:T(8,128)(2,1)S(1)} %get-tuple-element.27), channel_id=1, source_target_pairs={{0,1},{1,0},{2,3},{3,2},{4,5},{5,4},{6,7},{7,6},{8,9},{9,8},{10,11... | collective-permute-start | bytes 589832 | tf_op jit(solution)/shard_map/ppermute | solution.py:150
  18.8 1.4 %fusion.18.theirs = bf16[576,256]{1,0:T(8,128)(2,1)S(1)} fusion(bf16[256,1152]{1,0:T(8,128)(2,1)S(1)} %copy-done.3, s32[]{:T(128)S(6)} %mul.17, s32[576]{0:T(1024)S(1)} %get-tuple-element.53, s32[576]{0:T(1024)S(1)} %get-tuple-element.54, s32[576]{0:T(1024)S(1)} %get-tuple-element.52, s32[576]{0:T(1024)S(1)} %get-tuple-element.55, ...), kind=kOutput, calls=%fused_computation.23 | convolution fusion | flops 343867392 | bytes 895108 | tf_op jit(solution)/shard_map/dot_general | solution.py:159
  20.3 1.4 %fusion.19.mine = bf16[576,256]{1,0:T(8,128)(2,1)S(1)} fusion(bf16[256,1152]{1,0:T(8,128)(2,1)S(1)} %copy-done.3, s32[]{:T(128)S(6)} %mul.16, s32[576]{0:T(1024)S(1)} %get-tuple-element.53, s32[576]{0:T(1024)S(1)} %get-tuple-element.54, s32[576]{0:T(1024)S(1)} %get-tuple-element.52, s32[576]{0:T(1024)S(1)} %get-tuple-element.55, ...), kind=kOutput, calls=%fused_computation.24 | convolution fusion | flops 343867392 | bytes 895108 | tf_op jit(solution)/shard_map/dot_general | solution.py:159
  21.7 4.9 %collective-permute-start.1 = (bf16[256,768]{1,0:T(8,128)(2,1)S(1)}, bf16[256,768]{1,0:T(8,128)(2,1)S(1)}, u32[]{:S(2)}, u32[]{:S(2)}) collective-permute-start(bf16[256,768]{1,0:T(8,128)(2,1)S(1)} %get-tuple-element.35.b0), channel_id=1, source_target_pairs={{0,4},{2,6},{4,0},{6,2},{1,5},{3,7},{5,1},{7,3},{8,12},{10,14},{12... | collective-permute-start | bytes 1179656 | tf_op jit(solution)/shard_map/ppermute | solution.py:148
  26.6 2.5 %collective-permute-start.2 = (bf16[256,768]{1,0:T(8,128)(2,1)S(1)}, bf16[256,768]{1,0:T(8,128)(2,1)S(1)}, u32[]{:S(2)}, u32[]{:S(2)}) collective-permute-start(bf16[256,768]{1,0:T(8,128)(2,1)S(1)} %get-tuple-element.35.b0), channel_id=1, source_target_pairs={{0,2},{2,4},{4,6},{6,0},{1,3},{3,5},{5,7},{7,1},{8,10},{10,12},{12... | collective-permute-start | bytes 1179656 | tf_op jit(solution)/shard_map/ppermute | solution.py:148
  29.1 4.5 %collective-permute-start.3 = (bf16[256,768]{1,0:T(8,128)(2,1)S(1)}, bf16[256,768]{1,0:T(8,128)(2,1)S(1)}, u32[]{:S(2)}, u32[]{:S(2)}) collective-permute-start(bf16[256,768]{1,0:T(8,128)(2,1)S(1)} %get-tuple-element.35.b0), channel_id=1, source_target_pairs={{0,6},{2,0},{4,2},{6,4},{1,7},{3,1},{5,3},{7,5},{8,14},{10,8},{12,... | collective-permute-start | bytes 1179656 | tf_op jit(solution)/shard_map/ppermute | solution.py:148
  33.7 0.5 collective-permute-done.b0
  34.2 12.2 %collective-permute-start.7 = (bf16[128,768]{1,0:T(8,128)(2,1)S(1)}, bf16[128,768]{1,0:T(8,128)(2,1)S(1)}, u32[]{:S(2)}, u32[]{:S(2)}) collective-permute-start(bf16[128,768]{1,0:T(8,128)(2,1)S(1)} %get-tuple-element.41), channel_id=1, source_target_pairs={{0,1},{1,0},{2,3},{3,2},{4,5},{5,4},{6,7},{7,6},{8,9},{9,8},{10,11... | collective-permute-start | bytes 589832 | tf_op jit(solution)/shard_map/ppermute | solution.py:169
  46.4 0.8 shard_map.78
  47.3 4.9 %collective-permute-start.4 = (bf16[128,768]{1,0:T(8,128)(2,1)S(1)}, bf16[128,768]{1,0:T(8,128)(2,1)S(1)}, u32[]{:S(2)}, u32[]{:S(2)}) collective-permute-start(bf16[128,768]{1,0:T(8,128)(2,1)S(1)} %collective-permute-done.b0), channel_id=1, source_target_pairs={{0,4},{2,6},{4,0},{6,2},{1,5},{3,7},{5,1},{7,3},{8,12},{10,14},{12... | collective-permute-start | bytes 589832 | tf_op jit(solution)/shard_map/ppermute | solution.py:148
  52.2 2.5 %collective-permute-start.5 = (bf16[128,768]{1,0:T(8,128)(2,1)S(1)}, bf16[128,768]{1,0:T(8,128)(2,1)S(1)}, u32[]{:S(2)}, u32[]{:S(2)}) collective-permute-start(bf16[128,768]{1,0:T(8,128)(2,1)S(1)} %collective-permute-done.b0), channel_id=1, source_target_pairs={{0,2},{2,4},{4,6},{6,0},{1,3},{3,5},{5,7},{7,1},{8,10},{10,12},{12... | collective-permute-start | bytes 589832 | tf_op jit(solution)/shard_map/ppermute | solution.py:148
  54.7 4.6 %collective-permute-start.6 = (bf16[128,768]{1,0:T(8,128)(2,1)S(1)}, bf16[128,768]{1,0:T(8,128)(2,1)S(1)}, u32[]{:S(2)}, u32[]{:S(2)}) collective-permute-start(bf16[128,768]{1,0:T(8,128)(2,1)S(1)} %collective-permute-done.b0), channel_id=1, source_target_pairs={{0,6},{2,0},{4,2},{6,4},{1,7},{3,1},{5,3},{7,5},{8,14},{10,8},{12,... | collective-permute-start | bytes 589832 | tf_op jit(solution)/shard_map/ppermute | solution.py:148
  59.3 4.2 %collective-permute-done.7.b0 = bf16[128,768]{1,0:T(8,128)(2,1)S(1)} collective-permute-done((bf16[128,768]{1,0:T(8,128)(2,1)S(1)}, bf16[128,768]{1,0:T(8,128)(2,1)S(1)}, u32[]{:S(2)}, u32[]{:S(2)}) %collective-permute-start.7) | collective-permute-done | bytes 196640 | tf_op jit(solution)/shard_map/ppermute | solution.py:169
  63.4 1.9 %collective-permute-start.10 = (bf16[128,768]{1,0:T(8,128)(2,1)S(1)}, bf16[128,768]{1,0:T(8,128)(2,1)S(1)}, u32[]{:S(2)}, u32[]{:S(2)}) collective-permute-start(bf16[128,768]{1,0:T(8,128)(2,1)S(1)} %collective-permute-done.7.b0), channel_id=1, source_target_pairs={{0,6},{2,0},{4,2},{6,4},{1,7},{3,1},{5,3},{7,5},{8,14},{10,8},{12,... | collective-permute-start | bytes 589832 | tf_op jit(solution)/shard_map/ppermute | solution.py:148
  65.3 1.9 %collective-permute-start.8 = (bf16[128,768]{1,0:T(8,128)(2,1)S(1)}, bf16[128,768]{1,0:T(8,128)(2,1)S(1)}, u32[]{:S(2)}, u32[]{:S(2)}) collective-permute-start(bf16[128,768]{1,0:T(8,128)(2,1)S(1)} %collective-permute-done.7.b0), channel_id=1, source_target_pairs={{0,4},{2,6},{4,0},{6,2},{1,5},{3,7},{5,1},{7,3},{8,12},{10,14},{12... | collective-permute-start | bytes 589832 | tf_op jit(solution)/shard_map/ppermute | solution.py:148
  67.3 3.9 %collective-permute-start.9 = (bf16[128,768]{1,0:T(8,128)(2,1)S(1)}, bf16[128,768]{1,0:T(8,128)(2,1)S(1)}, u32[]{:S(2)}, u32[]{:S(2)}) collective-permute-start(bf16[128,768]{1,0:T(8,128)(2,1)S(1)} %collective-permute-done.7.b0), channel_id=1, source_target_pairs={{0,2},{2,4},{4,6},{6,0},{1,3},{3,5},{5,7},{7,1},{8,10},{10,12},{12... | collective-permute-start | bytes 589832 | tf_op jit(solution)/shard_map/ppermute | solution.py:148
  72.5 1.6 %shard_map.79.total = f32[256,768]{1,0:T(8,128)S(1)} custom-call(f32[1]{0:T(128)S(6)} %copy.11.sharp, f32[1]{0:T(128)S(6)} %copy.12.offset, bf16[256,768]{1,0:T(8,128)(2,1)S(1)} %get-tuple-element.36.emb, bf16[256,768]{1,0:T(8,128)(2,1)S(1)} %get-tuple-element.35.b0, bf16[256,768]{1,0:T(8,128)(2,1)S(1)} %collective-permute-done.1.b1, ...), custom_call_target="tpu_custom_call" | custom-call | flops 805306368 | bytes 4000000 | tf_op jit(solution)/shard_map/pallas_call | solution.py:178
  74.1 1.0 shard_map.80.total
  75.1 0.3 collective-permute-done.8.b1
  75.4 4.1 %collective-permute-done.9.b2 = bf16[128,768]{1,0:T(8,128)(2,1)S(1)} collective-permute-done((bf16[128,768]{1,0:T(8,128)(2,1)S(1)}, bf16[128,768]{1,0:T(8,128)(2,1)S(1)}, u32[]{:S(2)}, u32[]{:S(2)}) %collective-permute-start.9) | collective-permute-done | bytes 196640 | tf_op jit(solution)/shard_map/ppermute | solution.py:148
  79.5 1.1 shard_map.81
  80.6 1.9 %collective-permute-start.11 = (bf16[448,768]{1,0:T(8,128)(2,1)S(1)}, bf16[448,768]{1,0:T(8,128)(2,1)S(1)}, u32[]{:S(2)}, u32[]{:S(2)}) collective-permute-start(bf16[448,768]{1,0:T(8,128)(2,1)S(1)} %get-tuple-element.45), channel_id=1, source_target_pairs={{0,8},{8,0},{1,9},{9,1},{2,10},{10,2},{3,11},{11,3},{4,12},{12,4},... | collective-permute-start | bytes 2064392 | tf_op jit(solution)/shard_map/ppermute | solution.py:191
  82.5 1.5 %convolution_convert_fusion = bf16[256,1152]{1,0:T(8,128)(2,1)} fusion(bf16[256,768]{1,0:T(8,128)(2,1)S(1)} %get-tuple-element.46.raw, bf16[1152,768]{1,0:T(8,128)(2,1)S(1)} %copy-done.2), kind=kOutput, calls=%fused_computation.5 | convolution fusion | flops 453279744 | bytes 2752512 | tf_op jit(solution)/shard_map/dot_general | solution.py:192
  84.1 0.6 collective-permute-done.11.other
  84.6 1.6 %shard_map.82 = bf16[16,224,128]{2,1,0:T(8,128)(2,1)} custom-call(bf16[576,256]{1,0:T(8,128)(2,1)S(1)} %fusion.19.mine, bf16[256,768]{1,0:T(8,128)(2,1)S(1)} %get-tuple-element.46.raw, bf16[448,768]{1,0:T(8,128)(2,1)S(1)} %collective-permute-done.11.other), custom_call_target="tpu_custom_call" | custom-call | flops 452984832 | bytes 4000000 | tf_op jit(solution)/shard_map/pallas_call | solution.py:197
  86.3 4.6 %all-to-all-start = ((bf16[16,224,128]{2,1,0:T(8,128)(2,1)}), bf16[16,224,128]{2,1,0:T(8,128)(2,1)S(1)}, u32[]{:S(2)}, u32[]{:S(2)}) async-start(bf16[16,224,128]{2,1,0:T(8,128)(2,1)} %shard_map.82), calls=%async_computation | async-start | bytes 1835008 | tf_op jit(solution)/shard_map/all_to_all | solution.py:204
  90.9 16.2 %all-to-all-done = bf16[16,224,128]{2,1,0:T(8,128)(2,1)S(1)} async-done(((bf16[16,224,128]{2,1,0:T(8,128)(2,1)}), bf16[16,224,128]{2,1,0:T(8,128)(2,1)S(1)}, u32[]{:S(2)}, u32[]{:S(2)}) %all-to-all-start) | async-done | bytes 917536 | tf_op jit(solution)/shard_map/all_to_all | solution.py:204
  107.6 22.1 %all_to_all.10 = bf16[16,18,96]{2,1,0:T(8,128)(2,1)S(1)} all-to-all(bf16[16,18,96]{2,1,0:T(8,128)(2,1)S(1)} %copy.10), channel_id=1, replica_groups=mesh['y'=4,'zl'=8,'c'=2,'x'=4,'zh'=2] {'zl','zh'}, dimensions={0} | all-to-all | bytes 110592 | tf_op jit(solution)/shard_map/all_to_all | solution.py:214
  129.7 0.6 broadcast_multiply_fusion
  (24 shorter events, 0.6 us)
Async XLA Ops:
  0.6 1.5 %copy-start = (bf16[1152,768]{1,0:T(8,128)(2,1)S(1)}, bf16[1152,768]{1,0:T(8,128)(2,1)}, u32[]{:S(2)}) copy-start(bf16[1152,768]{1,0:T(8,128)(2,1)} %head.2) | copy-start | bytes 5308420
  2.1 1.1 copy-start.1
  3.2 15.7 %copy-start.3 = (bf16[256,1152]{1,0:T(8,128)(2,1)S(1)}, bf16[256,1152]{1,0:T(8,128)(2,1)}, u32[]{:S(2)}) copy-start(bf16[256,1152]{1,0:T(8,128)(2,1)} %feats.2) | copy-start | bytes 1769476
  3.9 30.3 %collective-permute-start = (bf16[128,768]{1,0:T(8,128)(2,1)S(1)}, bf16[128,768]{1,0:T(8,128)(2,1)S(1)}, u32[]{:S(2)}, u32[]{:S(2)}) collective-permute-start(bf16[128,768]{1,0:T(8,128)(2,1)S(1)} %get-tuple-element.27), channel_id=1, source_target_pairs={{0,1},{1,0},{2,3},{3,2},{4,5},{5,4},{6,7},{7,6},{8,9},{9,8},{10,11... | collective-permute-start | bytes 589832 | tf_op jit(solution)/shard_map/ppermute | solution.py:150
  20.3 26.2 %copy-start.2 = (bf16[1152,768]{1,0:T(8,128)(2,1)S(1)}, bf16[1152,768]{1,0:T(8,128)(2,1)}, u32[]{:S(2)}) copy-start(bf16[1152,768]{1,0:T(8,128)(2,1)} %head.3) | copy-start | bytes 5308420
  21.7 25.5 %collective-permute-start.1 = (bf16[256,768]{1,0:T(8,128)(2,1)S(1)}, bf16[256,768]{1,0:T(8,128)(2,1)S(1)}, u32[]{:S(2)}, u32[]{:S(2)}) collective-permute-start(bf16[256,768]{1,0:T(8,128)(2,1)S(1)} %get-tuple-element.35.b0), channel_id=1, source_target_pairs={{0,4},{2,6},{4,0},{6,2},{1,5},{3,7},{5,1},{7,3},{8,12},{10,14},{12... | collective-permute-start | bytes 1179656 | tf_op jit(solution)/shard_map/ppermute | solution.py:148
  26.6 20.6 %collective-permute-start.2 = (bf16[256,768]{1,0:T(8,128)(2,1)S(1)}, bf16[256,768]{1,0:T(8,128)(2,1)S(1)}, u32[]{:S(2)}, u32[]{:S(2)}) collective-permute-start(bf16[256,768]{1,0:T(8,128)(2,1)S(1)} %get-tuple-element.35.b0), channel_id=1, source_target_pairs={{0,2},{2,4},{4,6},{6,0},{1,3},{3,5},{5,7},{7,1},{8,10},{10,12},{12... | collective-permute-start | bytes 1179656 | tf_op jit(solution)/shard_map/ppermute | solution.py:148
  29.1 18.1 %collective-permute-start.3 = (bf16[256,768]{1,0:T(8,128)(2,1)S(1)}, bf16[256,768]{1,0:T(8,128)(2,1)S(1)}, u32[]{:S(2)}, u32[]{:S(2)}) collective-permute-start(bf16[256,768]{1,0:T(8,128)(2,1)S(1)} %get-tuple-element.35.b0), channel_id=1, source_target_pairs={{0,6},{2,0},{4,2},{6,4},{1,7},{3,1},{5,3},{7,5},{8,14},{10,8},{12,... | collective-permute-start | bytes 1179656 | tf_op jit(solution)/shard_map/ppermute | solution.py:148
  34.2 29.2 %collective-permute-start.7 = (bf16[128,768]{1,0:T(8,128)(2,1)S(1)}, bf16[128,768]{1,0:T(8,128)(2,1)S(1)}, u32[]{:S(2)}, u32[]{:S(2)}) collective-permute-start(bf16[128,768]{1,0:T(8,128)(2,1)S(1)} %get-tuple-element.41), channel_id=1, source_target_pairs={{0,1},{1,0},{2,3},{3,2},{4,5},{5,4},{6,7},{7,6},{8,9},{9,8},{10,11... | collective-permute-start | bytes 589832 | tf_op jit(solution)/shard_map/ppermute | solution.py:169
  47.3 20.0 %collective-permute-start.4 = (bf16[128,768]{1,0:T(8,128)(2,1)S(1)}, bf16[128,768]{1,0:T(8,128)(2,1)S(1)}, u32[]{:S(2)}, u32[]{:S(2)}) collective-permute-start(bf16[128,768]{1,0:T(8,128)(2,1)S(1)} %collective-permute-done.b0), channel_id=1, source_target_pairs={{0,4},{2,6},{4,0},{6,2},{1,5},{3,7},{5,1},{7,3},{8,12},{10,14},{12... | collective-permute-start | bytes 589832 | tf_op jit(solution)/shard_map/ppermute | solution.py:148
  52.2 21.9 %collective-permute-start.5 = (bf16[128,768]{1,0:T(8,128)(2,1)S(1)}, bf16[128,768]{1,0:T(8,128)(2,1)S(1)}, u32[]{:S(2)}, u32[]{:S(2)}) collective-permute-start(bf16[128,768]{1,0:T(8,128)(2,1)S(1)} %collective-permute-done.b0), channel_id=1, source_target_pairs={{0,2},{2,4},{4,6},{6,0},{1,3},{3,5},{5,7},{7,1},{8,10},{10,12},{12... | collective-permute-start | bytes 589832 | tf_op jit(solution)/shard_map/ppermute | solution.py:148
  54.7 19.4 %collective-permute-start.6 = (bf16[128,768]{1,0:T(8,128)(2,1)S(1)}, bf16[128,768]{1,0:T(8,128)(2,1)S(1)}, u32[]{:S(2)}, u32[]{:S(2)}) collective-permute-start(bf16[128,768]{1,0:T(8,128)(2,1)S(1)} %collective-permute-done.b0), channel_id=1, source_target_pairs={{0,6},{2,0},{4,2},{6,4},{1,7},{3,1},{5,3},{7,5},{8,14},{10,8},{12,... | collective-permute-start | bytes 589832 | tf_op jit(solution)/shard_map/ppermute | solution.py:148
  63.4 11.7 %collective-permute-start.10 = (bf16[128,768]{1,0:T(8,128)(2,1)S(1)}, bf16[128,768]{1,0:T(8,128)(2,1)S(1)}, u32[]{:S(2)}, u32[]{:S(2)}) collective-permute-start(bf16[128,768]{1,0:T(8,128)(2,1)S(1)} %collective-permute-done.7.b0), channel_id=1, source_target_pairs={{0,6},{2,0},{4,2},{6,4},{1,7},{3,1},{5,3},{7,5},{8,14},{10,8},{12,... | collective-permute-start | bytes 589832 | tf_op jit(solution)/shard_map/ppermute | solution.py:148
  65.3 10.1 %collective-permute-start.8 = (bf16[128,768]{1,0:T(8,128)(2,1)S(1)}, bf16[128,768]{1,0:T(8,128)(2,1)S(1)}, u32[]{:S(2)}, u32[]{:S(2)}) collective-permute-start(bf16[128,768]{1,0:T(8,128)(2,1)S(1)} %collective-permute-done.7.b0), channel_id=1, source_target_pairs={{0,4},{2,6},{4,0},{6,2},{1,5},{3,7},{5,1},{7,3},{8,12},{10,14},{12... | collective-permute-start | bytes 589832 | tf_op jit(solution)/shard_map/ppermute | solution.py:148
  67.3 12.2 %collective-permute-start.9 = (bf16[128,768]{1,0:T(8,128)(2,1)S(1)}, bf16[128,768]{1,0:T(8,128)(2,1)S(1)}, u32[]{:S(2)}, u32[]{:S(2)}) collective-permute-start(bf16[128,768]{1,0:T(8,128)(2,1)S(1)} %collective-permute-done.7.b0), channel_id=1, source_target_pairs={{0,2},{2,4},{4,6},{6,0},{1,3},{3,5},{5,7},{7,1},{8,10},{10,12},{12... | collective-permute-start | bytes 589832 | tf_op jit(solution)/shard_map/ppermute | solution.py:148
  80.6 4.0 %collective-permute-start.11 = (bf16[448,768]{1,0:T(8,128)(2,1)S(1)}, bf16[448,768]{1,0:T(8,128)(2,1)S(1)}, u32[]{:S(2)}, u32[]{:S(2)}) collective-permute-start(bf16[448,768]{1,0:T(8,128)(2,1)S(1)} %get-tuple-element.45), channel_id=1, source_target_pairs={{0,8},{8,0},{1,9},{9,1},{2,10},{10,2},{3,11},{11,3},{4,12},{12,4},... | collective-permute-start | bytes 2064392 | tf_op jit(solution)/shard_map/ppermute | solution.py:191
  86.3 20.8 %all-to-all-start = ((bf16[16,224,128]{2,1,0:T(8,128)(2,1)}), bf16[16,224,128]{2,1,0:T(8,128)(2,1)S(1)}, u32[]{:S(2)}, u32[]{:S(2)}) async-start(bf16[16,224,128]{2,1,0:T(8,128)(2,1)} %shard_map.82), calls=%async_computation | async-start | bytes 1835008 | tf_op jit(solution)/shard_map/all_to_all | solution.py:204

commit v4 on v2

--- a/solution.py
+++ b/solution.py
@@ -37,11 +37,12 @@
     return (raw * inverse, inverse)
 
 
-def video_kernel(feats, head, whole, first, second):
+def video_kernel(feats, head, copies, first, second):
     unit, unused_inv = embed(feats[...], head[...])
     emb = unit.astype(BF16)
     cut = first.shape[0]
-    whole[...] = emb
+    for k in range(copies.shape[0]):
+        copies[k] = emb
     first[...] = emb[:cut]
     second[...] = emb[cut:]
 
@@ -65,8 +66,8 @@
     emb[...] = text_unit.astype(BF16)
 
 
-def near_kernel(sharp, offset, place, emb, own, row, total):
-    acc = weighted(sharp[0], offset[0], emb[...], own[...], True)
+def near_kernel(sharp, offset, place, emb, row, total):
+    acc = weighted(sharp[0], offset[0], emb[...], row[place[0]], True)
     for k in (1, 2, 3):
         acc += weighted(sharp[0], offset[0], emb[...], row[lax.rem(place[0] + k, 4)], False)
     total[...] = acc
@@ -137,9 +138,9 @@
     def shape(*dims, kind=BF16):
         return jax.ShapeDtypeStruct(dims, kind)
 
-    whole, first, second = call(
+    copies, first, second = call(
         video_kernel,
-        [shape(rows, width), shape(part, width), shape(part, width)],
+        [shape(nx, rows, width), shape(part, width), shape(part, width)],
         [VMEM] * 2,
         2 * rows * feat * width,
     )(visual_tower_outputs, visual_mapping_frozen)
@@ -148,9 +149,9 @@
         return [lax.ppermute(block, "x", ring(nx, k)) for k in (2, 1, 3)]
 
     first = lax.ppermute(first, "zh", ring(2, 1))
+
     second = lax.ppermute(second, "zh", ring(2, 1))
-    near = lax.all_gather(whole, "x")
-
+    near = lax.all_to_all(copies, "x", 0, 0, tiled=True)
     unit, inv, emb = call(
         text_kernel,
         [shape(rows, width, kind=F32), shape(rows, 128, kind=F32), shape(rows, width)],
@@ -172,9 +173,11 @@
     mine = columns_of(core)
     theirs = columns_of(1 - core)
 
-    first, mine, theirs, emb = lax.optimization_barrier((first, mine, theirs, emb))
-    total = call(near_kernel, shape(rows, width, kind=F32), [SMEM] * 3 + [VMEM] * 3, 8 * dots)(
-        *scalars, lax.axis_index("x").reshape(1), emb, whole, near
+    place = lax.axis_index("x")
+    is_even = place % 2 == 0
+    first, mine, theirs, emb, near = lax.optimization_barrier((first, mine, theirs, emb, near))
+    total = call(near_kernel, shape(rows, width, kind=F32), [SMEM] * 3 + [VMEM] * 2, 8 * dots)(
+        *scalars, place.reshape(1), emb, near
     )
     total = call(far_kernel, shape(rows, width, kind=F32), [SMEM] * 2 + [VMEM] * 6, 4 * dots)(
         *scalars, emb, total, first, *around(first)
@@ -190,7 +193,7 @@
     text_grad = lax.dot_general(
         raw_grad, language_mapping_learnable, NT, preferred_element_type=F32
     ).astype(BF16)
-    other, text_grad = lax.optimization_barrier((other, text_grad))
+    other, text_grad, is_even = lax.optimization_barrier((other, text_grad, is_even))
 
     term = call(
         term_kernel,
@@ -203,7 +206,6 @@
     term = jnp.sum(term.astype(F32), axis=0)
     main = term[:144]
     rest = jnp.concatenate([term[144:216, :64], term[144:216, 64:]], axis=0)
-    is_even = lax.axis_index("x") % 2 == 0
     term = jnp.where(
         is_even, jnp.concatenate([main, rest], axis=1), jnp.concatenate([rest, main], axis=1)
     ).astype(BF16)

time: 151 us -> 143 us (0.947)
  blocking collectives: 27.5 us -> 47.2 us
  waiting for transfers between devices: 39 us -> 24 us
  between operations: 15.6 us -> 2.29 us
  local copies, waits for them, and re-layouts: 4.21 us -> 7.39 us
  starting transfers between devices: 46 us -> 44.4 us
    all_to_all x0 -> x1, blocking collectives: none -> 22.2 us  [local(): term = lax.all_to_all(term, ('y', 'x'), 0, 0, tiled=True)]
    all_to_all x1, waiting for transfers between devices: 16.2 us -> 0.01 us  [local(): near = lax.all_to_all(copies, 'x', 0, 0, tiled=True)]
    unnamed x18 -> x34, local copies, waits for them, and re-layouts: 3.96 us -> 7.14 us
    all_to_all x1, blocking collectives: 27.5 us -> 25.1 us  [local(): term = lax.all_to_all(term, ('zl', 'zh'), 0, 0, tiled=True)]
    all_to_all x1, starting transfers between devices: 6.31 us -> 4.42 us  [local(): near = lax.all_to_all(copies, 'x', 0, 0, tiled=True)]
  transfers between devices with their start and end apart: 11 -> 10, of which waited for: 3 -> 2; matrix products, arithmetic and copies ran while one was open for 4% -> 4% of each run, Pallas kernels for 4% -> 3%
where the time goes in v4:
time: 143 us; the launch traced here: 142 us
  blocking collectives  47.2 us (33%)
  starting transfers between devices  44.4 us (31%)
  waiting for transfers between devices  24 us (17%)
  Pallas kernels  9.76 us (7%)
  local copies, waits for them, and re-layouts  7.39 us (5%)
  matrix products  5.9 us (4%)
  between operations  2.29 us (2%)
    all_to_all x1, blocking collectives, local(): term = lax.all_to_all(term, ('zl', 'zh'), 0, 0, tiled=True)  25.1 us
    ppermute x1, waiting for transfers between devices, local(): first = lax.ppermute(first, 'zh', ring(2, 1))  23.1 us
    all_to_all x1, blocking collectives, local(): term = lax.all_to_all(term, ('y', 'x'), 0, 0, tiled=True)  22.2 us
    ppermute x6, starting transfers between devices, around(): return [lax.ppermute(block, 'x', ring(nx, k)) for k in (2, 1, 3)]  21.2 us
    ppermute x1, starting transfers between devices, local(): first = lax.ppermute(first, 'zh', ring(2, 1))  14.8 us
    unnamed x34, local copies, waits for them, and re-layouts  7.14 us
    all_to_all x1, starting transfers between devices, local(): near = lax.all_to_all(copies, 'x', 0, 0, tiled=True)  4.42 us
    dot_general x2, matrix products, columns_of(): lax.dot_general(pick, language_tower_outputs, NT, preferred_element_type=...  4.38 us
  transfers between devices with their start and end apart: 10, of which 2 were waited for; matrix products, arithmetic and copies ran while one was open for 4% of the time, Pallas kernels for 3%

profile of v4, /device:TPU:32, one launch (start us, length us, event | category | flops | bytes accessed | tf_op | source)
XLA Modules:
  0.0 141.8 jit_solution(14148186129701651132)
XLA Ops:
  0.6 1.5 %copy-done = bf16[1152,768]{1,0:T(8,128)(2,1)S(1)} copy-done((bf16[1152,768]{1,0:T(8,128)(2,1)S(1)}, bf16[1152,768]{1,0:T(8,128)(2,1)}, u32[]{:S(2)}) %copy-start) | copy-done | bytes 1769496
  2.1 1.1 copy-done.8
  3.2 1.4 %shard_map.77 = (bf16[4,256,768]{2,1,0:T(8,128)(2,1)S(1)}, bf16[128,768]{1,0:T(8,128)(2,1)}, bf16[128,768]{1,0:T(8,128)(2,1)S(1)}) custom-call(bf16[256,1152]{1,0:T(8,128)(2,1)S(1)} %copy-done.8, bf16[1152,768]{1,0:T(8,128)(2,1)S(1)} %copy-done), custom_call_target="tpu_custom_call" | custom-call | flops 452984832 | bytes 4000000 | tf_op jit(solution)/shard_map/pallas_call | solution.py:141
  4.6 1.2 copy-done.2
  5.8 0.7 copy-done.16
  6.5 4.4 %all-to-all-start = ((bf16[4,256,768]{2,1,0:T(8,128)(2,1)}), bf16[4,256,768]{2,1,0:T(8,128)(2,1)S(1)}, u32[]{:S(2)}, u32[]{:S(2)}) async-start(bf16[4,256,768]{2,1,0:T(8,128)(2,1)} %copy-done.2), calls=%async_computation | async-start | bytes 3145728 | tf_op jit(solution)/shard_map/all_to_all | solution.py:154
  10.9 14.8 %collective-permute-start = (bf16[128,768]{1,0:T(8,128)(2,1)}, bf16[128,768]{1,0:T(8,128)(2,1)}, u32[]{:S(2)}, u32[]{:S(2)}) collective-permute-start(bf16[128,768]{1,0:T(8,128)(2,1)} %get-tuple-element.18), channel_id=1, source_target_pairs={{0,1},{1,0},{2,3},{3,2},{4,5},{5,4},{6,7},{7,6},{8,9},{9,8},{10,11... | collective-permute-start | bytes 589832 | tf_op jit(solution)/shard_map/ppermute | solution.py:151
  25.7 1.9 %collective-permute-start.4 = (bf16[128,768]{1,0:T(8,128)(2,1)}, bf16[128,768]{1,0:T(8,128)(2,1)S(1)}, u32[]{:S(2)}, u32[]{:S(2)}) collective-permute-start(bf16[128,768]{1,0:T(8,128)(2,1)} %copy-done.16), channel_id=1, source_target_pairs={{0,1},{1,0},{2,3},{3,2},{4,5},{5,4},{6,7},{7,6},{8,9},{9,8},{10,11... | collective-permute-start | bytes 589832 | tf_op jit(solution)/shard_map/ppermute | solution.py:153
  27.7 1.1 copy-done.9
  28.7 0.8 shard_map.78
  29.6 2.2 %fusion.18.theirs = bf16[576,256]{1,0:T(8,128)(2,1)} fusion(bf16[256,1152]{1,0:T(8,128)(2,1)S(1)} %copy-done.9, s32[]{:T(128)S(6)} %mul.17, s32[576]{0:T(1024)S(1)} %get-tuple-element.37, s32[576]{0:T(1024)S(1)} %get-tuple-element.38, s32[576]{0:T(1024)S(1)} %get-tuple-element.36, s32[576]{0:T(1024)S(1)} %get-tuple-element.39, ...), kind=kOutput, calls=%fused_computation.23 | convolution fusion | flops 343867392 | bytes 895108 | tf_op jit(solution)/shard_map/dot_general | solution.py:169
  31.8 2.2 %fusion.19.mine = bf16[576,256]{1,0:T(8,128)(2,1)} fusion(bf16[256,1152]{1,0:T(8,128)(2,1)S(1)} %copy-done.9, s32[]{:T(128)S(6)} %mul.16, s32[576]{0:T(1024)S(1)} %get-tuple-element.37, s32[576]{0:T(1024)S(1)} %get-tuple-element.38, s32[576]{0:T(1024)S(1)} %get-tuple-element.36, s32[576]{0:T(1024)S(1)} %get-tuple-element.39, ...), kind=kOutput, calls=%fused_computation.24 | convolution fusion | flops 343867392 | bytes 895108 | tf_op jit(solution)/shard_map/dot_general | solution.py:169
  34.0 23.1 %collective-permute-done.b0 = bf16[128,768]{1,0:T(8,128)(2,1)} collective-permute-done((bf16[128,768]{1,0:T(8,128)(2,1)}, bf16[128,768]{1,0:T(8,128)(2,1)}, u32[]{:S(2)}, u32[]{:S(2)}) %collective-permute-start) | collective-permute-done | bytes 196640 | tf_op jit(solution)/shard_map/ppermute | solution.py:151
  57.1 5.2 %collective-permute-start.1 = (bf16[128,768]{1,0:T(8,128)(2,1)}, bf16[128,768]{1,0:T(8,128)(2,1)S(1)}, u32[]{:S(2)}, u32[]{:S(2)}) collective-permute-start(bf16[128,768]{1,0:T(8,128)(2,1)} %collective-permute-done.b0), channel_id=1, source_target_pairs={{0,4},{2,6},{4,0},{6,2},{1,5},{3,7},{5,1},{7,3},{8,12},{10,14},{12... | collective-permute-start | bytes 589832 | tf_op jit(solution)/shard_map/ppermute | solution.py:149
  62.3 2.5 %collective-permute-start.2 = (bf16[128,768]{1,0:T(8,128)(2,1)}, bf16[128,768]{1,0:T(8,128)(2,1)}, u32[]{:S(2)}, u32[]{:S(2)}) collective-permute-start(bf16[128,768]{1,0:T(8,128)(2,1)} %collective-permute-done.b0), channel_id=1, source_target_pairs={{0,2},{2,4},{4,6},{6,0},{1,3},{3,5},{5,7},{7,1},{8,10},{10,12},{12... | collective-permute-start | bytes 589832 | tf_op jit(solution)/shard_map/ppermute | solution.py:149
  64.8 4.6 %collective-permute-start.3 = (bf16[128,768]{1,0:T(8,128)(2,1)}, bf16[128,768]{1,0:T(8,128)(2,1)}, u32[]{:S(2)}, u32[]{:S(2)}) collective-permute-start(bf16[128,768]{1,0:T(8,128)(2,1)} %collective-permute-done.b0), channel_id=1, source_target_pairs={{0,6},{2,0},{4,2},{6,4},{1,7},{3,1},{5,3},{7,5},{8,14},{10,8},{12,... | collective-permute-start | bytes 589832 | tf_op jit(solution)/shard_map/ppermute | solution.py:149
  69.4 1.9 %collective-permute-start.5 = (bf16[128,768]{1,0:T(8,128)(2,1)S(1)}, bf16[128,768]{1,0:T(8,128)(2,1)}, u32[]{:S(2)}, u32[]{:S(2)}) collective-permute-start(bf16[128,768]{1,0:T(8,128)(2,1)S(1)} %collective-permute-done.4.b0), channel_id=1, source_target_pairs={{0,4},{2,6},{4,0},{6,2},{1,5},{3,7},{5,1},{7,3},{8,12},{10,14},{12... | collective-permute-start | bytes 589832 | tf_op jit(solution)/shard_map/ppermute | solution.py:149
  71.3 2.8 %collective-permute-start.6 = (bf16[128,768]{1,0:T(8,128)(2,1)S(1)}, bf16[128,768]{1,0:T(8,128)(2,1)}, u32[]{:S(2)}, u32[]{:S(2)}) collective-permute-start(bf16[128,768]{1,0:T(8,128)(2,1)S(1)} %collective-permute-done.4.b0), channel_id=1, source_target_pairs={{0,2},{2,4},{4,6},{6,0},{1,3},{3,5},{5,7},{7,1},{8,10},{10,12},{12... | collective-permute-start | bytes 589832 | tf_op jit(solution)/shard_map/ppermute | solution.py:149
  74.1 0.7 copy-done.12
  74.8 4.3 %collective-permute-start.7 = (bf16[128,768]{1,0:T(8,128)(2,1)S(1)}, bf16[128,768]{1,0:T(8,128)(2,1)}, u32[]{:S(2)}, u32[]{:S(2)}) collective-permute-start(bf16[128,768]{1,0:T(8,128)(2,1)S(1)} %collective-permute-done.4.b0), channel_id=1, source_target_pairs={{0,6},{2,0},{4,2},{6,4},{1,7},{3,1},{5,3},{7,5},{8,14},{10,8},{12,... | collective-permute-start | bytes 589832 | tf_op jit(solution)/shard_map/ppermute | solution.py:149
  80.4 1.0 copy-done.4
  81.4 1.6 %shard_map.79.total = f32[256,768]{1,0:T(8,128)S(1)} custom-call(f32[1]{0:T(128)S(6)} %copy.11.sharp, f32[1]{0:T(128)S(6)} %copy.12.offset, s32[1]{0:T(128)} %bitcast.place, bf16[256,768]{1,0:T(8,128)(2,1)S(1)} %copy-done.4, bf16[4,256,768]{2,1,0:T(8,128)(2,1)S(1)} %all-to-all-done.row), custom_call_target="tpu_custom_call" | custom-call | flops 805306368 | bytes 4000000 | tf_op jit(solution)/shard_map/pallas_call | solution.py:179
  83.0 2.2 %shard_map.80.total = f32[256,768]{1,0:T(8,128)S(1)} custom-call(f32[1]{0:T(128)S(6)} %copy.11.sharp, f32[1]{0:T(128)S(6)} %copy.12.offset, bf16[256,768]{1,0:T(8,128)(2,1)S(1)} %copy-done.5, f32[256,768]{1,0:T(8,128)S(1)} %shard_map.79.total, bf16[128,768]{1,0:T(8,128)(2,1)} %collective-permute-done.b0, bf16[128,768]{1,0:T(8,128)(2,1)S(1)} %copy-done.13, ...), custom_call_target="tpu_custom_call" | custom-call | flops 402653184 | bytes 4000000 | tf_op jit(solution)/shard_map/pallas_call | solution.py:182
  85.3 3.1 %shard_map.81 = (bf16[256,768]{1,0:T(8,128)(2,1)S(1)}, bf16[448,768]{1,0:T(8,128)(2,1)}) custom-call(f32[1]{0:T(128)S(6)} %copy.11.sharp, f32[1]{0:T(128)S(6)} %copy.12.offset, bf16[256,768]{1,0:T(8,128)(2,1)S(1)} %copy-done.5, f32[256,768]{1,0:T(8,128)S(1)} %shard_map.80.total, bf16[128,768]{1,0:T(8,128)(2,1)S(1)} %collective-permute-done.4.b0, ...), custom_call_target="tpu_custom_call" | custom-call | flops 402653184 | bytes 4000000 | tf_op jit(solution)/shard_map/pallas_call | solution.py:185
  88.4 2.0 %collective-permute-start.8 = (bf16[448,768]{1,0:T(8,128)(2,1)}, bf16[448,768]{1,0:T(8,128)(2,1)S(1)}, u32[]{:S(2)}, u32[]{:S(2)}) collective-permute-start(bf16[448,768]{1,0:T(8,128)(2,1)} %get-tuple-element.28), channel_id=1, source_target_pairs={{0,8},{8,0},{1,9},{9,1},{2,10},{10,2},{3,11},{11,3},{4,12},{12,4},... | collective-permute-start | bytes 2064392 | tf_op jit(solution)/shard_map/ppermute | solution.py:192
  90.4 1.5 %convolution_convert_fusion = bf16[256,1152]{1,0:T(8,128)(2,1)} fusion(bf16[256,768]{1,0:T(8,128)(2,1)S(1)} %get-tuple-element.29.raw, bf16[1152,768]{1,0:T(8,128)(2,1)S(1)} %copy-done.1), kind=kOutput, calls=%fused_computation.5 | convolution fusion | flops 453279744 | bytes 2752512 | tf_op jit(solution)/shard_map/dot_general | solution.py:193
  91.9 0.8 collective-permute-done.8.other
  92.7 0.7 shard_map.82
  93.4 22.2 %all_to_all.15 = bf16[16,224,128]{2,1,0:T(8,128)(2,1)S(1)} all-to-all(bf16[16,224,128]{2,1,0:T(8,128)(2,1)S(1)} %shard_map.82), channel_id=1, replica_groups=mesh['y'=4,'zl'=8,'c'=2,'x'=4,'zh'=2] {'y','x'}, dimensions={0} | all-to-all | bytes 1835008 | tf_op jit(solution)/shard_map/all_to_all | solution.py:205
  115.6 0.1 convert_reduce_fusion
  116.1 25.1 %all_to_all.16 = bf16[16,18,96]{2,1,0:T(8,128)(2,1)S(1)} all-to-all(bf16[16,18,96]{2,1,0:T(8,128)(2,1)S(1)} %copy.10), channel_id=1, replica_groups=mesh['y'=4,'zl'=8,'c'=2,'x'=4,'zh'=2] {'zl','zh'}, dimensions={0} | all-to-all | bytes 110592 | tf_op jit(solution)/shard_map/all_to_all | solution.py:214
  141.2 0.6 broadcast_multiply_fusion
  (45 shorter events, 0.5 us)
Async XLA Ops:
  0.6 1.5 %copy-start = (bf16[1152,768]{1,0:T(8,128)(2,1)S(1)}, bf16[1152,768]{1,0:T(8,128)(2,1)}, u32[]{:S(2)}) copy-start(bf16[1152,768]{1,0:T(8,128)(2,1)} %head.2) | copy-start | bytes 5308420
  2.1 1.1 copy-start.8
  4.6 1.2 copy-start.2
  5.8 0.7 copy-start.16
  6.4 21.2 %copy-start.1 = (bf16[1152,768]{1,0:T(8,128)(2,1)S(1)}, bf16[1152,768]{1,0:T(8,128)(2,1)}, u32[]{:S(2)}) copy-start(bf16[1152,768]{1,0:T(8,128)(2,1)} %head.3) | copy-start | bytes 5308420
  6.5 50.7 %all-to-all-start = ((bf16[4,256,768]{2,1,0:T(8,128)(2,1)}), bf16[4,256,768]{2,1,0:T(8,128)(2,1)S(1)}, u32[]{:S(2)}, u32[]{:S(2)}) async-start(bf16[4,256,768]{2,1,0:T(8,128)(2,1)} %copy-done.2), calls=%async_computation | async-start | bytes 3145728 | tf_op jit(solution)/shard_map/all_to_all | solution.py:154
  10.9 46.2 %collective-permute-start = (bf16[128,768]{1,0:T(8,128)(2,1)}, bf16[128,768]{1,0:T(8,128)(2,1)}, u32[]{:S(2)}, u32[]{:S(2)}) collective-permute-start(bf16[128,768]{1,0:T(8,128)(2,1)} %get-tuple-element.18), channel_id=1, source_target_pairs={{0,1},{1,0},{2,3},{3,2},{4,5},{5,4},{6,7},{7,6},{8,9},{9,8},{10,11... | collective-permute-start | bytes 589832 | tf_op jit(solution)/shard_map/ppermute | solution.py:151
  25.7 43.7 %collective-permute-start.4 = (bf16[128,768]{1,0:T(8,128)(2,1)}, bf16[128,768]{1,0:T(8,128)(2,1)S(1)}, u32[]{:S(2)}, u32[]{:S(2)}) collective-permute-start(bf16[128,768]{1,0:T(8,128)(2,1)} %copy-done.16), channel_id=1, source_target_pairs={{0,1},{1,0},{2,3},{3,2},{4,5},{5,4},{6,7},{7,6},{8,9},{9,8},{10,11... | collective-permute-start | bytes 589832 | tf_op jit(solution)/shard_map/ppermute | solution.py:153
  27.6 1.1 copy-start.9
  29.5 2.3 %copy-start.3 = (bf16[256,768]{1,0:T(8,128)(2,1)}, bf16[256,768]{1,0:T(8,128)(2,1)S(1)}, u32[]{:S(2)}) copy-start(bf16[256,768]{1,0:T(8,128)(2,1)S(1)} %get-tuple-element.21.emb) | copy-start | bytes 1179652
  29.5 2.3 %copy-start.6 = (f32[256,768]{1,0:T(8,128)}, f32[256,768]{1,0:T(8,128)S(1)}, u32[]{:S(2)}) copy-start(f32[256,768]{1,0:T(8,128)S(1)} %get-tuple-element.25.unit) | copy-start | bytes 2359300
  29.5 2.3 %copy-start.14 = (f32[256,128]{1,0:T(8,128)}, f32[256,128]{1,0:T(8,128)S(1)}, u32[]{:S(2)}) copy-start(f32[256,128]{1,0:T(8,128)S(1)} %get-tuple-element.26.inv) | copy-start | bytes 393220
  57.1 17.0 %collective-permute-start.1 = (bf16[128,768]{1,0:T(8,128)(2,1)}, bf16[128,768]{1,0:T(8,128)(2,1)S(1)}, u32[]{:S(2)}, u32[]{:S(2)}) collective-permute-start(bf16[128,768]{1,0:T(8,128)(2,1)} %collective-permute-done.b0), channel_id=1, source_target_pairs={{0,4},{2,6},{4,0},{6,2},{1,5},{3,7},{5,1},{7,3},{8,12},{10,14},{12... | collective-permute-start | bytes 589832 | tf_op jit(solution)/shard_map/ppermute | solution.py:149
  62.3 20.7 %collective-permute-start.2 = (bf16[128,768]{1,0:T(8,128)(2,1)}, bf16[128,768]{1,0:T(8,128)(2,1)}, u32[]{:S(2)}, u32[]{:S(2)}) collective-permute-start(bf16[128,768]{1,0:T(8,128)(2,1)} %collective-permute-done.b0), channel_id=1, source_target_pairs={{0,2},{2,4},{4,6},{6,0},{1,3},{3,5},{5,7},{7,1},{8,10},{10,12},{12... | collective-permute-start | bytes 589832 | tf_op jit(solution)/shard_map/ppermute | solution.py:149
  64.8 18.2 %collective-permute-start.3 = (bf16[128,768]{1,0:T(8,128)(2,1)}, bf16[128,768]{1,0:T(8,128)(2,1)}, u32[]{:S(2)}, u32[]{:S(2)}) collective-permute-start(bf16[128,768]{1,0:T(8,128)(2,1)} %collective-permute-done.b0), channel_id=1, source_target_pairs={{0,6},{2,0},{4,2},{6,4},{1,7},{3,1},{5,3},{7,5},{8,14},{10,8},{12,... | collective-permute-start | bytes 589832 | tf_op jit(solution)/shard_map/ppermute | solution.py:149
  69.4 15.8 %collective-permute-start.5 = (bf16[128,768]{1,0:T(8,128)(2,1)S(1)}, bf16[128,768]{1,0:T(8,128)(2,1)}, u32[]{:S(2)}, u32[]{:S(2)}) collective-permute-start(bf16[128,768]{1,0:T(8,128)(2,1)S(1)} %collective-permute-done.4.b0), channel_id=1, source_target_pairs={{0,4},{2,6},{4,0},{6,2},{1,5},{3,7},{5,1},{7,3},{8,12},{10,14},{12... | collective-permute-start | bytes 589832 | tf_op jit(solution)/shard_map/ppermute | solution.py:149
  71.3 13.9 %collective-permute-start.6 = (bf16[128,768]{1,0:T(8,128)(2,1)S(1)}, bf16[128,768]{1,0:T(8,128)(2,1)}, u32[]{:S(2)}, u32[]{:S(2)}) collective-permute-start(bf16[128,768]{1,0:T(8,128)(2,1)S(1)} %collective-permute-done.4.b0), channel_id=1, source_target_pairs={{0,2},{2,4},{4,6},{6,0},{1,3},{3,5},{5,7},{7,1},{8,10},{10,12},{12... | collective-permute-start | bytes 589832 | tf_op jit(solution)/shard_map/ppermute | solution.py:149
  74.1 0.7 copy-start.12
  74.8 10.5 %collective-permute-start.7 = (bf16[128,768]{1,0:T(8,128)(2,1)S(1)}, bf16[128,768]{1,0:T(8,128)(2,1)}, u32[]{:S(2)}, u32[]{:S(2)}) collective-permute-start(bf16[128,768]{1,0:T(8,128)(2,1)S(1)} %collective-permute-done.4.b0), channel_id=1, source_target_pairs={{0,6},{2,0},{4,2},{6,4},{1,7},{3,1},{5,3},{7,5},{8,14},{10,8},{12,... | collective-permute-start | bytes 589832 | tf_op jit(solution)/shard_map/ppermute | solution.py:149
  80.4 1.0 copy-start.4
  81.3 1.7 %copy-start.5 = (bf16[256,768]{1,0:T(8,128)(2,1)S(1)}, bf16[256,768]{1,0:T(8,128)(2,1)}, u32[]{:S(2)}) copy-start(bf16[256,768]{1,0:T(8,128)(2,1)} %copy-done.3) | copy-start | bytes 1179652
  81.4 1.7 %copy-start.13 = (bf16[128,768]{1,0:T(8,128)(2,1)S(1)}, bf16[128,768]{1,0:T(8,128)(2,1)}, u32[]{:S(2)}) copy-start(bf16[128,768]{1,0:T(8,128)(2,1)} %copy-done.12) | copy-start | bytes 589828
  83.0 2.3 %copy-start.7 = (f32[256,768]{1,0:T(8,128)S(1)}, f32[256,768]{1,0:T(8,128)}, u32[]{:S(2)}) copy-start(f32[256,768]{1,0:T(8,128)} %copy-done.6) | copy-start | bytes 2359300
  83.0 2.3 %copy-start.11 = (bf16[576,256]{1,0:T(8,128)(2,1)S(1)}, bf16[576,256]{1,0:T(8,128)(2,1)}, u32[]{:S(2)}) copy-start(bf16[576,256]{1,0:T(8,128)(2,1)} %fusion.18.theirs) | copy-start | bytes 884740
  83.0 2.3 %copy-start.15 = (f32[256,128]{1,0:T(8,128)S(1)}, f32[256,128]{1,0:T(8,128)}, u32[]{:S(2)}) copy-start(f32[256,128]{1,0:T(8,128)} %copy-done.14) | copy-start | bytes 393220
  88.4 4.4 %copy-start.10 = (bf16[576,256]{1,0:T(8,128)(2,1)S(1)}, bf16[576,256]{1,0:T(8,128)(2,1)}, u32[]{:S(2)}) copy-start(bf16[576,256]{1,0:T(8,128)(2,1)} %fusion.19.mine) | copy-start | bytes 884740
  88.4 4.4 %collective-permute-start.8 = (bf16[448,768]{1,0:T(8,128)(2,1)}, bf16[448,768]{1,0:T(8,128)(2,1)S(1)}, u32[]{:S(2)}, u32[]{:S(2)}) collective-permute-start(bf16[448,768]{1,0:T(8,128)(2,1)} %get-tuple-element.28), channel_id=1, source_target_pairs={{0,8},{8,0},{1,9},{9,1},{2,10},{10,2},{3,11},{11,3},{4,12},{12,4},... | collective-permute-start | bytes 2064392 | tf_op jit(solution)/shard_map/ppermute | solution.py:192

commit v5 on v3

--- a/solution.py
+++ b/solution.py
@@ -37,13 +37,14 @@
     return (raw * inverse, inverse)
 
 
-def video_kernel(feats, head, whole, first, second):
+def video_kernel(feats, head, whole):
     unit, unused_inv = embed(feats[...], head[...])
-    emb = unit.astype(BF16)
-    cut = first.shape[0]
-    whole[...] = emb
-    first[...] = emb[:cut]
-    second[...] = emb[cut:]
+    whole[...] = unit.astype(BF16)
+
+
+def copies_kernel(block, out):
+    for k in range(out.shape[0]):
+        out[k] = block[...]
 
 
 def weighted(sharp, offset, emb, block, diagonal):
@@ -72,20 +73,11 @@
     total[...] = acc
 
 
-def far_sum(sharp, offset, emb, total, b0, b1, b2, b3):
+def last_kernel(sharp, offset, emb, total, row, unit, inv, theirs, out, packed):
     acc = total[...]
-    for pair in ((b0, b1), (b2, b3)):
-        block = jnp.concatenate([pair[0][...], pair[1][...]], axis=0)
-        acc += weighted(sharp[0], offset[0], emb[...], block, False)
-    return acc
-
-
-def far_kernel(sharp, offset, emb, total, b0, b1, b2, b3, out):
-    out[...] = far_sum(sharp, offset, emb, total, b0, b1, b2, b3)
-
-
-def last_kernel(sharp, offset, emb, total, b0, b1, b2, b3, unit, inv, theirs, out, packed):
-    grad = sharp[0] * far_sum(sharp, offset, emb, total, b0, b1, b2, b3)
+    for k in range(row.shape[0]):
+        acc += weighted(sharp[0], offset[0], emb[...], row[k], False)
+    grad = sharp[0] * acc
     text_unit = unit[...]
     inner = jnp.sum(text_unit * grad, axis=-1, keepdims=True)
     raw = (inv[:, :1] * (grad - text_unit * inner)).astype(BF16)
@@ -131,15 +123,14 @@
     piece_c = width // (nx * nzh)
     core = lax.axis_index("c")
     scalars = (sigmoid_sharpness_array, sigmoid_offset_array)
-    part = rows // 2
     dots = 2 * rows * rows * width
 
     def shape(*dims, kind=BF16):
         return jax.ShapeDtypeStruct(dims, kind)
 
-    whole, first, second = call(
+    whole = call(
         video_kernel,
-        [shape(rows, width), shape(part, width), shape(part, width)],
+        shape(rows, width),
         [VMEM] * 2,
         2 * rows * feat * width,
     )(visual_tower_outputs, visual_mapping_frozen)
@@ -147,7 +138,7 @@
     def around(block):
         return [lax.ppermute(block, "x", ring(nx, k)) for k in (2, 1, 3)]
 
-    first = lax.ppermute(first, "zh", ring(2, 1))
+    across = lax.ppermute(whole, "zh", ring(2, 1))
 
     half = feat // 2
     place = lax.broadcasted_iota(jnp.int32, (half, feat), 0)
@@ -165,28 +156,23 @@
     whole, mine, theirs = lax.optimization_barrier((whole, mine, theirs))
     near = around(whole)
 
-    second, first = lax.optimization_barrier((second, first))
-    second = lax.ppermute(second, "zh", ring(2, 1))
-    feats, first = lax.optimization_barrier((language_tower_outputs, first))
     unit, inv, emb = call(
         text_kernel,
         [shape(rows, width, kind=F32), shape(rows, 128, kind=F32), shape(rows, width)],
         [VMEM] * 2,
-        20_000_000_000,
-    )(feats, language_mapping_learnable)
-    first, mine, theirs, emb, near = lax.optimization_barrier((first, mine, theirs, emb, near))
+        2 * rows * feat * width,
+    )(language_tower_outputs, language_mapping_learnable)
     total = call(near_kernel, shape(rows, width, kind=F32), [SMEM] * 2 + [VMEM] * 5, 8 * dots)(
         *scalars, emb, whole, *near
     )
-    total = call(far_kernel, shape(rows, width, kind=F32), [SMEM] * 2 + [VMEM] * 6, 4 * dots)(
-        *scalars, emb, total, first, *around(first)
-    )
+    copies = call(copies_kernel, shape(nx, rows, width), [VMEM], 1_000_000)(across)
+    far = lax.all_to_all(copies, "x", 0, 0, tiled=True)
     raw_grad, packed = call(
         last_kernel,
         [shape(rows, width), shape(rows + half // 3, width)],
-        [SMEM] * 2 + [VMEM] * 9,
-        4 * dots,
-    )(*scalars, emb, total, second, *around(second), unit, inv, theirs)
+        [SMEM] * 2 + [VMEM] * 6,
+        8 * dots,
+    )(*scalars, emb, total, far, unit, inv, theirs)
 
     other = lax.ppermute(packed, "c", ring(2, 1))
     text_grad = lax.dot_general(

time: 131 us -> 159 us (1.21)
  waiting for transfers between devices: 25.9 us -> 69.5 us
  starting transfers between devices: 65.2 us -> 37.8 us
  local copies, waits for them, and re-layouts: 2.8 us -> 9.56 us
  blocking collectives: 22.1 us -> 25 us
  matrix products: 4.35 us -> 5.94 us
    ppermute x2 -> x1, waiting for transfers between devices: 4.71 us -> 34.7 us  [local(): across = lax.ppermute(whole, 'zh', ring(2, 1))]
    ppermute x9 -> x3, starting transfers between devices: 31.7 us -> 11.3 us  [around(): return [lax.ppermute(block, 'x', ring(nx, k)) for k in (2, 1, 3)]]
    ppermute x9 -> x3, waiting for transfers between devices: 4.39 us -> 18.1 us  [around(): return [lax.ppermute(block, 'x', ring(nx, k)) for k in (2, 1, 3)]]
    ppermute x2 -> x1, starting transfers between devices: 27 us -> 14.8 us  [local(): across = lax.ppermute(whole, 'zh', ring(2, 1))]
    unnamed x8 -> x30, local copies, waits for them, and re-layouts: 2.54 us -> 9.31 us
    all_to_all x0 -> x1, starting transfers between devices: none -> 4.44 us  [local(): far = lax.all_to_all(copies, 'x', 0, 0, tiled=True)]
    all_to_all x1, blocking collectives: 22.1 us -> 25 us  [local(): term = lax.all_to_all(term, ('zl', 'zh'), 0, 0, tiled=True)]
    dot_general x2, matrix products: 2.82 us -> 4.41 us  [columns_of(): lax.dot_general(pick, language_tower_outputs, NT, preferred_element_type=...]
  transfers between devices with their start and end apart: 13 -> 7, of which waited for: 6 -> 6; matrix products, arithmetic and copies ran while one was open for 3% -> 4% of each run, Pallas kernels for 3% -> 2%
where the time goes in v5:
time: 159 us; the launch traced here: 158 us
  waiting for transfers between devices  69.5 us (44%)
  starting transfers between devices  37.8 us (24%)
  blocking collectives  25 us (16%)
  local copies, waits for them, and re-layouts  9.56 us (6%)
  Pallas kernels  7.55 us (5%)
  matrix products  5.94 us (4%)
  between operations  2.15 us (1%)
    ppermute x1, waiting for transfers between devices, local(): across = lax.ppermute(whole, 'zh', ring(2, 1))  34.7 us
    all_to_all x1, blocking collectives, local(): term = lax.all_to_all(term, ('zl', 'zh'), 0, 0, tiled=True)  25 us
    ppermute x3, waiting for transfers between devices, around(): return [lax.ppermute(block, 'x', ring(nx, k)) for k in (2, 1, 3)]  18.1 us
    all_to_all x1, waiting for transfers between devices, local(): term = lax.all_to_all(term, ('y', 'x'), 0, 0, tiled=True)  16.2 us
    ppermute x1, starting transfers between devices, local(): across = lax.ppermute(whole, 'zh', ring(2, 1))  14.8 us
    ppermute x3, starting transfers between devices, around(): return [lax.ppermute(block, 'x', ring(nx, k)) for k in (2, 1, 3)]  11.3 us
    unnamed x30, local copies, waits for them, and re-layouts  9.31 us
    all_to_all x1, starting transfers between devices, local(): term = lax.all_to_all(term, ('y', 'x'), 0, 0, tiled=True)  5.18 us
  transfers between devices with their start and end apart: 7, of which 6 were waited for; matrix products, arithmetic and copies ran while one was open for 4% of the time, Pallas kernels for 2%

profile of v5, /device:TPU:32, one launch (start us, length us, event | category | flops | bytes accessed | tf_op | source)
XLA Modules:
  0.0 158.3 jit_solution(6870121845351487681)
XLA Ops:
  0.6 1.5 copy-done.1
  2.1 1.1 copy-done.6
  3.2 0.8 shard_map.78.b0
  4.0 14.8 %collective-permute-start.3 = (bf16[256,768]{1,0:T(8,128)(2,1)S(1)}, bf16[256,768]{1,0:T(8,128)(2,1)S(1)}, u32[]{:S(2)}, u32[]{:S(2)}) collective-permute-start(bf16[256,768]{1,0:T(8,128)(2,1)S(1)} %shard_map.78.b0), channel_id=1, source_target_pairs={{0,1},{1,0},{2,3},{3,2},{4,5},{5,4},{6,7},{7,6},{8,9},{9,8},{10,11... | collective-permute-start | bytes 1179656 | tf_op jit(solution)/shard_map/ppermute | solution.py:141
  18.8 34.7 %collective-permute-done.3.block = bf16[256,768]{1,0:T(8,128)(2,1)S(1)} collective-permute-done((bf16[256,768]{1,0:T(8,128)(2,1)S(1)}, bf16[256,768]{1,0:T(8,128)(2,1)S(1)}, u32[]{:S(2)}, u32[]{:S(2)}) %collective-permute-start.3) | collective-permute-done | bytes 393248 | tf_op jit(solution)/shard_map/ppermute | solution.py:141
  53.5 1.3 shard_map.80
  54.7 4.4 %all-to-all-start = ((bf16[4,256,768]{2,1,0:T(8,128)(2,1)}), bf16[4,256,768]{2,1,0:T(8,128)(2,1)S(1)}, u32[]{:S(2)}, u32[]{:S(2)}) async-start(bf16[4,256,768]{2,1,0:T(8,128)(2,1)} %shard_map.80), calls=%async_computation | async-start | bytes 3145728 | tf_op jit(solution)/shard_map/all_to_all | solution.py:169
  59.2 2.2 %fusion.19.mine = bf16[576,256]{1,0:T(8,128)(2,1)} fusion(bf16[256,1152]{1,0:T(8,128)(2,1)S(1)} %copy-done.7, s32[]{:T(128)S(6)} %mul.16, s32[576]{0:T(1024)S(1)} %get-tuple-element.25, s32[576]{0:T(1024)S(1)} %get-tuple-element.26, s32[576]{0:T(1024)S(1)} %get-tuple-element.24, s32[576]{0:T(1024)S(1)} %get-tuple-element.27, ...), kind=kOutput, calls=%fused_computation.24 | convolution fusion | flops 343867392 | bytes 895108 | tf_op jit(solution)/shard_map/dot_general | solution.py:150
  61.4 2.2 %fusion.18.theirs = bf16[576,256]{1,0:T(8,128)(2,1)} fusion(bf16[256,1152]{1,0:T(8,128)(2,1)S(1)} %copy-done.8, s32[]{:T(128)S(6)} %mul.17, s32[576]{0:T(1024)S(1)} %get-tuple-element.25, s32[576]{0:T(1024)S(1)} %get-tuple-element.26, s32[576]{0:T(1024)S(1)} %get-tuple-element.24, s32[576]{0:T(1024)S(1)} %get-tuple-element.27, ...), kind=kOutput, calls=%fused_computation.23 | convolution fusion | flops 343867392 | bytes 895108 | tf_op jit(solution)/shard_map/dot_general | solution.py:150
  63.6 5.1 %collective-permute-start.2 = (bf16[256,768]{1,0:T(8,128)(2,1)S(1)}, bf16[256,768]{1,0:T(8,128)(2,1)S(1)}, u32[]{:S(2)}, u32[]{:S(2)}) collective-permute-start(bf16[256,768]{1,0:T(8,128)(2,1)S(1)} %copy-done.12), channel_id=1, source_target_pairs={{0,6},{2,0},{4,2},{6,4},{1,7},{3,1},{5,3},{7,5},{8,14},{10,8},{12,... | collective-permute-start | bytes 1179656 | tf_op jit(solution)/shard_map/ppermute | solution.py:139
  68.8 1.9 %collective-permute-start.1 = (bf16[256,768]{1,0:T(8,128)(2,1)S(1)}, bf16[256,768]{1,0:T(8,128)(2,1)S(1)}, u32[]{:S(2)}, u32[]{:S(2)}) collective-permute-start(bf16[256,768]{1,0:T(8,128)(2,1)S(1)} %copy-done.12), channel_id=1, source_target_pairs={{0,2},{2,4},{4,6},{6,0},{1,3},{3,5},{5,7},{7,1},{8,10},{10,12},{12... | collective-permute-start | bytes 1179656 | tf_op jit(solution)/shard_map/ppermute | solution.py:139
  70.7 4.2 %collective-permute-start = (bf16[256,768]{1,0:T(8,128)(2,1)S(1)}, bf16[256,768]{1,0:T(8,128)(2,1)S(1)}, u32[]{:S(2)}, u32[]{:S(2)}) collective-permute-start(bf16[256,768]{1,0:T(8,128)(2,1)S(1)} %copy-done.12), channel_id=1, source_target_pairs={{0,4},{2,6},{4,0},{6,2},{1,5},{3,7},{5,1},{7,3},{8,12},{10,14},{12... | collective-permute-start | bytes 1179656 | tf_op jit(solution)/shard_map/ppermute | solution.py:139
  76.2 0.8 shard_map.77
  77.0 0.9 copy-done.2
  77.9 10.4 %collective-permute-done.2.b3 = bf16[256,768]{1,0:T(8,128)(2,1)S(1)} collective-permute-done((bf16[256,768]{1,0:T(8,128)(2,1)S(1)}, bf16[256,768]{1,0:T(8,128)(2,1)S(1)}, u32[]{:S(2)}, u32[]{:S(2)}) %collective-permute-start.2) | collective-permute-done | bytes 393248 | tf_op jit(solution)/shard_map/ppermute | solution.py:139
  88.3 1.2 collective-permute-done.1.b2
  89.5 6.5 %collective-permute-done.b1 = bf16[256,768]{1,0:T(8,128)(2,1)S(1)} collective-permute-done((bf16[256,768]{1,0:T(8,128)(2,1)S(1)}, bf16[256,768]{1,0:T(8,128)(2,1)S(1)}, u32[]{:S(2)}, u32[]{:S(2)}) %collective-permute-start) | collective-permute-done | bytes 393248 | tf_op jit(solution)/shard_map/ppermute | solution.py:139
  96.0 1.6 %shard_map.79.total = f32[256,768]{1,0:T(8,128)S(1)} custom-call(f32[1]{0:T(128)S(6)} %copy.11.sharp, f32[1]{0:T(128)S(6)} %copy.12.offset, bf16[256,768]{1,0:T(8,128)(2,1)S(1)} %get-tuple-element.12.emb, bf16[256,768]{1,0:T(8,128)(2,1)S(1)} %copy-done.12, bf16[256,768]{1,0:T(8,128)(2,1)S(1)} %collective-permute-done.b1, ...), custom_call_target="tpu_custom_call" | custom-call | flops 805306368 | bytes 4000000 | tf_op jit(solution)/shard_map/pallas_call | solution.py:165
  97.6 0.9 copy-done.4
  98.5 0.7 copy-done.9
  99.2 1.1 copy-done.3
  100.4 1.1 copy-done.5
  101.5 1.0 copy-done.10
  102.5 1.0 copy-done.14
  103.5 1.5 shard_map.81
  105.0 2.1 %collective-permute-start.4 = (bf16[448,768]{1,0:T(8,128)(2,1)S(1)}, bf16[448,768]{1,0:T(8,128)(2,1)S(1)}, u32[]{:S(2)}, u32[]{:S(2)}) collective-permute-start(bf16[448,768]{1,0:T(8,128)(2,1)S(1)} %get-tuple-element.17), channel_id=1, source_target_pairs={{0,8},{8,0},{1,9},{9,1},{2,10},{10,2},{3,11},{11,3},{4,12},{12,4},... | collective-permute-start | bytes 2064392 | tf_op jit(solution)/shard_map/ppermute | solution.py:177
  107.0 1.5 convolution_convert_fusion
  109.2 1.6 %shard_map.82 = bf16[16,224,128]{2,1,0:T(8,128)(2,1)} custom-call(bf16[576,256]{1,0:T(8,128)(2,1)S(1)} %copy-done.13, bf16[256,768]{1,0:T(8,128)(2,1)S(1)} %get-tuple-element.18.raw, bf16[448,768]{1,0:T(8,128)(2,1)S(1)} %collective-permute-done.4.other), custom_call_target="tpu_custom_call" | custom-call | flops 452984832 | bytes 4000000 | tf_op jit(solution)/shard_map/pallas_call | solution.py:183
  110.8 5.2 %all-to-all-start.1 = ((bf16[16,224,128]{2,1,0:T(8,128)(2,1)}), bf16[16,224,128]{2,1,0:T(8,128)(2,1)S(1)}, u32[]{:S(2)}, u32[]{:S(2)}) async-start(bf16[16,224,128]{2,1,0:T(8,128)(2,1)} %shard_map.82), calls=%async_computation.1 | async-start | bytes 1835008 | tf_op jit(solution)/shard_map/all_to_all | solution.py:190
  116.0 16.2 %all-to-all-done.1 = bf16[16,224,128]{2,1,0:T(8,128)(2,1)S(1)} async-done(((bf16[16,224,128]{2,1,0:T(8,128)(2,1)}), bf16[16,224,128]{2,1,0:T(8,128)(2,1)S(1)}, u32[]{:S(2)}, u32[]{:S(2)}) %all-to-all-start.1) | async-done | bytes 917536 | tf_op jit(solution)/shard_map/all_to_all | solution.py:190
  132.7 25.0 %all_to_all.15 = bf16[16,18,96]{2,1,0:T(8,128)(2,1)S(1)} all-to-all(bf16[16,18,96]{2,1,0:T(8,128)(2,1)S(1)} %copy.10), channel_id=1, replica_groups=mesh['y'=4,'zl'=8,'c'=2,'x'=4,'zh'=2] {'zl','zh'}, dimensions={0} | all-to-all | bytes 110592 | tf_op jit(solution)/shard_map/all_to_all | solution.py:200
  157.7 0.6 broadcast_multiply_fusion
  (34 shorter events, 1.2 us)
Async XLA Ops:
  0.6 1.5 copy-start.1
  2.1 1.1 copy-start.6
  3.9 49.5 %copy-start.11 = (bf16[256,768]{1,0:T(8,128)(2,1)}, bf16[256,768]{1,0:T(8,128)(2,1)S(1)}, u32[]{:S(2)}) copy-start(bf16[256,768]{1,0:T(8,128)(2,1)S(1)} %shard_map.78.b0) | copy-start | bytes 1179652
  4.0 49.5 %collective-permute-start.3 = (bf16[256,768]{1,0:T(8,128)(2,1)S(1)}, bf16[256,768]{1,0:T(8,128)(2,1)S(1)}, u32[]{:S(2)}, u32[]{:S(2)}) collective-permute-start(bf16[256,768]{1,0:T(8,128)(2,1)S(1)} %shard_map.78.b0), channel_id=1, source_target_pairs={{0,1},{1,0},{2,3},{3,2},{4,5},{5,4},{6,7},{7,6},{8,9},{9,8},{10,11... | collective-permute-start | bytes 1179656 | tf_op jit(solution)/shard_map/ppermute | solution.py:141
  54.7 4.5 %copy-start.7 = (bf16[256,1152]{1,0:T(8,128)(2,1)S(1)}, bf16[256,1152]{1,0:T(8,128)(2,1)}, u32[]{:S(2)}) copy-start(bf16[256,1152]{1,0:T(8,128)(2,1)} %feats.2) | copy-start | bytes 1769476
  54.7 44.5 %all-to-all-start = ((bf16[4,256,768]{2,1,0:T(8,128)(2,1)}), bf16[4,256,768]{2,1,0:T(8,128)(2,1)S(1)}, u32[]{:S(2)}, u32[]{:S(2)}) async-start(bf16[4,256,768]{2,1,0:T(8,128)(2,1)} %shard_map.80), calls=%async_computation | async-start | bytes 3145728 | tf_op jit(solution)/shard_map/all_to_all | solution.py:169
  59.2 2.2 %copy-start.8 = (bf16[256,1152]{1,0:T(8,128)(2,1)S(1)}, bf16[256,1152]{1,0:T(8,128)(2,1)}, u32[]{:S(2)}) copy-start(bf16[256,1152]{1,0:T(8,128)(2,1)} %feats.2) | copy-start | bytes 1769476
  61.4 2.2 %copy-start.12 = (bf16[256,768]{1,0:T(8,128)(2,1)S(1)}, bf16[256,768]{1,0:T(8,128)(2,1)}, u32[]{:S(2)}) copy-start(bf16[256,768]{1,0:T(8,128)(2,1)} %copy-done.11) | copy-start | bytes 1179652
  61.4 14.8 %copy-start = (bf16[1152,768]{1,0:T(8,128)(2,1)S(1)}, bf16[1152,768]{1,0:T(8,128)(2,1)}, u32[]{:S(2)}) copy-start(bf16[1152,768]{1,0:T(8,128)(2,1)} %head.2) | copy-start | bytes 5308420
  63.6 24.7 %collective-permute-start.2 = (bf16[256,768]{1,0:T(8,128)(2,1)S(1)}, bf16[256,768]{1,0:T(8,128)(2,1)S(1)}, u32[]{:S(2)}, u32[]{:S(2)}) collective-permute-start(bf16[256,768]{1,0:T(8,128)(2,1)S(1)} %copy-done.12), channel_id=1, source_target_pairs={{0,6},{2,0},{4,2},{6,4},{1,7},{3,1},{5,3},{7,5},{8,14},{10,8},{12,... | collective-permute-start | bytes 1179656 | tf_op jit(solution)/shard_map/ppermute | solution.py:139
  68.8 20.7 %collective-permute-start.1 = (bf16[256,768]{1,0:T(8,128)(2,1)S(1)}, bf16[256,768]{1,0:T(8,128)(2,1)S(1)}, u32[]{:S(2)}, u32[]{:S(2)}) collective-permute-start(bf16[256,768]{1,0:T(8,128)(2,1)S(1)} %copy-done.12), channel_id=1, source_target_pairs={{0,2},{2,4},{4,6},{6,0},{1,3},{3,5},{5,7},{7,1},{8,10},{10,12},{12... | collective-permute-start | bytes 1179656 | tf_op jit(solution)/shard_map/ppermute | solution.py:139
  70.7 25.3 %collective-permute-start = (bf16[256,768]{1,0:T(8,128)(2,1)S(1)}, bf16[256,768]{1,0:T(8,128)(2,1)S(1)}, u32[]{:S(2)}, u32[]{:S(2)}) collective-permute-start(bf16[256,768]{1,0:T(8,128)(2,1)S(1)} %copy-done.12), channel_id=1, source_target_pairs={{0,4},{2,6},{4,0},{6,2},{1,5},{3,7},{5,1},{7,3},{8,12},{10,14},{12... | collective-permute-start | bytes 1179656 | tf_op jit(solution)/shard_map/ppermute | solution.py:139
  77.0 0.9 copy-start.2
  97.6 0.9 copy-start.4
  98.5 0.7 copy-start.9
  99.2 1.1 copy-start.3
  100.4 1.1 copy-start.5
  101.5 1.0 copy-start.10
  102.5 1.0 copy-start.14
  105.0 4.2 %copy-start.13 = (bf16[576,256]{1,0:T(8,128)(2,1)S(1)}, bf16[576,256]{1,0:T(8,128)(2,1)}, u32[]{:S(2)}) copy-start(bf16[576,256]{1,0:T(8,128)(2,1)} %fusion.19.mine) | copy-start | bytes 884740
  105.0 4.2 %collective-permute-start.4 = (bf16[448,768]{1,0:T(8,128)(2,1)S(1)}, bf16[448,768]{1,0:T(8,128)(2,1)S(1)}, u32[]{:S(2)}, u32[]{:S(2)}) collective-permute-start(bf16[448,768]{1,0:T(8,128)(2,1)S(1)} %get-tuple-element.17), channel_id=1, source_target_pairs={{0,8},{8,0},{1,9},{9,1},{2,10},{10,2},{3,11},{11,3},{4,12},{12,4},... | collective-permute-start | bytes 2064392 | tf_op jit(solution)/shard_map/ppermute | solution.py:177
  110.8 21.4 %all-to-all-start.1 = ((bf16[16,224,128]{2,1,0:T(8,128)(2,1)}), bf16[16,224,128]{2,1,0:T(8,128)(2,1)S(1)}, u32[]{:S(2)}, u32[]{:S(2)}) async-start(bf16[16,224,128]{2,1,0:T(8,128)(2,1)} %shard_map.82), calls=%async_computation.1 | async-start | bytes 1835008 | tf_op jit(solution)/shard_map/all_to_all | solution.py:190

commit v6 on v3

--- a/solution.py
+++ b/solution.py
@@ -43,7 +43,8 @@
     cut = first.shape[0]
     whole[...] = emb
     first[...] = emb[:cut]
-    second[...] = emb[cut:]
+    for k in range(second.shape[0]):
+        second[k] = emb[cut:]
 
 
 def weighted(sharp, offset, emb, block, diagonal):
@@ -139,7 +140,7 @@
 
     whole, first, second = call(
         video_kernel,
-        [shape(rows, width), shape(part, width), shape(part, width)],
+        [shape(rows, width), shape(part, width), shape(nzh, part, width)],
         [VMEM] * 2,
         2 * rows * feat * width,
     )(visual_tower_outputs, visual_mapping_frozen)
@@ -148,6 +149,8 @@
         return [lax.ppermute(block, "x", ring(nx, k)) for k in (2, 1, 3)]
 
     first = lax.ppermute(first, "zh", ring(2, 1))
+    second = lax.all_to_all(second, "zh", 0, 0, tiled=True)
+    second = lax.dynamic_index_in_dim(second, 1 - lax.axis_index("zh"), 0, keepdims=False)
 
     half = feat // 2
     place = lax.broadcasted_iota(jnp.int32, (half, feat), 0)
@@ -165,8 +168,6 @@
     whole, mine, theirs = lax.optimization_barrier((whole, mine, theirs))
     near = around(whole)
 
-    second, first = lax.optimization_barrier((second, first))
-    second = lax.ppermute(second, "zh", ring(2, 1))
     feats, first = lax.optimization_barrier((language_tower_outputs, first))
     unit, inv, emb = call(
         text_kernel,

time: 131 us -> 131 us (level)
  starting transfers between devices: 65.2 us -> 60.1 us
  waiting for transfers between devices: 25.9 us -> 29.5 us
  blocking collectives: 22.1 us -> 19.1 us
  local copies, waits for them, and re-layouts: 2.8 us -> 5.21 us
  Pallas kernels: 6.85 us -> 8.73 us
    ppermute x1 -> x0, starting transfers between devices: 12.2 us -> none  [local(): second = lax.ppermute(second, 'zh', ring(2, 1))]
    all_to_all x0 -> x1, waiting for transfers between devices: none -> 8.6 us  [local(): second = lax.all_to_all(second, 'zh', 0, 0, tiled=True)]
    all_to_all x0 -> x1, starting transfers between devices: none -> 4.17 us  [local(): second = lax.all_to_all(second, 'zh', 0, 0, tiled=True)]
    ppermute x1 -> x0, waiting for transfers between devices: 4.16 us -> none  [local(): second = lax.ppermute(second, 'zh', ring(2, 1))]
    all_to_all x1, blocking collectives: 22.1 us -> 19.1 us  [local(): term = lax.all_to_all(term, ('zl', 'zh'), 0, 0, tiled=True)]
    all_to_all x1, starting transfers between devices: 4.56 us -> 6.32 us  [local(): term = lax.all_to_all(term, ('y', 'x'), 0, 0, tiled=True)]
    unnamed x8 -> x10, local copies, waits for them, and re-layouts: 2.54 us -> 4.01 us
  transfers between devices with their start and end apart: 13 -> 13, of which waited for: 6 -> 5; matrix products, arithmetic and copies ran while one was open for 3% -> 4% of each run, Pallas kernels for 3% -> 3%
where the time goes in v6:
time: 131 us; the launch traced here: 130 us
  starting transfers between devices  60.1 us (46%)
  waiting for transfers between devices  29.5 us (23%)
  blocking collectives  19.1 us (15%)
  Pallas kernels  8.73 us (7%)
  local copies, waits for them, and re-layouts  5.21 us (4%)
  matrix products  4.35 us (3%)
  between operations  2.26 us (2%)
    ppermute x9, starting transfers between devices, around(): return [lax.ppermute(block, 'x', ring(nx, k)) for k in (2, 1, 3)]  32.8 us
    all_to_all x1, blocking collectives, local(): term = lax.all_to_all(term, ('zl', 'zh'), 0, 0, tiled=True)  19.1 us
    all_to_all x1, waiting for transfers between devices, local(): term = lax.all_to_all(term, ('y', 'x'), 0, 0, tiled=True)  16.2 us
    ppermute x1, starting transfers between devices, local(): first = lax.ppermute(first, 'zh', ring(2, 1))  14.8 us
    all_to_all x1, waiting for transfers between devices, local(): second = lax.all_to_all(second, 'zh', 0, 0, tiled=True)  8.6 us
    all_to_all x1, starting transfers between devices, local(): term = lax.all_to_all(term, ('y', 'x'), 0, 0, tiled=True)  6.32 us
    all_to_all x1, starting transfers between devices, local(): second = lax.all_to_all(second, 'zh', 0, 0, tiled=True)  4.17 us
    ppermute x9, waiting for transfers between devices, around(): return [lax.ppermute(block, 'x', ring(nx, k)) for k in (2, 1, 3)]  4.13 us
  transfers between devices with their start and end apart: 13, of which 5 were waited for; matrix products, arithmetic and copies ran while one was open for 4% of the time, Pallas kernels for 3%

profile of v6, /device:TPU:32, one launch (start us, length us, event | category | flops | bytes accessed | tf_op | source)
XLA Modules:
  0.0 130.1 jit_solution(15063732151671525204)
XLA Ops:
  0.6 1.5 %copy-done = bf16[1152,768]{1,0:T(8,128)(2,1)S(1)} copy-done((bf16[1152,768]{1,0:T(8,128)(2,1)S(1)}, bf16[1152,768]{1,0:T(8,128)(2,1)}, u32[]{:S(2)}) %copy-start) | copy-done | bytes 1769496
  2.1 1.1 copy-done.1
  3.2 1.5 %shard_map.77 = (bf16[256,768]{1,0:T(8,128)(2,1)S(1)}, bf16[128,768]{1,0:T(8,128)(2,1)S(1)}, bf16[2,128,768]{2,1,0:T(8,128)(2,1)}) custom-call(bf16[256,1152]{1,0:T(8,128)(2,1)S(1)} %copy-done.1, bf16[1152,768]{1,0:T(8,128)(2,1)S(1)} %copy-done), custom_call_target="tpu_custom_call" | custom-call | flops 452984832 | bytes 4000000 | tf_op jit(solution)/shard_map/pallas_call | solution.py:141
  4.7 14.8 %collective-permute-start = (bf16[128,768]{1,0:T(8,128)(2,1)S(1)}, bf16[128,768]{1,0:T(8,128)(2,1)S(1)}, u32[]{:S(2)}, u32[]{:S(2)}) collective-permute-start(bf16[128,768]{1,0:T(8,128)(2,1)S(1)} %get-tuple-element.24), channel_id=1, source_target_pairs={{0,1},{1,0},{2,3},{3,2},{4,5},{5,4},{6,7},{7,6},{8,9},{9,8},{10,11... | collective-permute-start | bytes 589832 | tf_op jit(solution)/shard_map/ppermute | solution.py:151
  19.6 1.4 %fusion.18.theirs = bf16[576,256]{1,0:T(8,128)(2,1)S(1)} fusion(bf16[256,1152]{1,0:T(8,128)(2,1)S(1)} %copy-done.4, s32[]{:T(128)S(6)} %mul.17, s32[576]{0:T(1024)S(1)} %get-tuple-element.49, s32[576]{0:T(1024)S(1)} %get-tuple-element.50, s32[576]{0:T(1024)S(1)} %get-tuple-element.48, s32[576]{0:T(1024)S(1)} %get-tuple-element.51, ...), kind=kOutput, calls=%fused_computation.23 | convolution fusion | flops 343867392 | bytes 895108 | tf_op jit(solution)/shard_map/dot_general | solution.py:162
  21.0 1.4 %fusion.19.mine = bf16[576,256]{1,0:T(8,128)(2,1)S(1)} fusion(bf16[256,1152]{1,0:T(8,128)(2,1)S(1)} %copy-done.4, s32[]{:T(128)S(6)} %mul.16, s32[576]{0:T(1024)S(1)} %get-tuple-element.49, s32[576]{0:T(1024)S(1)} %get-tuple-element.50, s32[576]{0:T(1024)S(1)} %get-tuple-element.48, s32[576]{0:T(1024)S(1)} %get-tuple-element.51, ...), kind=kOutput, calls=%fused_computation.24 | convolution fusion | flops 343867392 | bytes 895108 | tf_op jit(solution)/shard_map/dot_general | solution.py:162
  22.4 4.9 %collective-permute-start.1 = (bf16[256,768]{1,0:T(8,128)(2,1)S(1)}, bf16[256,768]{1,0:T(8,128)(2,1)S(1)}, u32[]{:S(2)}, u32[]{:S(2)}) collective-permute-start(bf16[256,768]{1,0:T(8,128)(2,1)S(1)} %get-tuple-element.31.b0), channel_id=1, source_target_pairs={{0,4},{2,6},{4,0},{6,2},{1,5},{3,7},{5,1},{7,3},{8,12},{10,14},{12... | collective-permute-start | bytes 1179656 | tf_op jit(solution)/shard_map/ppermute | solution.py:149
  27.4 2.5 %collective-permute-start.2 = (bf16[256,768]{1,0:T(8,128)(2,1)S(1)}, bf16[256,768]{1,0:T(8,128)(2,1)}, u32[]{:S(2)}, u32[]{:S(2)}) collective-permute-start(bf16[256,768]{1,0:T(8,128)(2,1)S(1)} %get-tuple-element.31.b0), channel_id=1, source_target_pairs={{0,2},{2,4},{4,6},{6,0},{1,3},{3,5},{5,7},{7,1},{8,10},{10,12},{12... | collective-permute-start | bytes 1179656 | tf_op jit(solution)/shard_map/ppermute | solution.py:149
  29.9 4.6 %collective-permute-start.3 = (bf16[256,768]{1,0:T(8,128)(2,1)S(1)}, bf16[256,768]{1,0:T(8,128)(2,1)}, u32[]{:S(2)}, u32[]{:S(2)}) collective-permute-start(bf16[256,768]{1,0:T(8,128)(2,1)S(1)} %get-tuple-element.31.b0), channel_id=1, source_target_pairs={{0,6},{2,0},{4,2},{6,4},{1,7},{3,1},{5,3},{7,5},{8,14},{10,8},{12,... | collective-permute-start | bytes 1179656 | tf_op jit(solution)/shard_map/ppermute | solution.py:149
  34.4 4.2 %all-to-all-start = ((bf16[2,128,768]{2,1,0:T(8,128)(2,1)}), bf16[2,128,768]{2,1,0:T(8,128)(2,1)}, u32[]{:S(2)}, u32[]{:S(2)}) async-start(bf16[2,128,768]{2,1,0:T(8,128)(2,1)} %get-tuple-element.37), calls=%async_computation | async-start | bytes 786432 | tf_op jit(solution)/shard_map/all_to_all | solution.py:152
  38.6 1.5 %copy-done.2 = bf16[1152,768]{1,0:T(8,128)(2,1)S(1)} copy-done((bf16[1152,768]{1,0:T(8,128)(2,1)S(1)}, bf16[1152,768]{1,0:T(8,128)(2,1)}, u32[]{:S(2)}) %copy-start.2) | copy-done | bytes 1769496
  40.1 0.8 shard_map.78
  40.9 4.0 %collective-permute-done.2.b2 = bf16[256,768]{1,0:T(8,128)(2,1)} collective-permute-done((bf16[256,768]{1,0:T(8,128)(2,1)S(1)}, bf16[256,768]{1,0:T(8,128)(2,1)}, u32[]{:S(2)}, u32[]{:S(2)}) %collective-permute-start.2) | collective-permute-done | bytes 393248 | tf_op jit(solution)/shard_map/ppermute | solution.py:149
  45.0 4.8 %collective-permute-start.4 = (bf16[128,768]{1,0:T(8,128)(2,1)S(1)}, bf16[128,768]{1,0:T(8,128)(2,1)S(1)}, u32[]{:S(2)}, u32[]{:S(2)}) collective-permute-start(bf16[128,768]{1,0:T(8,128)(2,1)S(1)} %collective-permute-done.b0), channel_id=1, source_target_pairs={{0,4},{2,6},{4,0},{6,2},{1,5},{3,7},{5,1},{7,3},{8,12},{10,14},{12... | collective-permute-start | bytes 589832 | tf_op jit(solution)/shard_map/ppermute | solution.py:149
  49.8 2.5 %collective-permute-start.5 = (bf16[128,768]{1,0:T(8,128)(2,1)S(1)}, bf16[128,768]{1,0:T(8,128)(2,1)S(1)}, u32[]{:S(2)}, u32[]{:S(2)}) collective-permute-start(bf16[128,768]{1,0:T(8,128)(2,1)S(1)} %collective-permute-done.b0), channel_id=1, source_target_pairs={{0,2},{2,4},{4,6},{6,0},{1,3},{3,5},{5,7},{7,1},{8,10},{10,12},{12... | collective-permute-start | bytes 589832 | tf_op jit(solution)/shard_map/ppermute | solution.py:149
  52.4 4.5 %collective-permute-start.6 = (bf16[128,768]{1,0:T(8,128)(2,1)S(1)}, bf16[128,768]{1,0:T(8,128)(2,1)S(1)}, u32[]{:S(2)}, u32[]{:S(2)}) collective-permute-start(bf16[128,768]{1,0:T(8,128)(2,1)S(1)} %collective-permute-done.b0), channel_id=1, source_target_pairs={{0,6},{2,0},{4,2},{6,4},{1,7},{3,1},{5,3},{7,5},{8,14},{10,8},{12,... | collective-permute-start | bytes 589832 | tf_op jit(solution)/shard_map/ppermute | solution.py:149
  56.9 8.6 %all-to-all-done = bf16[2,128,768]{2,1,0:T(8,128)(2,1)} async-done(((bf16[2,128,768]{2,1,0:T(8,128)(2,1)}), bf16[2,128,768]{2,1,0:T(8,128)(2,1)}, u32[]{:S(2)}, u32[]{:S(2)}) %all-to-all-start) | async-done | bytes 393248 | tf_op jit(solution)/shard_map/all_to_all | solution.py:152
  65.5 0.9 dynamic-slice_bitcast_fusion.b0
  66.5 1.9 %collective-permute-start.7 = (bf16[128,768]{1,0:T(8,128)(2,1)S(1)}, bf16[128,768]{1,0:T(8,128)(2,1)S(1)}, u32[]{:S(2)}, u32[]{:S(2)}) collective-permute-start(bf16[128,768]{1,0:T(8,128)(2,1)S(1)} %dynamic-slice_bitcast_fusion.b0), channel_id=1, source_target_pairs={{0,4},{2,6},{4,0},{6,2},{1,5},{3,7},{5,1},{7,3},{8,12},{10,14},{12... | collective-permute-start | bytes 589832 | tf_op jit(solution)/shard_map/ppermute | solution.py:149
  68.4 3.2 %collective-permute-start.8 = (bf16[128,768]{1,0:T(8,128)(2,1)S(1)}, bf16[128,768]{1,0:T(8,128)(2,1)S(1)}, u32[]{:S(2)}, u32[]{:S(2)}) collective-permute-start(bf16[128,768]{1,0:T(8,128)(2,1)S(1)} %dynamic-slice_bitcast_fusion.b0), channel_id=1, source_target_pairs={{0,2},{2,4},{4,6},{6,0},{1,3},{3,5},{5,7},{7,1},{8,10},{10,12},{12... | collective-permute-start | bytes 589832 | tf_op jit(solution)/shard_map/ppermute | solution.py:149
  71.6 3.8 %collective-permute-start.9 = (bf16[128,768]{1,0:T(8,128)(2,1)S(1)}, bf16[128,768]{1,0:T(8,128)(2,1)S(1)}, u32[]{:S(2)}, u32[]{:S(2)}) collective-permute-start(bf16[128,768]{1,0:T(8,128)(2,1)S(1)} %dynamic-slice_bitcast_fusion.b0), channel_id=1, source_target_pairs={{0,6},{2,0},{4,2},{6,4},{1,7},{3,1},{5,3},{7,5},{8,14},{10,8},{12,... | collective-permute-start | bytes 589832 | tf_op jit(solution)/shard_map/ppermute | solution.py:149
  76.8 2.7 %shard_map.79.total = f32[256,768]{1,0:T(8,128)S(1)} custom-call(f32[1]{0:T(128)S(6)} %copy.11.sharp, f32[1]{0:T(128)S(6)} %copy.12.offset, bf16[256,768]{1,0:T(8,128)(2,1)S(1)} %get-tuple-element.32.emb, bf16[256,768]{1,0:T(8,128)(2,1)S(1)} %get-tuple-element.31.b0, bf16[256,768]{1,0:T(8,128)(2,1)S(1)} %collective-permute-done.1.b1, ...), custom_call_target="tpu_custom_call" | custom-call | flops 805306368 | bytes 4000000 | tf_op jit(solution)/shard_map/pallas_call | solution.py:179
  79.5 1.0 shard_map.80.total
  80.5 1.1 shard_map.81
  81.6 1.9 %collective-permute-start.10 = (bf16[448,768]{1,0:T(8,128)(2,1)S(1)}, bf16[448,768]{1,0:T(8,128)(2,1)S(1)}, u32[]{:S(2)}, u32[]{:S(2)}) collective-permute-start(bf16[448,768]{1,0:T(8,128)(2,1)S(1)} %get-tuple-element.41), channel_id=1, source_target_pairs={{0,8},{8,0},{1,9},{9,1},{2,10},{10,2},{3,11},{11,3},{4,12},{12,4},... | collective-permute-start | bytes 2064392 | tf_op jit(solution)/shard_map/ppermute | solution.py:192
  83.6 1.5 %convolution_convert_fusion = bf16[256,1152]{1,0:T(8,128)(2,1)} fusion(bf16[256,768]{1,0:T(8,128)(2,1)S(1)} %get-tuple-element.42.raw, bf16[1152,768]{1,0:T(8,128)(2,1)S(1)} %copy-done.3), kind=kOutput, calls=%fused_computation.5 | convolution fusion | flops 453279744 | bytes 2752512 | tf_op jit(solution)/shard_map/dot_general | solution.py:193
  85.1 0.6 collective-permute-done.10.other
  85.7 1.6 %shard_map.82 = bf16[16,224,128]{2,1,0:T(8,128)(2,1)} custom-call(bf16[576,256]{1,0:T(8,128)(2,1)S(1)} %fusion.19.mine, bf16[256,768]{1,0:T(8,128)(2,1)S(1)} %get-tuple-element.42.raw, bf16[448,768]{1,0:T(8,128)(2,1)S(1)} %collective-permute-done.10.other), custom_call_target="tpu_custom_call" | custom-call | flops 452984832 | bytes 4000000 | tf_op jit(solution)/shard_map/pallas_call | solution.py:198
  87.3 6.3 %all-to-all-start.1 = ((bf16[16,224,128]{2,1,0:T(8,128)(2,1)}), bf16[16,224,128]{2,1,0:T(8,128)(2,1)S(1)}, u32[]{:S(2)}, u32[]{:S(2)}) async-start(bf16[16,224,128]{2,1,0:T(8,128)(2,1)} %shard_map.82), calls=%async_computation.1 | async-start | bytes 1835008 | tf_op jit(solution)/shard_map/all_to_all | solution.py:205
  93.7 16.2 %all-to-all-done.1 = bf16[16,224,128]{2,1,0:T(8,128)(2,1)S(1)} async-done(((bf16[16,224,128]{2,1,0:T(8,128)(2,1)}), bf16[16,224,128]{2,1,0:T(8,128)(2,1)S(1)}, u32[]{:S(2)}, u32[]{:S(2)}) %all-to-all-start.1) | async-done | bytes 917536 | tf_op jit(solution)/shard_map/all_to_all | solution.py:205
  110.4 19.1 %all_to_all.15 = bf16[16,18,96]{2,1,0:T(8,128)(2,1)S(1)} all-to-all(bf16[16,18,96]{2,1,0:T(8,128)(2,1)S(1)} %copy.10), channel_id=1, replica_groups=mesh['y'=4,'zl'=8,'c'=2,'x'=4,'zh'=2] {'zl','zh'}, dimensions={0} | all-to-all | bytes 110592 | tf_op jit(solution)/shard_map/all_to_all | solution.py:215
  129.5 0.6 broadcast_multiply_fusion
  (27 shorter events, 0.7 us)
Async XLA Ops:
  0.6 1.5 %copy-start = (bf16[1152,768]{1,0:T(8,128)(2,1)S(1)}, bf16[1152,768]{1,0:T(8,128)(2,1)}, u32[]{:S(2)}) copy-start(bf16[1152,768]{1,0:T(8,128)(2,1)} %head.2) | copy-start | bytes 5308420
  2.1 1.1 copy-start.1
  3.2 16.4 %copy-start.4 = (bf16[256,1152]{1,0:T(8,128)(2,1)S(1)}, bf16[256,1152]{1,0:T(8,128)(2,1)}, u32[]{:S(2)}) copy-start(bf16[256,1152]{1,0:T(8,128)(2,1)} %feats.2) | copy-start | bytes 1769476
  4.7 33.9 %collective-permute-start = (bf16[128,768]{1,0:T(8,128)(2,1)S(1)}, bf16[128,768]{1,0:T(8,128)(2,1)S(1)}, u32[]{:S(2)}, u32[]{:S(2)}) collective-permute-start(bf16[128,768]{1,0:T(8,128)(2,1)S(1)} %get-tuple-element.24), channel_id=1, source_target_pairs={{0,1},{1,0},{2,3},{3,2},{4,5},{5,4},{6,7},{7,6},{8,9},{9,8},{10,11... | collective-permute-start | bytes 589832 | tf_op jit(solution)/shard_map/ppermute | solution.py:151
  22.4 18.5 %collective-permute-start.1 = (bf16[256,768]{1,0:T(8,128)(2,1)S(1)}, bf16[256,768]{1,0:T(8,128)(2,1)S(1)}, u32[]{:S(2)}, u32[]{:S(2)}) collective-permute-start(bf16[256,768]{1,0:T(8,128)(2,1)S(1)} %get-tuple-element.31.b0), channel_id=1, source_target_pairs={{0,4},{2,6},{4,0},{6,2},{1,5},{3,7},{5,1},{7,3},{8,12},{10,14},{12... | collective-permute-start | bytes 1179656 | tf_op jit(solution)/shard_map/ppermute | solution.py:149
  27.4 17.6 %collective-permute-start.2 = (bf16[256,768]{1,0:T(8,128)(2,1)S(1)}, bf16[256,768]{1,0:T(8,128)(2,1)}, u32[]{:S(2)}, u32[]{:S(2)}) collective-permute-start(bf16[256,768]{1,0:T(8,128)(2,1)S(1)} %get-tuple-element.31.b0), channel_id=1, source_target_pairs={{0,2},{2,4},{4,6},{6,0},{1,3},{3,5},{5,7},{7,1},{8,10},{10,12},{12... | collective-permute-start | bytes 1179656 | tf_op jit(solution)/shard_map/ppermute | solution.py:149
  29.9 15.1 %collective-permute-start.3 = (bf16[256,768]{1,0:T(8,128)(2,1)S(1)}, bf16[256,768]{1,0:T(8,128)(2,1)}, u32[]{:S(2)}, u32[]{:S(2)}) collective-permute-start(bf16[256,768]{1,0:T(8,128)(2,1)S(1)} %get-tuple-element.31.b0), channel_id=1, source_target_pairs={{0,6},{2,0},{4,2},{6,4},{1,7},{3,1},{5,3},{7,5},{8,14},{10,8},{12,... | collective-permute-start | bytes 1179656 | tf_op jit(solution)/shard_map/ppermute | solution.py:149
  34.4 31.1 %all-to-all-start = ((bf16[2,128,768]{2,1,0:T(8,128)(2,1)}), bf16[2,128,768]{2,1,0:T(8,128)(2,1)}, u32[]{:S(2)}, u32[]{:S(2)}) async-start(bf16[2,128,768]{2,1,0:T(8,128)(2,1)} %get-tuple-element.37), calls=%async_computation | async-start | bytes 786432 | tf_op jit(solution)/shard_map/all_to_all | solution.py:152
  38.6 1.5 %copy-start.2 = (bf16[1152,768]{1,0:T(8,128)(2,1)S(1)}, bf16[1152,768]{1,0:T(8,128)(2,1)}, u32[]{:S(2)}) copy-start(bf16[1152,768]{1,0:T(8,128)(2,1)} %head.3) | copy-start | bytes 5308420
  45.0 26.6 %collective-permute-start.4 = (bf16[128,768]{1,0:T(8,128)(2,1)S(1)}, bf16[128,768]{1,0:T(8,128)(2,1)S(1)}, u32[]{:S(2)}, u32[]{:S(2)}) collective-permute-start(bf16[128,768]{1,0:T(8,128)(2,1)S(1)} %collective-permute-done.b0), channel_id=1, source_target_pairs={{0,4},{2,6},{4,0},{6,2},{1,5},{3,7},{5,1},{7,3},{8,12},{10,14},{12... | collective-permute-start | bytes 589832 | tf_op jit(solution)/shard_map/ppermute | solution.py:149
  49.8 29.6 %collective-permute-start.5 = (bf16[128,768]{1,0:T(8,128)(2,1)S(1)}, bf16[128,768]{1,0:T(8,128)(2,1)S(1)}, u32[]{:S(2)}, u32[]{:S(2)}) collective-permute-start(bf16[128,768]{1,0:T(8,128)(2,1)S(1)} %collective-permute-done.b0), channel_id=1, source_target_pairs={{0,2},{2,4},{4,6},{6,0},{1,3},{3,5},{5,7},{7,1},{8,10},{10,12},{12... | collective-permute-start | bytes 589832 | tf_op jit(solution)/shard_map/ppermute | solution.py:149
  52.4 27.1 %collective-permute-start.6 = (bf16[128,768]{1,0:T(8,128)(2,1)S(1)}, bf16[128,768]{1,0:T(8,128)(2,1)S(1)}, u32[]{:S(2)}, u32[]{:S(2)}) collective-permute-start(bf16[128,768]{1,0:T(8,128)(2,1)S(1)} %collective-permute-done.b0), channel_id=1, source_target_pairs={{0,6},{2,0},{4,2},{6,4},{1,7},{3,1},{5,3},{7,5},{8,14},{10,8},{12,... | collective-permute-start | bytes 589832 | tf_op jit(solution)/shard_map/ppermute | solution.py:149
  66.5 14.0 %collective-permute-start.7 = (bf16[128,768]{1,0:T(8,128)(2,1)S(1)}, bf16[128,768]{1,0:T(8,128)(2,1)S(1)}, u32[]{:S(2)}, u32[]{:S(2)}) collective-permute-start(bf16[128,768]{1,0:T(8,128)(2,1)S(1)} %dynamic-slice_bitcast_fusion.b0), channel_id=1, source_target_pairs={{0,4},{2,6},{4,0},{6,2},{1,5},{3,7},{5,1},{7,3},{8,12},{10,14},{12... | collective-permute-start | bytes 589832 | tf_op jit(solution)/shard_map/ppermute | solution.py:149
  68.4 12.1 %collective-permute-start.8 = (bf16[128,768]{1,0:T(8,128)(2,1)S(1)}, bf16[128,768]{1,0:T(8,128)(2,1)S(1)}, u32[]{:S(2)}, u32[]{:S(2)}) collective-permute-start(bf16[128,768]{1,0:T(8,128)(2,1)S(1)} %dynamic-slice_bitcast_fusion.b0), channel_id=1, source_target_pairs={{0,2},{2,4},{4,6},{6,0},{1,3},{3,5},{5,7},{7,1},{8,10},{10,12},{12... | collective-permute-start | bytes 589832 | tf_op jit(solution)/shard_map/ppermute | solution.py:149
  71.6 8.9 %collective-permute-start.9 = (bf16[128,768]{1,0:T(8,128)(2,1)S(1)}, bf16[128,768]{1,0:T(8,128)(2,1)S(1)}, u32[]{:S(2)}, u32[]{:S(2)}) collective-permute-start(bf16[128,768]{1,0:T(8,128)(2,1)S(1)} %dynamic-slice_bitcast_fusion.b0), channel_id=1, source_target_pairs={{0,6},{2,0},{4,2},{6,4},{1,7},{3,1},{5,3},{7,5},{8,14},{10,8},{12,... | collective-permute-start | bytes 589832 | tf_op jit(solution)/shard_map/ppermute | solution.py:149
  80.5 3.1 %copy-start.3 = (bf16[1152,768]{1,0:T(8,128)(2,1)S(1)}, bf16[1152,768]{1,0:T(8,128)(2,1)}, u32[]{:S(2)}) copy-start(bf16[1152,768]{1,0:T(8,128)(2,1)} %head.3) | copy-start | bytes 5308420
  81.6 4.0 %collective-permute-start.10 = (bf16[448,768]{1,0:T(8,128)(2,1)S(1)}, bf16[448,768]{1,0:T(8,128)(2,1)S(1)}, u32[]{:S(2)}, u32[]{:S(2)}) collective-permute-start(bf16[448,768]{1,0:T(8,128)(2,1)S(1)} %get-tuple-element.41), channel_id=1, source_target_pairs={{0,8},{8,0},{1,9},{9,1},{2,10},{10,2},{3,11},{11,3},{4,12},{12,4},... | collective-permute-start | bytes 2064392 | tf_op jit(solution)/shard_map/ppermute | solution.py:192
  87.3 22.5 %all-to-all-start.1 = ((bf16[16,224,128]{2,1,0:T(8,128)(2,1)}), bf16[16,224,128]{2,1,0:T(8,128)(2,1)S(1)}, u32[]{:S(2)}, u32[]{:S(2)}) async-start(bf16[16,224,128]{2,1,0:T(8,128)(2,1)} %shard_map.82), calls=%async_computation.1 | async-start | bytes 1835008 | tf_op jit(solution)/shard_map/all_to_all | solution.py:205

commit v7 on v3

--- a/solution.py
+++ b/solution.py
@@ -165,7 +165,6 @@
     whole, mine, theirs = lax.optimization_barrier((whole, mine, theirs))
     near = around(whole)
 
-    second, first = lax.optimization_barrier((second, first))
     second = lax.ppermute(second, "zh", ring(2, 1))
     feats, first = lax.optimization_barrier((language_tower_outputs, first))
     unit, inv, emb = call(

time: 131 us -> 128 us (0.977)
  starting transfers between devices: 65.2 us -> 56.9 us
  waiting for transfers between devices: 25.9 us -> 32.6 us
  blocking collectives: 22.1 us -> 20.7 us
    ppermute x1, starting transfers between devices: 12.2 us -> 1.92 us  [local(): second = lax.ppermute(second, 'zh', ring(2, 1))]
    ppermute x9, waiting for transfers between devices: 4.39 us -> 12 us  [around(): return [lax.ppermute(block, 'x', ring(nx, k)) for k in (2, 1, 3)]]
    ppermute x9, starting transfers between devices: 31.7 us -> 33.3 us  [around(): return [lax.ppermute(block, 'x', ring(nx, k)) for k in (2, 1, 3)]]
    all_to_all x1, blocking collectives: 22.1 us -> 20.7 us  [local(): term = lax.all_to_all(term, ('zl', 'zh'), 0, 0, tiled=True)]
  transfers between devices with their start and end apart: 13 -> 13, of which waited for: 6 -> 8; matrix products, arithmetic and copies ran while one was open for 3% -> 3% of each run, Pallas kernels for 3% -> 3%
where the time goes in v7:
time: 128 us; the launch traced here: 127 us
  starting transfers between devices  56.9 us (44%)
  waiting for transfers between devices  32.6 us (25%)
  blocking collectives  20.7 us (16%)
  Pallas kernels  6.85 us (5%)
  matrix products  4.35 us (3%)
  local copies, waits for them, and re-layouts  2.8 us (2%)
  between operations  2.22 us (2%)
    ppermute x9, starting transfers between devices, around(): return [lax.ppermute(block, 'x', ring(nx, k)) for k in (2, 1, 3)]  33.3 us
    all_to_all x1, blocking collectives, local(): term = lax.all_to_all(term, ('zl', 'zh'), 0, 0, tiled=True)  20.7 us
    all_to_all x1, waiting for transfers between devices, local(): term = lax.all_to_all(term, ('y', 'x'), 0, 0, tiled=True)  16.2 us
    ppermute x1, starting transfers between devices, local(): first = lax.ppermute(first, 'zh', ring(2, 1))  14.8 us
    ppermute x9, waiting for transfers between devices, around(): return [lax.ppermute(block, 'x', ring(nx, k)) for k in (2, 1, 3)]  12 us
    all_to_all x1, starting transfers between devices, local(): term = lax.all_to_all(term, ('y', 'x'), 0, 0, tiled=True)  4.9 us
    ppermute x1, waiting for transfers between devices, local(): second = lax.ppermute(second, 'zh', ring(2, 1))  3.84 us
    dot_general x2, matrix products, columns_of(): lax.dot_general(pick, language_tower_outputs, NT, preferred_element_type=...  2.82 us
  transfers between devices with their start and end apart: 13, of which 8 were waited for; matrix products, arithmetic and copies ran while one was open for 3% of the time, Pallas kernels for 3%

profile of v7, /device:TPU:32, one launch (start us, length us, event | category | flops | bytes accessed | tf_op | source)
XLA Modules:
  0.0 127.3 jit_solution(9009135575936971671)
XLA Ops:
  0.6 1.5 %copy-done = bf16[1152,768]{1,0:T(8,128)(2,1)S(1)} copy-done((bf16[1152,768]{1,0:T(8,128)(2,1)S(1)}, bf16[1152,768]{1,0:T(8,128)(2,1)}, u32[]{:S(2)}) %copy-start) | copy-done | bytes 1769496
  2.1 1.1 copy-done.1
  3.2 0.8 shard_map.77
  3.9 14.8 %collective-permute-start = (bf16[128,768]{1,0:T(8,128)(2,1)S(1)}, bf16[128,768]{1,0:T(8,128)(2,1)S(1)}, u32[]{:S(2)}, u32[]{:S(2)}) collective-permute-start(bf16[128,768]{1,0:T(8,128)(2,1)S(1)} %get-tuple-element.24), channel_id=1, source_target_pairs={{0,1},{1,0},{2,3},{3,2},{4,5},{5,4},{6,7},{7,6},{8,9},{9,8},{10,11... | collective-permute-start | bytes 589832 | tf_op jit(solution)/shard_map/ppermute | solution.py:150
  18.8 1.4 %fusion.18.theirs = bf16[576,256]{1,0:T(8,128)(2,1)S(1)} fusion(bf16[256,1152]{1,0:T(8,128)(2,1)S(1)} %copy-done.3, s32[]{:T(128)S(6)} %mul.17, s32[576]{0:T(1024)S(1)} %get-tuple-element.49, s32[576]{0:T(1024)S(1)} %get-tuple-element.50, s32[576]{0:T(1024)S(1)} %get-tuple-element.48, s32[576]{0:T(1024)S(1)} %get-tuple-element.51, ...), kind=kOutput, calls=%fused_computation.23 | convolution fusion | flops 343867392 | bytes 895108 | tf_op jit(solution)/shard_map/dot_general | solution.py:159
  20.3 1.4 %fusion.19.mine = bf16[576,256]{1,0:T(8,128)(2,1)S(1)} fusion(bf16[256,1152]{1,0:T(8,128)(2,1)S(1)} %copy-done.3, s32[]{:T(128)S(6)} %mul.16, s32[576]{0:T(1024)S(1)} %get-tuple-element.49, s32[576]{0:T(1024)S(1)} %get-tuple-element.50, s32[576]{0:T(1024)S(1)} %get-tuple-element.48, s32[576]{0:T(1024)S(1)} %get-tuple-element.51, ...), kind=kOutput, calls=%fused_computation.24 | convolution fusion | flops 343867392 | bytes 895108 | tf_op jit(solution)/shard_map/dot_general | solution.py:159
  21.7 4.9 %collective-permute-start.1 = (bf16[256,768]{1,0:T(8,128)(2,1)S(1)}, bf16[256,768]{1,0:T(8,128)(2,1)S(1)}, u32[]{:S(2)}, u32[]{:S(2)}) collective-permute-start(bf16[256,768]{1,0:T(8,128)(2,1)S(1)} %get-tuple-element.31.b0), channel_id=1, source_target_pairs={{0,4},{2,6},{4,0},{6,2},{1,5},{3,7},{5,1},{7,3},{8,12},{10,14},{12... | collective-permute-start | bytes 1179656 | tf_op jit(solution)/shard_map/ppermute | solution.py:148
  26.6 2.5 %collective-permute-start.2 = (bf16[256,768]{1,0:T(8,128)(2,1)S(1)}, bf16[256,768]{1,0:T(8,128)(2,1)S(1)}, u32[]{:S(2)}, u32[]{:S(2)}) collective-permute-start(bf16[256,768]{1,0:T(8,128)(2,1)S(1)} %get-tuple-element.31.b0), channel_id=1, source_target_pairs={{0,2},{2,4},{4,6},{6,0},{1,3},{3,5},{5,7},{7,1},{8,10},{10,12},{12... | collective-permute-start | bytes 1179656 | tf_op jit(solution)/shard_map/ppermute | solution.py:148
  29.1 4.5 %collective-permute-start.3 = (bf16[256,768]{1,0:T(8,128)(2,1)S(1)}, bf16[256,768]{1,0:T(8,128)(2,1)S(1)}, u32[]{:S(2)}, u32[]{:S(2)}) collective-permute-start(bf16[256,768]{1,0:T(8,128)(2,1)S(1)} %get-tuple-element.31.b0), channel_id=1, source_target_pairs={{0,6},{2,0},{4,2},{6,4},{1,7},{3,1},{5,3},{7,5},{8,14},{10,8},{12,... | collective-permute-start | bytes 1179656 | tf_op jit(solution)/shard_map/ppermute | solution.py:148
  33.7 1.9 %collective-permute-start.7 = (bf16[128,768]{1,0:T(8,128)(2,1)S(1)}, bf16[128,768]{1,0:T(8,128)(2,1)S(1)}, u32[]{:S(2)}, u32[]{:S(2)}) collective-permute-start(bf16[128,768]{1,0:T(8,128)(2,1)S(1)} %get-tuple-element.37), channel_id=1, source_target_pairs={{0,1},{1,0},{2,3},{3,2},{4,5},{5,4},{6,7},{7,6},{8,9},{9,8},{10,11... | collective-permute-start | bytes 589832 | tf_op jit(solution)/shard_map/ppermute | solution.py:168
  35.6 0.8 shard_map.78
  36.4 0.7 collective-permute-done.1.b1
  37.2 6.9 %collective-permute-done.2.b2 = bf16[256,768]{1,0:T(8,128)(2,1)S(1)} collective-permute-done((bf16[256,768]{1,0:T(8,128)(2,1)S(1)}, bf16[256,768]{1,0:T(8,128)(2,1)S(1)}, u32[]{:S(2)}, u32[]{:S(2)}) %collective-permute-start.2) | collective-permute-done | bytes 393248 | tf_op jit(solution)/shard_map/ppermute | solution.py:148
  44.2 4.8 %collective-permute-start.4 = (bf16[128,768]{1,0:T(8,128)(2,1)S(1)}, bf16[128,768]{1,0:T(8,128)(2,1)S(1)}, u32[]{:S(2)}, u32[]{:S(2)}) collective-permute-start(bf16[128,768]{1,0:T(8,128)(2,1)S(1)} %collective-permute-done.b0), channel_id=1, source_target_pairs={{0,4},{2,6},{4,0},{6,2},{1,5},{3,7},{5,1},{7,3},{8,12},{10,14},{12... | collective-permute-start | bytes 589832 | tf_op jit(solution)/shard_map/ppermute | solution.py:148
  49.0 2.8 %collective-permute-start.5 = (bf16[128,768]{1,0:T(8,128)(2,1)S(1)}, bf16[128,768]{1,0:T(8,128)(2,1)S(1)}, u32[]{:S(2)}, u32[]{:S(2)}) collective-permute-start(bf16[128,768]{1,0:T(8,128)(2,1)S(1)} %collective-permute-done.b0), channel_id=1, source_target_pairs={{0,2},{2,4},{4,6},{6,0},{1,3},{3,5},{5,7},{7,1},{8,10},{10,12},{12... | collective-permute-start | bytes 589832 | tf_op jit(solution)/shard_map/ppermute | solution.py:148
  51.8 4.3 %collective-permute-start.6 = (bf16[128,768]{1,0:T(8,128)(2,1)S(1)}, bf16[128,768]{1,0:T(8,128)(2,1)S(1)}, u32[]{:S(2)}, u32[]{:S(2)}) collective-permute-start(bf16[128,768]{1,0:T(8,128)(2,1)S(1)} %collective-permute-done.b0), channel_id=1, source_target_pairs={{0,6},{2,0},{4,2},{6,4},{1,7},{3,1},{5,3},{7,5},{8,14},{10,8},{12,... | collective-permute-start | bytes 589832 | tf_op jit(solution)/shard_map/ppermute | solution.py:148
  56.1 3.8 %collective-permute-done.7.b0 = bf16[128,768]{1,0:T(8,128)(2,1)S(1)} collective-permute-done((bf16[128,768]{1,0:T(8,128)(2,1)S(1)}, bf16[128,768]{1,0:T(8,128)(2,1)S(1)}, u32[]{:S(2)}, u32[]{:S(2)}) %collective-permute-start.7) | collective-permute-done | bytes 196640 | tf_op jit(solution)/shard_map/ppermute | solution.py:168
  59.9 4.5 %collective-permute-start.10 = (bf16[128,768]{1,0:T(8,128)(2,1)S(1)}, bf16[128,768]{1,0:T(8,128)(2,1)S(1)}, u32[]{:S(2)}, u32[]{:S(2)}) collective-permute-start(bf16[128,768]{1,0:T(8,128)(2,1)S(1)} %collective-permute-done.7.b0), channel_id=1, source_target_pairs={{0,6},{2,0},{4,2},{6,4},{1,7},{3,1},{5,3},{7,5},{8,14},{10,8},{12,... | collective-permute-start | bytes 589832 | tf_op jit(solution)/shard_map/ppermute | solution.py:148
  64.5 2.2 %collective-permute-start.8 = (bf16[128,768]{1,0:T(8,128)(2,1)S(1)}, bf16[128,768]{1,0:T(8,128)(2,1)S(1)}, u32[]{:S(2)}, u32[]{:S(2)}) collective-permute-start(bf16[128,768]{1,0:T(8,128)(2,1)S(1)} %collective-permute-done.7.b0), channel_id=1, source_target_pairs={{0,4},{2,6},{4,0},{6,2},{1,5},{3,7},{5,1},{7,3},{8,12},{10,14},{12... | collective-permute-start | bytes 589832 | tf_op jit(solution)/shard_map/ppermute | solution.py:148
  66.7 2.7 %collective-permute-start.9 = (bf16[128,768]{1,0:T(8,128)(2,1)S(1)}, bf16[128,768]{1,0:T(8,128)(2,1)S(1)}, u32[]{:S(2)}, u32[]{:S(2)}) collective-permute-start(bf16[128,768]{1,0:T(8,128)(2,1)S(1)} %collective-permute-done.7.b0), channel_id=1, source_target_pairs={{0,2},{2,4},{4,6},{6,0},{1,3},{3,5},{5,7},{7,1},{8,10},{10,12},{12... | collective-permute-start | bytes 589832 | tf_op jit(solution)/shard_map/ppermute | solution.py:148
  70.7 1.6 %shard_map.79.total = f32[256,768]{1,0:T(8,128)S(1)} custom-call(f32[1]{0:T(128)S(6)} %copy.11.sharp, f32[1]{0:T(128)S(6)} %copy.12.offset, bf16[256,768]{1,0:T(8,128)(2,1)S(1)} %get-tuple-element.32.emb, bf16[256,768]{1,0:T(8,128)(2,1)S(1)} %get-tuple-element.31.b0, bf16[256,768]{1,0:T(8,128)(2,1)S(1)} %collective-permute-done.1.b1, ...), custom_call_target="tpu_custom_call" | custom-call | flops 805306368 | bytes 4000000 | tf_op jit(solution)/shard_map/pallas_call | solution.py:177
  72.3 1.0 shard_map.80.total
  73.3 2.2 %collective-permute-done.8.b1 = bf16[128,768]{1,0:T(8,128)(2,1)S(1)} collective-permute-done((bf16[128,768]{1,0:T(8,128)(2,1)S(1)}, bf16[128,768]{1,0:T(8,128)(2,1)S(1)}, u32[]{:S(2)}, u32[]{:S(2)}) %collective-permute-start.8) | collective-permute-done | bytes 196640 | tf_op jit(solution)/shard_map/ppermute | solution.py:148
  75.5 2.1 %collective-permute-done.9.b2 = bf16[128,768]{1,0:T(8,128)(2,1)S(1)} collective-permute-done((bf16[128,768]{1,0:T(8,128)(2,1)S(1)}, bf16[128,768]{1,0:T(8,128)(2,1)S(1)}, u32[]{:S(2)}, u32[]{:S(2)}) %collective-permute-start.9) | collective-permute-done | bytes 196640 | tf_op jit(solution)/shard_map/ppermute | solution.py:148
  77.6 1.1 shard_map.81
  78.7 1.9 %collective-permute-start.11 = (bf16[448,768]{1,0:T(8,128)(2,1)S(1)}, bf16[448,768]{1,0:T(8,128)(2,1)S(1)}, u32[]{:S(2)}, u32[]{:S(2)}) collective-permute-start(bf16[448,768]{1,0:T(8,128)(2,1)S(1)} %get-tuple-element.41), channel_id=1, source_target_pairs={{0,8},{8,0},{1,9},{9,1},{2,10},{10,2},{3,11},{11,3},{4,12},{12,4},... | collective-permute-start | bytes 2064392 | tf_op jit(solution)/shard_map/ppermute | solution.py:190
  80.6 1.5 %convolution_convert_fusion = bf16[256,1152]{1,0:T(8,128)(2,1)} fusion(bf16[256,768]{1,0:T(8,128)(2,1)S(1)} %get-tuple-element.42.raw, bf16[1152,768]{1,0:T(8,128)(2,1)S(1)} %copy-done.2), kind=kOutput, calls=%fused_computation.5 | convolution fusion | flops 453279744 | bytes 2752512 | tf_op jit(solution)/shard_map/dot_general | solution.py:191
  82.7 1.6 %shard_map.82 = bf16[16,224,128]{2,1,0:T(8,128)(2,1)} custom-call(bf16[576,256]{1,0:T(8,128)(2,1)S(1)} %fusion.19.mine, bf16[256,768]{1,0:T(8,128)(2,1)S(1)} %get-tuple-element.42.raw, bf16[448,768]{1,0:T(8,128)(2,1)S(1)} %collective-permute-done.11.other), custom_call_target="tpu_custom_call" | custom-call | flops 452984832 | bytes 4000000 | tf_op jit(solution)/shard_map/pallas_call | solution.py:196
  84.4 4.9 %all-to-all-start = ((bf16[16,224,128]{2,1,0:T(8,128)(2,1)}), bf16[16,224,128]{2,1,0:T(8,128)(2,1)S(1)}, u32[]{:S(2)}, u32[]{:S(2)}) async-start(bf16[16,224,128]{2,1,0:T(8,128)(2,1)} %shard_map.82), calls=%async_computation | async-start | bytes 1835008 | tf_op jit(solution)/shard_map/all_to_all | solution.py:203
  89.3 16.2 %all-to-all-done = bf16[16,224,128]{2,1,0:T(8,128)(2,1)S(1)} async-done(((bf16[16,224,128]{2,1,0:T(8,128)(2,1)}), bf16[16,224,128]{2,1,0:T(8,128)(2,1)S(1)}, u32[]{:S(2)}, u32[]{:S(2)}) %all-to-all-start) | async-done | bytes 917536 | tf_op jit(solution)/shard_map/all_to_all | solution.py:203
  106.0 20.7 %all_to_all.10 = bf16[16,18,96]{2,1,0:T(8,128)(2,1)S(1)} all-to-all(bf16[16,18,96]{2,1,0:T(8,128)(2,1)S(1)} %copy.10), channel_id=1, replica_groups=mesh['y'=4,'zl'=8,'c'=2,'x'=4,'zh'=2] {'zl','zh'}, dimensions={0} | all-to-all | bytes 110592 | tf_op jit(solution)/shard_map/all_to_all | solution.py:213
  126.7 0.6 broadcast_multiply_fusion
  (24 shorter events, 1.2 us)
Async XLA Ops:
  0.6 1.5 %copy-start = (bf16[1152,768]{1,0:T(8,128)(2,1)S(1)}, bf16[1152,768]{1,0:T(8,128)(2,1)}, u32[]{:S(2)}) copy-start(bf16[1152,768]{1,0:T(8,128)(2,1)} %head.2) | copy-start | bytes 5308420
  2.1 1.1 copy-start.1
  3.2 15.7 %copy-start.3 = (bf16[256,1152]{1,0:T(8,128)(2,1)S(1)}, bf16[256,1152]{1,0:T(8,128)(2,1)}, u32[]{:S(2)}) copy-start(bf16[256,1152]{1,0:T(8,128)(2,1)} %feats.2) | copy-start | bytes 1769476
  3.9 31.7 %collective-permute-start = (bf16[128,768]{1,0:T(8,128)(2,1)S(1)}, bf16[128,768]{1,0:T(8,128)(2,1)S(1)}, u32[]{:S(2)}, u32[]{:S(2)}) collective-permute-start(bf16[128,768]{1,0:T(8,128)(2,1)S(1)} %get-tuple-element.24), channel_id=1, source_target_pairs={{0,1},{1,0},{2,3},{3,2},{4,5},{5,4},{6,7},{7,6},{8,9},{9,8},{10,11... | collective-permute-start | bytes 589832 | tf_op jit(solution)/shard_map/ppermute | solution.py:150
  20.3 15.4 %copy-start.2 = (bf16[1152,768]{1,0:T(8,128)(2,1)S(1)}, bf16[1152,768]{1,0:T(8,128)(2,1)}, u32[]{:S(2)}) copy-start(bf16[1152,768]{1,0:T(8,128)(2,1)} %head.3) | copy-start | bytes 5308420
  21.7 15.5 %collective-permute-start.1 = (bf16[256,768]{1,0:T(8,128)(2,1)S(1)}, bf16[256,768]{1,0:T(8,128)(2,1)S(1)}, u32[]{:S(2)}, u32[]{:S(2)}) collective-permute-start(bf16[256,768]{1,0:T(8,128)(2,1)S(1)} %get-tuple-element.31.b0), channel_id=1, source_target_pairs={{0,4},{2,6},{4,0},{6,2},{1,5},{3,7},{5,1},{7,3},{8,12},{10,14},{12... | collective-permute-start | bytes 1179656 | tf_op jit(solution)/shard_map/ppermute | solution.py:148
  26.6 17.5 %collective-permute-start.2 = (bf16[256,768]{1,0:T(8,128)(2,1)S(1)}, bf16[256,768]{1,0:T(8,128)(2,1)S(1)}, u32[]{:S(2)}, u32[]{:S(2)}) collective-permute-start(bf16[256,768]{1,0:T(8,128)(2,1)S(1)} %get-tuple-element.31.b0), channel_id=1, source_target_pairs={{0,2},{2,4},{4,6},{6,0},{1,3},{3,5},{5,7},{7,1},{8,10},{10,12},{12... | collective-permute-start | bytes 1179656 | tf_op jit(solution)/shard_map/ppermute | solution.py:148
  29.1 15.0 %collective-permute-start.3 = (bf16[256,768]{1,0:T(8,128)(2,1)S(1)}, bf16[256,768]{1,0:T(8,128)(2,1)S(1)}, u32[]{:S(2)}, u32[]{:S(2)}) collective-permute-start(bf16[256,768]{1,0:T(8,128)(2,1)S(1)} %get-tuple-element.31.b0), channel_id=1, source_target_pairs={{0,6},{2,0},{4,2},{6,4},{1,7},{3,1},{5,3},{7,5},{8,14},{10,8},{12,... | collective-permute-start | bytes 1179656 | tf_op jit(solution)/shard_map/ppermute | solution.py:148
  33.7 26.2 %collective-permute-start.7 = (bf16[128,768]{1,0:T(8,128)(2,1)S(1)}, bf16[128,768]{1,0:T(8,128)(2,1)S(1)}, u32[]{:S(2)}, u32[]{:S(2)}) collective-permute-start(bf16[128,768]{1,0:T(8,128)(2,1)S(1)} %get-tuple-element.37), channel_id=1, source_target_pairs={{0,1},{1,0},{2,3},{3,2},{4,5},{5,4},{6,7},{7,6},{8,9},{9,8},{10,11... | collective-permute-start | bytes 589832 | tf_op jit(solution)/shard_map/ppermute | solution.py:168
  44.2 22.5 %collective-permute-start.4 = (bf16[128,768]{1,0:T(8,128)(2,1)S(1)}, bf16[128,768]{1,0:T(8,128)(2,1)S(1)}, u32[]{:S(2)}, u32[]{:S(2)}) collective-permute-start(bf16[128,768]{1,0:T(8,128)(2,1)S(1)} %collective-permute-done.b0), channel_id=1, source_target_pairs={{0,4},{2,6},{4,0},{6,2},{1,5},{3,7},{5,1},{7,3},{8,12},{10,14},{12... | collective-permute-start | bytes 589832 | tf_op jit(solution)/shard_map/ppermute | solution.py:148
  49.0 23.3 %collective-permute-start.5 = (bf16[128,768]{1,0:T(8,128)(2,1)S(1)}, bf16[128,768]{1,0:T(8,128)(2,1)S(1)}, u32[]{:S(2)}, u32[]{:S(2)}) collective-permute-start(bf16[128,768]{1,0:T(8,128)(2,1)S(1)} %collective-permute-done.b0), channel_id=1, source_target_pairs={{0,2},{2,4},{4,6},{6,0},{1,3},{3,5},{5,7},{7,1},{8,10},{10,12},{12... | collective-permute-start | bytes 589832 | tf_op jit(solution)/shard_map/ppermute | solution.py:148
  51.8 20.5 %collective-permute-start.6 = (bf16[128,768]{1,0:T(8,128)(2,1)S(1)}, bf16[128,768]{1,0:T(8,128)(2,1)S(1)}, u32[]{:S(2)}, u32[]{:S(2)}) collective-permute-start(bf16[128,768]{1,0:T(8,128)(2,1)S(1)} %collective-permute-done.b0), channel_id=1, source_target_pairs={{0,6},{2,0},{4,2},{6,4},{1,7},{3,1},{5,3},{7,5},{8,14},{10,8},{12,... | collective-permute-start | bytes 589832 | tf_op jit(solution)/shard_map/ppermute | solution.py:148
  59.9 13.4 %collective-permute-start.10 = (bf16[128,768]{1,0:T(8,128)(2,1)S(1)}, bf16[128,768]{1,0:T(8,128)(2,1)S(1)}, u32[]{:S(2)}, u32[]{:S(2)}) collective-permute-start(bf16[128,768]{1,0:T(8,128)(2,1)S(1)} %collective-permute-done.7.b0), channel_id=1, source_target_pairs={{0,6},{2,0},{4,2},{6,4},{1,7},{3,1},{5,3},{7,5},{8,14},{10,8},{12,... | collective-permute-start | bytes 589832 | tf_op jit(solution)/shard_map/ppermute | solution.py:148
  64.5 11.0 %collective-permute-start.8 = (bf16[128,768]{1,0:T(8,128)(2,1)S(1)}, bf16[128,768]{1,0:T(8,128)(2,1)S(1)}, u32[]{:S(2)}, u32[]{:S(2)}) collective-permute-start(bf16[128,768]{1,0:T(8,128)(2,1)S(1)} %collective-permute-done.7.b0), channel_id=1, source_target_pairs={{0,4},{2,6},{4,0},{6,2},{1,5},{3,7},{5,1},{7,3},{8,12},{10,14},{12... | collective-permute-start | bytes 589832 | tf_op jit(solution)/shard_map/ppermute | solution.py:148
  66.7 10.9 %collective-permute-start.9 = (bf16[128,768]{1,0:T(8,128)(2,1)S(1)}, bf16[128,768]{1,0:T(8,128)(2,1)S(1)}, u32[]{:S(2)}, u32[]{:S(2)}) collective-permute-start(bf16[128,768]{1,0:T(8,128)(2,1)S(1)} %collective-permute-done.7.b0), channel_id=1, source_target_pairs={{0,2},{2,4},{4,6},{6,0},{1,3},{3,5},{5,7},{7,1},{8,10},{10,12},{12... | collective-permute-start | bytes 589832 | tf_op jit(solution)/shard_map/ppermute | solution.py:148
  78.7 4.0 %collective-permute-start.11 = (bf16[448,768]{1,0:T(8,128)(2,1)S(1)}, bf16[448,768]{1,0:T(8,128)(2,1)S(1)}, u32[]{:S(2)}, u32[]{:S(2)}) collective-permute-start(bf16[448,768]{1,0:T(8,128)(2,1)S(1)} %get-tuple-element.41), channel_id=1, source_target_pairs={{0,8},{8,0},{1,9},{9,1},{2,10},{10,2},{3,11},{11,3},{4,12},{12,4},... | collective-permute-start | bytes 2064392 | tf_op jit(solution)/shard_map/ppermute | solution.py:190
  84.4 21.1 %all-to-all-start = ((bf16[16,224,128]{2,1,0:T(8,128)(2,1)}), bf16[16,224,128]{2,1,0:T(8,128)(2,1)S(1)}, u32[]{:S(2)}, u32[]{:S(2)}) async-start(bf16[16,224,128]{2,1,0:T(8,128)(2,1)} %shard_map.82), calls=%async_computation | async-start | bytes 1835008 | tf_op jit(solution)/shard_map/all_to_all | solution.py:203

commit v8 on v7

--- a/solution.py
+++ b/solution.py
@@ -19,14 +19,14 @@
     return [(i, (i + step) % n) for i in range(n)]
 
 
-def call(kernel, outs, specs, flops, scratch=()):
+def call(kernel, outs, specs, flops, scratch=(), room=40):
     return pl.pallas_call(
         kernel,
         out_shape=outs,
         in_specs=specs,
         out_specs=jax.tree.map(lambda _: VMEM, outs),
         scratch_shapes=scratch,
-        compiler_params=pltpu.CompilerParams(vmem_limit_bytes=40 * 1024 * 1024),
+        compiler_params=pltpu.CompilerParams(vmem_limit_bytes=room * 1024 * 1024),
         cost_estimate=pl.CostEstimate(flops=flops, bytes_accessed=4_000_000, transcendentals=0),
     )
 
@@ -37,9 +37,30 @@
     return (raw * inverse, inverse)
 
 
-def video_kernel(feats, head, whole, first, second):
-    unit, unused_inv = embed(feats[...], head[...])
-    emb = unit.astype(BF16)
+def video_kernel(feats, head, whole, first, second, feats_in, head_in, landed):
+    pieces, depth = 6, feats.shape[1] // 3
+    step = feats.shape[1] // pieces
+    moves = []
+    for k in range(pieces):
+        rows = pl.ds(step * k, step)
+        moves.append(pltpu.make_async_copy(head.at[rows], head_in.at[rows], landed.at[k]))
+        if k % 2 == 0:
+            lanes = pl.ds(depth * (k // 2), depth)
+            moves.append(
+                pltpu.make_async_copy(
+                    feats.at[:, lanes], feats_in.at[:, lanes], landed.at[pieces + k // 2]
+                )
+            )
+    for move in moves:
+        move.start()
+    raw = jnp.zeros(whole.shape, F32)
+    for k in range(3):
+        for move in moves[3 * k : 3 * k + 3]:
+            move.wait()
+        span = slice(depth * k, depth * k + depth)
+        raw += jnp.dot(feats_in[:, span], head_in[span], preferred_element_type=F32)
+    inverse = lax.rsqrt(jnp.sum(raw * raw, axis=-1, keepdims=True) + EPSILON)
+    emb = (raw * inverse).astype(BF16)
     cut = first.shape[0]
     whole[...] = emb
     first[...] = emb[:cut]
@@ -140,12 +161,18 @@
     whole, first, second = call(
         video_kernel,
         [shape(rows, width), shape(part, width), shape(part, width)],
-        [VMEM] * 2,
+        [pl.BlockSpec(memory_space=pl.ANY)] * 2,
         2 * rows * feat * width,
+        scratch=[
+            pltpu.VMEM((rows, feat), BF16),
+            pltpu.VMEM((feat, width), BF16),
+            pltpu.SemaphoreType.DMA((9,)),
+        ],
+        room=56,
     )(visual_tower_outputs, visual_mapping_frozen)
 
     def around(block):
-        return [lax.ppermute(block, "x", ring(nx, k)) for k in (2, 1, 3)]
+        return [lax.ppermute(block, "x", ring(nx, k)) for k in (1, 3, 2)]
 
     first = lax.ppermute(first, "zh", ring(2, 1))
 

time: 128 us -> 127 us (level)
  Pallas kernels: 6.85 us -> 9.4 us
  local copies, waits for them, and re-layouts: 2.8 us -> 0.27 us
  starting transfers between devices: 56.9 us -> 59.1 us
  waiting for transfers between devices: 32.6 us -> 30.9 us
    pallas_call x1, Pallas kernels: 0.76 us -> 3.31 us  [local(): call(video_kernel, [shape(rows, width), shape(part, width), shape(part, w...]
    unnamed x8, local copies, waits for them, and re-layouts: 2.54 us -> 0.02 us
    ppermute x9, waiting for transfers between devices: 12 us -> 9.78 us  [around(): return [lax.ppermute(block, 'x', ring(nx, k)) for k in (1, 3, 2)]]
    all_to_all x1, starting transfers between devices: 4.9 us -> 6.94 us  [local(): term = lax.all_to_all(term, ('y', 'x'), 0, 0, tiled=True)]
  transfers between devices with their start and end apart: 13 -> 13, of which waited for: 8 -> 5; matrix products, arithmetic and copies ran while one was open for 3% -> 3% of each run, Pallas kernels for 3% -> 3%
where the time goes in v8:
time: 127 us
  starting transfers between devices  59.1 us (47%)
  waiting for transfers between devices  30.9 us (24%)
  blocking collectives  19.6 us (15%)
  Pallas kernels  9.4 us (7%)
  matrix products  4.35 us (3%)
  between operations  2.27 us (2%)
    ppermute x9, starting transfers between devices, around(): return [lax.ppermute(block, 'x', ring(nx, k)) for k in (1, 3, 2)]  33.5 us
    all_to_all x1, blocking collectives, local(): term = lax.all_to_all(term, ('zl', 'zh'), 0, 0, tiled=True)  19.6 us
    all_to_all x1, waiting for transfers between devices, local(): term = lax.all_to_all(term, ('y', 'x'), 0, 0, tiled=True)  16.2 us
    ppermute x1, starting transfers between devices, local(): first = lax.ppermute(first, 'zh', ring(2, 1))  14.8 us
    ppermute x9, waiting for transfers between devices, around(): return [lax.ppermute(block, 'x', ring(nx, k)) for k in (1, 3, 2)]  9.78 us
    all_to_all x1, starting transfers between devices, local(): term = lax.all_to_all(term, ('y', 'x'), 0, 0, tiled=True)  6.94 us
    ppermute x1, waiting for transfers between devices, local(): second = lax.ppermute(second, 'zh', ring(2, 1))  4.29 us
    pallas_call x1, Pallas kernels, local(): call(video_kernel, [shape(rows, width), shape(part, width), shape(part, w...  3.31 us
  transfers between devices with their start and end apart: 13, of which 5 were waited for; matrix products, arithmetic and copies ran while one was open for 3% of the time, Pallas kernels for 3%

profile of v8, /device:TPU:32, one launch (start us, length us, event | category | flops | bytes accessed | tf_op | source)
XLA Modules:
  0.0 126.7 jit_solution(10818516389561749266)
XLA Ops:
  0.6 3.3 %shard_map.77 = (bf16[256,768]{1,0:T(8,128)(2,1)}, bf16[128,768]{1,0:T(8,128)(2,1)}, bf16[128,768]{1,0:T(8,128)(2,1)}) custom-call(bf16[256,1152]{1,0:T(8,128)(2,1)} %feats.1, bf16[1152,768]{1,0:T(8,128)(2,1)} %head.2), custom_call_target="tpu_custom_call" | custom-call | flops 452984832 | bytes 4000000 | tf_op jit(solution)/shard_map/pallas_call | solution.py:161
  4.0 14.8 %collective-permute-start = (bf16[128,768]{1,0:T(8,128)(2,1)}, bf16[128,768]{1,0:T(8,128)(2,1)S(1)}, u32[]{:S(2)}, u32[]{:S(2)}) collective-permute-start(bf16[128,768]{1,0:T(8,128)(2,1)} %get-tuple-element.24), channel_id=1, source_target_pairs={{0,1},{1,0},{2,3},{3,2},{4,5},{5,4},{6,7},{7,6},{8,9},{9,8},{10,11... | collective-permute-start | bytes 589832 | tf_op jit(solution)/shard_map/ppermute | solution.py:177
  18.9 1.4 %fusion.18.theirs = bf16[576,256]{1,0:T(8,128)(2,1)S(1)} fusion(bf16[256,1152]{1,0:T(8,128)(2,1)S(1)} %copy-done.1, s32[]{:T(128)S(6)} %mul.17, s32[576]{0:T(1024)S(1)} %get-tuple-element.49, s32[576]{0:T(1024)S(1)} %get-tuple-element.50, s32[576]{0:T(1024)S(1)} %get-tuple-element.48, s32[576]{0:T(1024)S(1)} %get-tuple-element.51, ...), kind=kOutput, calls=%fused_computation.23 | convolution fusion | flops 343867392 | bytes 895108 | tf_op jit(solution)/shard_map/dot_general | solution.py:186
  20.3 1.4 %fusion.19.mine = bf16[576,256]{1,0:T(8,128)(2,1)S(1)} fusion(bf16[256,1152]{1,0:T(8,128)(2,1)S(1)} %copy-done.1, s32[]{:T(128)S(6)} %mul.16, s32[576]{0:T(1024)S(1)} %get-tuple-element.49, s32[576]{0:T(1024)S(1)} %get-tuple-element.50, s32[576]{0:T(1024)S(1)} %get-tuple-element.48, s32[576]{0:T(1024)S(1)} %get-tuple-element.51, ...), kind=kOutput, calls=%fused_computation.24 | convolution fusion | flops 343867392 | bytes 895108 | tf_op jit(solution)/shard_map/dot_general | solution.py:186
  21.7 3.4 %collective-permute-start.1 = (bf16[256,768]{1,0:T(8,128)(2,1)S(1)}, bf16[256,768]{1,0:T(8,128)(2,1)S(1)}, u32[]{:S(2)}, u32[]{:S(2)}) collective-permute-start(bf16[256,768]{1,0:T(8,128)(2,1)S(1)} %copy-done.2), channel_id=1, source_target_pairs={{0,2},{2,4},{4,6},{6,0},{1,3},{3,5},{5,7},{7,1},{8,10},{10,12},{12... | collective-permute-start | bytes 1179656 | tf_op jit(solution)/shard_map/ppermute | solution.py:175
  25.1 3.7 %collective-permute-start.2 = (bf16[256,768]{1,0:T(8,128)(2,1)S(1)}, bf16[256,768]{1,0:T(8,128)(2,1)S(1)}, u32[]{:S(2)}, u32[]{:S(2)}) collective-permute-start(bf16[256,768]{1,0:T(8,128)(2,1)S(1)} %copy-done.2), channel_id=1, source_target_pairs={{0,6},{2,0},{4,2},{6,4},{1,7},{3,1},{5,3},{7,5},{8,14},{10,8},{12,... | collective-permute-start | bytes 1179656 | tf_op jit(solution)/shard_map/ppermute | solution.py:175
  28.8 3.7 %collective-permute-start.3 = (bf16[256,768]{1,0:T(8,128)(2,1)S(1)}, bf16[256,768]{1,0:T(8,128)(2,1)S(1)}, u32[]{:S(2)}, u32[]{:S(2)}) collective-permute-start(bf16[256,768]{1,0:T(8,128)(2,1)S(1)} %copy-done.2), channel_id=1, source_target_pairs={{0,4},{2,6},{4,0},{6,2},{1,5},{3,7},{5,1},{7,3},{8,12},{10,14},{12... | collective-permute-start | bytes 1179656 | tf_op jit(solution)/shard_map/ppermute | solution.py:175
  32.5 1.9 %collective-permute-start.7 = (bf16[128,768]{1,0:T(8,128)(2,1)S(1)}, bf16[128,768]{1,0:T(8,128)(2,1)S(1)}, u32[]{:S(2)}, u32[]{:S(2)}) collective-permute-start(bf16[128,768]{1,0:T(8,128)(2,1)S(1)} %copy-done.3), channel_id=1, source_target_pairs={{0,1},{1,0},{2,3},{3,2},{4,5},{5,4},{6,7},{7,6},{8,9},{9,8},{10,11... | collective-permute-start | bytes 589832 | tf_op jit(solution)/shard_map/ppermute | solution.py:195
  34.5 0.8 shard_map.78
  35.3 0.6 collective-permute-done.1.b1
  35.9 9.2 %collective-permute-done.2.b2 = bf16[256,768]{1,0:T(8,128)(2,1)S(1)} collective-permute-done((bf16[256,768]{1,0:T(8,128)(2,1)S(1)}, bf16[256,768]{1,0:T(8,128)(2,1)S(1)}, u32[]{:S(2)}, u32[]{:S(2)}) %collective-permute-start.2) | collective-permute-done | bytes 393248 | tf_op jit(solution)/shard_map/ppermute | solution.py:175
  45.0 4.7 %collective-permute-start.4 = (bf16[128,768]{1,0:T(8,128)(2,1)S(1)}, bf16[128,768]{1,0:T(8,128)(2,1)S(1)}, u32[]{:S(2)}, u32[]{:S(2)}) collective-permute-start(bf16[128,768]{1,0:T(8,128)(2,1)S(1)} %collective-permute-done.b0), channel_id=1, source_target_pairs={{0,2},{2,4},{4,6},{6,0},{1,3},{3,5},{5,7},{7,1},{8,10},{10,12},{12... | collective-permute-start | bytes 589832 | tf_op jit(solution)/shard_map/ppermute | solution.py:175
  49.8 2.8 %collective-permute-start.5 = (bf16[128,768]{1,0:T(8,128)(2,1)S(1)}, bf16[128,768]{1,0:T(8,128)(2,1)S(1)}, u32[]{:S(2)}, u32[]{:S(2)}) collective-permute-start(bf16[128,768]{1,0:T(8,128)(2,1)S(1)} %collective-permute-done.b0), channel_id=1, source_target_pairs={{0,6},{2,0},{4,2},{6,4},{1,7},{3,1},{5,3},{7,5},{8,14},{10,8},{12,... | collective-permute-start | bytes 589832 | tf_op jit(solution)/shard_map/ppermute | solution.py:175
  52.5 3.4 %collective-permute-start.6 = (bf16[128,768]{1,0:T(8,128)(2,1)S(1)}, bf16[128,768]{1,0:T(8,128)(2,1)S(1)}, u32[]{:S(2)}, u32[]{:S(2)}) collective-permute-start(bf16[128,768]{1,0:T(8,128)(2,1)S(1)} %collective-permute-done.b0), channel_id=1, source_target_pairs={{0,4},{2,6},{4,0},{6,2},{1,5},{3,7},{5,1},{7,3},{8,12},{10,14},{12... | collective-permute-start | bytes 589832 | tf_op jit(solution)/shard_map/ppermute | solution.py:175
  55.9 4.3 %collective-permute-done.7.b0 = bf16[128,768]{1,0:T(8,128)(2,1)S(1)} collective-permute-done((bf16[128,768]{1,0:T(8,128)(2,1)S(1)}, bf16[128,768]{1,0:T(8,128)(2,1)S(1)}, u32[]{:S(2)}, u32[]{:S(2)}) %collective-permute-start.7) | collective-permute-done | bytes 196640 | tf_op jit(solution)/shard_map/ppermute | solution.py:195
  60.2 4.8 %collective-permute-start.10 = (bf16[128,768]{1,0:T(8,128)(2,1)S(1)}, bf16[128,768]{1,0:T(8,128)(2,1)S(1)}, u32[]{:S(2)}, u32[]{:S(2)}) collective-permute-start(bf16[128,768]{1,0:T(8,128)(2,1)S(1)} %collective-permute-done.7.b0), channel_id=1, source_target_pairs={{0,4},{2,6},{4,0},{6,2},{1,5},{3,7},{5,1},{7,3},{8,12},{10,14},{12... | collective-permute-start | bytes 589832 | tf_op jit(solution)/shard_map/ppermute | solution.py:175
  65.0 2.1 %collective-permute-start.8 = (bf16[128,768]{1,0:T(8,128)(2,1)S(1)}, bf16[128,768]{1,0:T(8,128)(2,1)S(1)}, u32[]{:S(2)}, u32[]{:S(2)}) collective-permute-start(bf16[128,768]{1,0:T(8,128)(2,1)S(1)} %collective-permute-done.7.b0), channel_id=1, source_target_pairs={{0,2},{2,4},{4,6},{6,0},{1,3},{3,5},{5,7},{7,1},{8,10},{10,12},{12... | collective-permute-start | bytes 589832 | tf_op jit(solution)/shard_map/ppermute | solution.py:175
  67.2 4.9 %collective-permute-start.9 = (bf16[128,768]{1,0:T(8,128)(2,1)S(1)}, bf16[128,768]{1,0:T(8,128)(2,1)S(1)}, u32[]{:S(2)}, u32[]{:S(2)}) collective-permute-start(bf16[128,768]{1,0:T(8,128)(2,1)S(1)} %collective-permute-done.7.b0), channel_id=1, source_target_pairs={{0,6},{2,0},{4,2},{6,4},{1,7},{3,1},{5,3},{7,5},{8,14},{10,8},{12,... | collective-permute-start | bytes 589832 | tf_op jit(solution)/shard_map/ppermute | solution.py:175
  73.4 1.6 %shard_map.79.total = f32[256,768]{1,0:T(8,128)S(1)} custom-call(f32[1]{0:T(128)S(6)} %copy.11.sharp, f32[1]{0:T(128)S(6)} %copy.12.offset, bf16[256,768]{1,0:T(8,128)(2,1)S(1)} %get-tuple-element.32.emb, bf16[256,768]{1,0:T(8,128)(2,1)S(1)} %copy-done.2, bf16[256,768]{1,0:T(8,128)(2,1)S(1)} %collective-permute-done.1.b1, ...), custom_call_target="tpu_custom_call" | custom-call | flops 805306368 | bytes 4000000 | tf_op jit(solution)/shard_map/pallas_call | solution.py:204
  75.0 1.0 shard_map.80.total
  76.0 1.1 shard_map.81
  77.1 1.9 %collective-permute-start.11 = (bf16[448,768]{1,0:T(8,128)(2,1)S(1)}, bf16[448,768]{1,0:T(8,128)(2,1)S(1)}, u32[]{:S(2)}, u32[]{:S(2)}) collective-permute-start(bf16[448,768]{1,0:T(8,128)(2,1)S(1)} %get-tuple-element.41), channel_id=1, source_target_pairs={{0,8},{8,0},{1,9},{9,1},{2,10},{10,2},{3,11},{11,3},{4,12},{12,4},... | collective-permute-start | bytes 2064392 | tf_op jit(solution)/shard_map/ppermute | solution.py:217
  79.1 1.5 %convolution_convert_fusion = bf16[256,1152]{1,0:T(8,128)(2,1)} fusion(bf16[256,768]{1,0:T(8,128)(2,1)S(1)} %get-tuple-element.42.raw, bf16[1152,768]{1,0:T(8,128)(2,1)S(1)} %copy-done), kind=kOutput, calls=%fused_computation.5 | convolution fusion | flops 453279744 | bytes 2752512 | tf_op jit(solution)/shard_map/dot_general | solution.py:218
  80.6 0.6 collective-permute-done.11.other
  81.2 1.6 %shard_map.82 = bf16[16,224,128]{2,1,0:T(8,128)(2,1)} custom-call(bf16[576,256]{1,0:T(8,128)(2,1)S(1)} %fusion.19.mine, bf16[256,768]{1,0:T(8,128)(2,1)S(1)} %get-tuple-element.42.raw, bf16[448,768]{1,0:T(8,128)(2,1)S(1)} %collective-permute-done.11.other), custom_call_target="tpu_custom_call" | custom-call | flops 452984832 | bytes 4000000 | tf_op jit(solution)/shard_map/pallas_call | solution.py:223
  82.8 6.9 %all-to-all-start = ((bf16[16,224,128]{2,1,0:T(8,128)(2,1)}), bf16[16,224,128]{2,1,0:T(8,128)(2,1)S(1)}, u32[]{:S(2)}, u32[]{:S(2)}) async-start(bf16[16,224,128]{2,1,0:T(8,128)(2,1)} %shard_map.82), calls=%async_computation | async-start | bytes 1835008 | tf_op jit(solution)/shard_map/all_to_all | solution.py:230
  89.8 16.2 %all-to-all-done = bf16[16,224,128]{2,1,0:T(8,128)(2,1)S(1)} async-done(((bf16[16,224,128]{2,1,0:T(8,128)(2,1)}), bf16[16,224,128]{2,1,0:T(8,128)(2,1)S(1)}, u32[]{:S(2)}, u32[]{:S(2)}) %all-to-all-start) | async-done | bytes 917536 | tf_op jit(solution)/shard_map/all_to_all | solution.py:230
  106.0 0.1 convert_reduce_fusion
  106.2 0.1 fusion.20
  106.3 0.1 convert_element_type.29
  106.5 19.6 %all_to_all.10 = bf16[16,18,96]{2,1,0:T(8,128)(2,1)S(1)} all-to-all(bf16[16,18,96]{2,1,0:T(8,128)(2,1)S(1)} %copy.10), channel_id=1, replica_groups=mesh['y'=4,'zl'=8,'c'=2,'x'=4,'zh'=2] {'zl','zh'}, dimensions={0} | all-to-all | bytes 110592 | tf_op jit(solution)/shard_map/all_to_all | solution.py:240
  126.1 0.6 broadcast_multiply_fusion
  (24 shorter events, 0.3 us)
Async XLA Ops:
  0.6 18.2 %copy-start.1 = (bf16[256,1152]{1,0:T(8,128)(2,1)S(1)}, bf16[256,1152]{1,0:T(8,128)(2,1)}, u32[]{:S(2)}) copy-start(bf16[256,1152]{1,0:T(8,128)(2,1)} %feats.2) | copy-start | bytes 1769476
  4.0 30.5 %collective-permute-start = (bf16[128,768]{1,0:T(8,128)(2,1)}, bf16[128,768]{1,0:T(8,128)(2,1)S(1)}, u32[]{:S(2)}, u32[]{:S(2)}) collective-permute-start(bf16[128,768]{1,0:T(8,128)(2,1)} %get-tuple-element.24), channel_id=1, source_target_pairs={{0,1},{1,0},{2,3},{3,2},{4,5},{5,4},{6,7},{7,6},{8,9},{9,8},{10,11... | collective-permute-start | bytes 589832 | tf_op jit(solution)/shard_map/ppermute | solution.py:177
  20.3 1.5 %copy-start.2 = (bf16[256,768]{1,0:T(8,128)(2,1)S(1)}, bf16[256,768]{1,0:T(8,128)(2,1)}, u32[]{:S(2)}) copy-start(bf16[256,768]{1,0:T(8,128)(2,1)} %get-tuple-element.31.b0) | copy-start | bytes 1179652
  20.3 12.3 %copy-start.3 = (bf16[128,768]{1,0:T(8,128)(2,1)S(1)}, bf16[128,768]{1,0:T(8,128)(2,1)}, u32[]{:S(2)}) copy-start(bf16[128,768]{1,0:T(8,128)(2,1)} %get-tuple-element.37) | copy-start | bytes 589828
  20.3 14.2 %copy-start = (bf16[1152,768]{1,0:T(8,128)(2,1)S(1)}, bf16[1152,768]{1,0:T(8,128)(2,1)}, u32[]{:S(2)}) copy-start(bf16[1152,768]{1,0:T(8,128)(2,1)} %head.3) | copy-start | bytes 5308420
  21.7 14.2 %collective-permute-start.1 = (bf16[256,768]{1,0:T(8,128)(2,1)S(1)}, bf16[256,768]{1,0:T(8,128)(2,1)S(1)}, u32[]{:S(2)}, u32[]{:S(2)}) collective-permute-start(bf16[256,768]{1,0:T(8,128)(2,1)S(1)} %copy-done.2), channel_id=1, source_target_pairs={{0,2},{2,4},{4,6},{6,0},{1,3},{3,5},{5,7},{7,1},{8,10},{10,12},{12... | collective-permute-start | bytes 1179656 | tf_op jit(solution)/shard_map/ppermute | solution.py:175
  25.1 19.9 %collective-permute-start.2 = (bf16[256,768]{1,0:T(8,128)(2,1)S(1)}, bf16[256,768]{1,0:T(8,128)(2,1)S(1)}, u32[]{:S(2)}, u32[]{:S(2)}) collective-permute-start(bf16[256,768]{1,0:T(8,128)(2,1)S(1)} %copy-done.2), channel_id=1, source_target_pairs={{0,6},{2,0},{4,2},{6,4},{1,7},{3,1},{5,3},{7,5},{8,14},{10,8},{12,... | collective-permute-start | bytes 1179656 | tf_op jit(solution)/shard_map/ppermute | solution.py:175
  28.8 16.2 %collective-permute-start.3 = (bf16[256,768]{1,0:T(8,128)(2,1)S(1)}, bf16[256,768]{1,0:T(8,128)(2,1)S(1)}, u32[]{:S(2)}, u32[]{:S(2)}) collective-permute-start(bf16[256,768]{1,0:T(8,128)(2,1)S(1)} %copy-done.2), channel_id=1, source_target_pairs={{0,4},{2,6},{4,0},{6,2},{1,5},{3,7},{5,1},{7,3},{8,12},{10,14},{12... | collective-permute-start | bytes 1179656 | tf_op jit(solution)/shard_map/ppermute | solution.py:175
  32.5 27.7 %collective-permute-start.7 = (bf16[128,768]{1,0:T(8,128)(2,1)S(1)}, bf16[128,768]{1,0:T(8,128)(2,1)S(1)}, u32[]{:S(2)}, u32[]{:S(2)}) collective-permute-start(bf16[128,768]{1,0:T(8,128)(2,1)S(1)} %copy-done.3), channel_id=1, source_target_pairs={{0,1},{1,0},{2,3},{3,2},{4,5},{5,4},{6,7},{7,6},{8,9},{9,8},{10,11... | collective-permute-start | bytes 589832 | tf_op jit(solution)/shard_map/ppermute | solution.py:195
  45.0 22.1 %collective-permute-start.4 = (bf16[128,768]{1,0:T(8,128)(2,1)S(1)}, bf16[128,768]{1,0:T(8,128)(2,1)S(1)}, u32[]{:S(2)}, u32[]{:S(2)}) collective-permute-start(bf16[128,768]{1,0:T(8,128)(2,1)S(1)} %collective-permute-done.b0), channel_id=1, source_target_pairs={{0,2},{2,4},{4,6},{6,0},{1,3},{3,5},{5,7},{7,1},{8,10},{10,12},{12... | collective-permute-start | bytes 589832 | tf_op jit(solution)/shard_map/ppermute | solution.py:175
  49.8 25.2 %collective-permute-start.5 = (bf16[128,768]{1,0:T(8,128)(2,1)S(1)}, bf16[128,768]{1,0:T(8,128)(2,1)S(1)}, u32[]{:S(2)}, u32[]{:S(2)}) collective-permute-start(bf16[128,768]{1,0:T(8,128)(2,1)S(1)} %collective-permute-done.b0), channel_id=1, source_target_pairs={{0,6},{2,0},{4,2},{6,4},{1,7},{3,1},{5,3},{7,5},{8,14},{10,8},{12,... | collective-permute-start | bytes 589832 | tf_op jit(solution)/shard_map/ppermute | solution.py:175
  52.5 22.5 %collective-permute-start.6 = (bf16[128,768]{1,0:T(8,128)(2,1)S(1)}, bf16[128,768]{1,0:T(8,128)(2,1)S(1)}, u32[]{:S(2)}, u32[]{:S(2)}) collective-permute-start(bf16[128,768]{1,0:T(8,128)(2,1)S(1)} %collective-permute-done.b0), channel_id=1, source_target_pairs={{0,4},{2,6},{4,0},{6,2},{1,5},{3,7},{5,1},{7,3},{8,12},{10,14},{12... | collective-permute-start | bytes 589832 | tf_op jit(solution)/shard_map/ppermute | solution.py:175
  60.2 15.8 %collective-permute-start.10 = (bf16[128,768]{1,0:T(8,128)(2,1)S(1)}, bf16[128,768]{1,0:T(8,128)(2,1)S(1)}, u32[]{:S(2)}, u32[]{:S(2)}) collective-permute-start(bf16[128,768]{1,0:T(8,128)(2,1)S(1)} %collective-permute-done.7.b0), channel_id=1, source_target_pairs={{0,4},{2,6},{4,0},{6,2},{1,5},{3,7},{5,1},{7,3},{8,12},{10,14},{12... | collective-permute-start | bytes 589832 | tf_op jit(solution)/shard_map/ppermute | solution.py:175
  65.0 11.0 %collective-permute-start.8 = (bf16[128,768]{1,0:T(8,128)(2,1)S(1)}, bf16[128,768]{1,0:T(8,128)(2,1)S(1)}, u32[]{:S(2)}, u32[]{:S(2)}) collective-permute-start(bf16[128,768]{1,0:T(8,128)(2,1)S(1)} %collective-permute-done.7.b0), channel_id=1, source_target_pairs={{0,2},{2,4},{4,6},{6,0},{1,3},{3,5},{5,7},{7,1},{8,10},{10,12},{12... | collective-permute-start | bytes 589832 | tf_op jit(solution)/shard_map/ppermute | solution.py:175
  67.2 8.8 %collective-permute-start.9 = (bf16[128,768]{1,0:T(8,128)(2,1)S(1)}, bf16[128,768]{1,0:T(8,128)(2,1)S(1)}, u32[]{:S(2)}, u32[]{:S(2)}) collective-permute-start(bf16[128,768]{1,0:T(8,128)(2,1)S(1)} %collective-permute-done.7.b0), channel_id=1, source_target_pairs={{0,6},{2,0},{4,2},{6,4},{1,7},{3,1},{5,3},{7,5},{8,14},{10,8},{12,... | collective-permute-start | bytes 589832 | tf_op jit(solution)/shard_map/ppermute | solution.py:175
  77.1 4.0 %collective-permute-start.11 = (bf16[448,768]{1,0:T(8,128)(2,1)S(1)}, bf16[448,768]{1,0:T(8,128)(2,1)S(1)}, u32[]{:S(2)}, u32[]{:S(2)}) collective-permute-start(bf16[448,768]{1,0:T(8,128)(2,1)S(1)} %get-tuple-element.41), channel_id=1, source_target_pairs={{0,8},{8,0},{1,9},{9,1},{2,10},{10,2},{3,11},{11,3},{4,12},{12,4},... | collective-permute-start | bytes 2064392 | tf_op jit(solution)/shard_map/ppermute | solution.py:217
  82.8 23.2 %all-to-all-start = ((bf16[16,224,128]{2,1,0:T(8,128)(2,1)}), bf16[16,224,128]{2,1,0:T(8,128)(2,1)S(1)}, u32[]{:S(2)}, u32[]{:S(2)}) async-start(bf16[16,224,128]{2,1,0:T(8,128)(2,1)} %shard_map.82), calls=%async_computation | async-start | bytes 1835008 | tf_op jit(solution)/shard_map/all_to_all | solution.py:230

commit v9 on v8

--- a/solution.py
+++ b/solution.py
@@ -116,11 +116,16 @@
         packed[256:, 256 * k : 256 * k + 256] = theirs[192 * k : 192 * k + 192]
 
 
-def term_kernel(mine, raw, other, out, term):
-    term[...] = jnp.dot(mine[...], raw[...], preferred_element_type=F32)
+def own_kernel(mine, raw, out):
+    out[...] = jnp.dot(mine[...], raw[...], preferred_element_type=F32)
+
+
+def term_kernel(own, other, out, term):
     for k in range(3):
         columns = other[256:, 256 * k : 256 * k + 256]
-        term[192 * k : 192 * k + 192] += jnp.dot(columns, other[:256], preferred_element_type=F32)
+        term[192 * k : 192 * k + 192] = own[192 * k : 192 * k + 192] + jnp.dot(
+            columns, other[:256], preferred_element_type=F32
+        )
     low = lax.broadcasted_iota(jnp.int32, (72, 128), 1) < 64
     pad = jnp.zeros((8, 128), F32)
     for y in range(4):
@@ -215,19 +220,24 @@
     )(*scalars, emb, total, second, *around(second), unit, inv, theirs)
 
     other = lax.ppermute(packed, "c", ring(2, 1))
+    own = call(own_kernel, shape(half, width, kind=F32), [VMEM] * 2, 2 * half * rows * width)(
+        mine, raw_grad
+    )
+    other, own = lax.optimization_barrier((other, own))
+
+    term = call(
+        term_kernel,
+        shape(ny * nx, 224, 128),
+        [VMEM] * 2,
+        2 * half * rows * width,
+        scratch=[pltpu.VMEM((half, width), F32)],
+    )(own, other)
+    raw_grad, term = lax.optimization_barrier((raw_grad, term))
     text_grad = lax.dot_general(
         raw_grad, language_mapping_learnable, NT, preferred_element_type=F32
     ).astype(BF16)
-    other, text_grad = lax.optimization_barrier((other, text_grad))
-
-    term = call(
-        term_kernel,
-        shape(ny * nx, 224, 128),
-        [VMEM] * 3,
-        4 * half * rows * width,
-        scratch=[pltpu.VMEM((half, width), F32)],
-    )(mine, raw_grad, other)
     term = lax.all_to_all(term, ("y", "x"), 0, 0, tiled=True)
+    term, text_grad = lax.optimization_barrier((term, text_grad))
     term = jnp.sum(term.astype(F32), axis=0)
     main = term[:144]
     rest = jnp.concatenate([term[144:216, :64], term[144:216, 64:]], axis=0)

time: 127 us -> 127 us (level)
    all_to_all x1, waiting for transfers between devices: 16.2 us -> 14.7 us  [local(): term = lax.all_to_all(term, ('y', 'x'), 0, 0, tiled=True)]
where the time goes in v9:
time: 127 us; the launch traced here: 126 us
  starting transfers between devices  59.1 us (47%)
  waiting for transfers between devices  30.5 us (24%)
  blocking collectives  19.6 us (15%)
  Pallas kernels  9.57 us (8%)
  matrix products  4.35 us (3%)
  between operations  2.27 us (2%)
    ppermute x9, starting transfers between devices, around(): return [lax.ppermute(block, 'x', ring(nx, k)) for k in (1, 3, 2)]  33.5 us
    all_to_all x1, blocking collectives, local(): term = lax.all_to_all(term, ('zl', 'zh'), 0, 0, tiled=True)  19.6 us
    ppermute x1, starting transfers between devices, local(): first = lax.ppermute(first, 'zh', ring(2, 1))  14.8 us
    all_to_all x1, waiting for transfers between devices, local(): term = lax.all_to_all(term, ('y', 'x'), 0, 0, tiled=True)  14.7 us
    ppermute x9, waiting for transfers between devices, around(): return [lax.ppermute(block, 'x', ring(nx, k)) for k in (1, 3, 2)]  9.78 us
    all_to_all x1, starting transfers between devices, local(): term = lax.all_to_all(term, ('y', 'x'), 0, 0, tiled=True)  6.94 us
    ppermute x1, waiting for transfers between devices, local(): second = lax.ppermute(second, 'zh', ring(2, 1))  4.29 us
    pallas_call x1, Pallas kernels, local(): call(video_kernel, [shape(rows, width), shape(part, width), shape(part, w...  3.31 us
  transfers between devices with their start and end apart: 13, of which 5 were waited for; matrix products, arithmetic and copies ran while one was open for 3% of the time, Pallas kernels for 3%

profile of v9, /device:TPU:32, one launch (start us, length us, event | category | flops | bytes accessed | tf_op | source)
XLA Modules:
  0.0 126.4 jit_solution(16215755108784317225)
XLA Ops:
  0.6 3.3 %shard_map.77 = (bf16[256,768]{1,0:T(8,128)(2,1)}, bf16[128,768]{1,0:T(8,128)(2,1)}, bf16[128,768]{1,0:T(8,128)(2,1)}) custom-call(bf16[256,1152]{1,0:T(8,128)(2,1)} %feats.1, bf16[1152,768]{1,0:T(8,128)(2,1)} %head.2), custom_call_target="tpu_custom_call" | custom-call | flops 452984832 | bytes 4000000 | tf_op jit(solution)/shard_map/pallas_call | solution.py:166
  4.0 14.8 %collective-permute-start = (bf16[128,768]{1,0:T(8,128)(2,1)}, bf16[128,768]{1,0:T(8,128)(2,1)S(1)}, u32[]{:S(2)}, u32[]{:S(2)}) collective-permute-start(bf16[128,768]{1,0:T(8,128)(2,1)} %get-tuple-element.28), channel_id=1, source_target_pairs={{0,1},{1,0},{2,3},{3,2},{4,5},{5,4},{6,7},{7,6},{8,9},{9,8},{10,11... | collective-permute-start | bytes 589832 | tf_op jit(solution)/shard_map/ppermute | solution.py:182
  18.9 1.4 %fusion.18.theirs = bf16[576,256]{1,0:T(8,128)(2,1)S(1)} fusion(bf16[256,1152]{1,0:T(8,128)(2,1)S(1)} %copy-done.1, s32[]{:T(128)S(6)} %mul.17, s32[576]{0:T(1024)S(1)} %get-tuple-element.57, s32[576]{0:T(1024)S(1)} %get-tuple-element.58, s32[576]{0:T(1024)S(1)} %get-tuple-element.56, s32[576]{0:T(1024)S(1)} %get-tuple-element.59, ...), kind=kOutput, calls=%fused_computation.23 | convolution fusion | flops 343867392 | bytes 895108 | tf_op jit(solution)/shard_map/dot_general | solution.py:191
  20.3 1.4 %fusion.19.mine = bf16[576,256]{1,0:T(8,128)(2,1)S(1)} fusion(bf16[256,1152]{1,0:T(8,128)(2,1)S(1)} %copy-done.1, s32[]{:T(128)S(6)} %mul.16, s32[576]{0:T(1024)S(1)} %get-tuple-element.57, s32[576]{0:T(1024)S(1)} %get-tuple-element.58, s32[576]{0:T(1024)S(1)} %get-tuple-element.56, s32[576]{0:T(1024)S(1)} %get-tuple-element.59, ...), kind=kOutput, calls=%fused_computation.24 | convolution fusion | flops 343867392 | bytes 895108 | tf_op jit(solution)/shard_map/dot_general | solution.py:191
  21.7 3.4 %collective-permute-start.1 = (bf16[256,768]{1,0:T(8,128)(2,1)S(1)}, bf16[256,768]{1,0:T(8,128)(2,1)S(1)}, u32[]{:S(2)}, u32[]{:S(2)}) collective-permute-start(bf16[256,768]{1,0:T(8,128)(2,1)S(1)} %copy-done.2), channel_id=1, source_target_pairs={{0,2},{2,4},{4,6},{6,0},{1,3},{3,5},{5,7},{7,1},{8,10},{10,12},{12... | collective-permute-start | bytes 1179656 | tf_op jit(solution)/shard_map/ppermute | solution.py:180
  25.1 3.7 %collective-permute-start.2 = (bf16[256,768]{1,0:T(8,128)(2,1)S(1)}, bf16[256,768]{1,0:T(8,128)(2,1)S(1)}, u32[]{:S(2)}, u32[]{:S(2)}) collective-permute-start(bf16[256,768]{1,0:T(8,128)(2,1)S(1)} %copy-done.2), channel_id=1, source_target_pairs={{0,6},{2,0},{4,2},{6,4},{1,7},{3,1},{5,3},{7,5},{8,14},{10,8},{12,... | collective-permute-start | bytes 1179656 | tf_op jit(solution)/shard_map/ppermute | solution.py:180
  28.8 3.7 %collective-permute-start.3 = (bf16[256,768]{1,0:T(8,128)(2,1)S(1)}, bf16[256,768]{1,0:T(8,128)(2,1)S(1)}, u32[]{:S(2)}, u32[]{:S(2)}) collective-permute-start(bf16[256,768]{1,0:T(8,128)(2,1)S(1)} %copy-done.2), channel_id=1, source_target_pairs={{0,4},{2,6},{4,0},{6,2},{1,5},{3,7},{5,1},{7,3},{8,12},{10,14},{12... | collective-permute-start | bytes 1179656 | tf_op jit(solution)/shard_map/ppermute | solution.py:180
  32.5 1.9 %collective-permute-start.7 = (bf16[128,768]{1,0:T(8,128)(2,1)S(1)}, bf16[128,768]{1,0:T(8,128)(2,1)S(1)}, u32[]{:S(2)}, u32[]{:S(2)}) collective-permute-start(bf16[128,768]{1,0:T(8,128)(2,1)S(1)} %copy-done.3), channel_id=1, source_target_pairs={{0,1},{1,0},{2,3},{3,2},{4,5},{5,4},{6,7},{7,6},{8,9},{9,8},{10,11... | collective-permute-start | bytes 589832 | tf_op jit(solution)/shard_map/ppermute | solution.py:200
  34.5 0.8 shard_map.78
  35.3 0.6 collective-permute-done.1.b1
  35.9 9.2 %collective-permute-done.2.b2 = bf16[256,768]{1,0:T(8,128)(2,1)S(1)} collective-permute-done((bf16[256,768]{1,0:T(8,128)(2,1)S(1)}, bf16[256,768]{1,0:T(8,128)(2,1)S(1)}, u32[]{:S(2)}, u32[]{:S(2)}) %collective-permute-start.2) | collective-permute-done | bytes 393248 | tf_op jit(solution)/shard_map/ppermute | solution.py:180
  45.0 4.7 %collective-permute-start.4 = (bf16[128,768]{1,0:T(8,128)(2,1)S(1)}, bf16[128,768]{1,0:T(8,128)(2,1)S(1)}, u32[]{:S(2)}, u32[]{:S(2)}) collective-permute-start(bf16[128,768]{1,0:T(8,128)(2,1)S(1)} %collective-permute-done.b0), channel_id=1, source_target_pairs={{0,2},{2,4},{4,6},{6,0},{1,3},{3,5},{5,7},{7,1},{8,10},{10,12},{12... | collective-permute-start | bytes 589832 | tf_op jit(solution)/shard_map/ppermute | solution.py:180
  49.8 2.8 %collective-permute-start.5 = (bf16[128,768]{1,0:T(8,128)(2,1)S(1)}, bf16[128,768]{1,0:T(8,128)(2,1)S(1)}, u32[]{:S(2)}, u32[]{:S(2)}) collective-permute-start(bf16[128,768]{1,0:T(8,128)(2,1)S(1)} %collective-permute-done.b0), channel_id=1, source_target_pairs={{0,6},{2,0},{4,2},{6,4},{1,7},{3,1},{5,3},{7,5},{8,14},{10,8},{12,... | collective-permute-start | bytes 589832 | tf_op jit(solution)/shard_map/ppermute | solution.py:180
  52.5 3.4 %collective-permute-start.6 = (bf16[128,768]{1,0:T(8,128)(2,1)S(1)}, bf16[128,768]{1,0:T(8,128)(2,1)S(1)}, u32[]{:S(2)}, u32[]{:S(2)}) collective-permute-start(bf16[128,768]{1,0:T(8,128)(2,1)S(1)} %collective-permute-done.b0), channel_id=1, source_target_pairs={{0,4},{2,6},{4,0},{6,2},{1,5},{3,7},{5,1},{7,3},{8,12},{10,14},{12... | collective-permute-start | bytes 589832 | tf_op jit(solution)/shard_map/ppermute | solution.py:180
  55.9 4.3 %collective-permute-done.7.b0 = bf16[128,768]{1,0:T(8,128)(2,1)S(1)} collective-permute-done((bf16[128,768]{1,0:T(8,128)(2,1)S(1)}, bf16[128,768]{1,0:T(8,128)(2,1)S(1)}, u32[]{:S(2)}, u32[]{:S(2)}) %collective-permute-start.7) | collective-permute-done | bytes 196640 | tf_op jit(solution)/shard_map/ppermute | solution.py:200
  60.2 4.8 %collective-permute-start.10 = (bf16[128,768]{1,0:T(8,128)(2,1)S(1)}, bf16[128,768]{1,0:T(8,128)(2,1)S(1)}, u32[]{:S(2)}, u32[]{:S(2)}) collective-permute-start(bf16[128,768]{1,0:T(8,128)(2,1)S(1)} %collective-permute-done.7.b0), channel_id=1, source_target_pairs={{0,4},{2,6},{4,0},{6,2},{1,5},{3,7},{5,1},{7,3},{8,12},{10,14},{12... | collective-permute-start | bytes 589832 | tf_op jit(solution)/shard_map/ppermute | solution.py:180
  65.0 2.1 %collective-permute-start.8 = (bf16[128,768]{1,0:T(8,128)(2,1)S(1)}, bf16[128,768]{1,0:T(8,128)(2,1)S(1)}, u32[]{:S(2)}, u32[]{:S(2)}) collective-permute-start(bf16[128,768]{1,0:T(8,128)(2,1)S(1)} %collective-permute-done.7.b0), channel_id=1, source_target_pairs={{0,2},{2,4},{4,6},{6,0},{1,3},{3,5},{5,7},{7,1},{8,10},{10,12},{12... | collective-permute-start | bytes 589832 | tf_op jit(solution)/shard_map/ppermute | solution.py:180
  67.2 4.9 %collective-permute-start.9 = (bf16[128,768]{1,0:T(8,128)(2,1)S(1)}, bf16[128,768]{1,0:T(8,128)(2,1)S(1)}, u32[]{:S(2)}, u32[]{:S(2)}) collective-permute-start(bf16[128,768]{1,0:T(8,128)(2,1)S(1)} %collective-permute-done.7.b0), channel_id=1, source_target_pairs={{0,6},{2,0},{4,2},{6,4},{1,7},{3,1},{5,3},{7,5},{8,14},{10,8},{12,... | collective-permute-start | bytes 589832 | tf_op jit(solution)/shard_map/ppermute | solution.py:180
  73.4 1.6 %shard_map.79.total = f32[256,768]{1,0:T(8,128)S(1)} custom-call(f32[1]{0:T(128)S(6)} %copy.11.sharp, f32[1]{0:T(128)S(6)} %copy.12.offset, bf16[256,768]{1,0:T(8,128)(2,1)S(1)} %get-tuple-element.36.emb, bf16[256,768]{1,0:T(8,128)(2,1)S(1)} %copy-done.2, bf16[256,768]{1,0:T(8,128)(2,1)S(1)} %collective-permute-done.1.b1, ...), custom_call_target="tpu_custom_call" | custom-call | flops 805306368 | bytes 4000000 | tf_op jit(solution)/shard_map/pallas_call | solution.py:209
  75.0 1.0 shard_map.80.total
  76.0 1.1 shard_map.81
  77.1 1.9 %collective-permute-start.11 = (bf16[448,768]{1,0:T(8,128)(2,1)S(1)}, bf16[448,768]{1,0:T(8,128)(2,1)S(1)}, u32[]{:S(2)}, u32[]{:S(2)}) collective-permute-start(bf16[448,768]{1,0:T(8,128)(2,1)S(1)} %get-tuple-element.46), channel_id=1, source_target_pairs={{0,8},{8,0},{1,9},{9,1},{2,10},{10,2},{3,11},{11,3},{4,12},{12,4},... | collective-permute-start | bytes 2064392 | tf_op jit(solution)/shard_map/ppermute | solution.py:222
  79.1 0.4 shard_map.82.own
  79.5 1.7 %collective-permute-done.11.other = bf16[448,768]{1,0:T(8,128)(2,1)S(1)} collective-permute-done((bf16[448,768]{1,0:T(8,128)(2,1)S(1)}, bf16[448,768]{1,0:T(8,128)(2,1)S(1)}, u32[]{:S(2)}, u32[]{:S(2)}) %collective-permute-start.11) | collective-permute-done | bytes 688160 | tf_op jit(solution)/shard_map/ppermute | solution.py:222
  81.2 1.4 %shard_map.83 = bf16[16,224,128]{2,1,0:T(8,128)(2,1)} custom-call(f32[576,768]{1,0:T(8,128)S(1)} %shard_map.82.own, bf16[448,768]{1,0:T(8,128)(2,1)S(1)} %collective-permute-done.11.other), custom_call_target="tpu_custom_call" | custom-call | flops 226492416 | bytes 4000000 | tf_op jit(solution)/shard_map/pallas_call | solution.py:228
  82.6 6.9 %all-to-all-start = ((bf16[16,224,128]{2,1,0:T(8,128)(2,1)}), bf16[16,224,128]{2,1,0:T(8,128)(2,1)S(1)}, u32[]{:S(2)}, u32[]{:S(2)}) async-start(bf16[16,224,128]{2,1,0:T(8,128)(2,1)} %shard_map.83), calls=%async_computation | async-start | bytes 1835008 | tf_op jit(solution)/shard_map/all_to_all | solution.py:239
  89.5 1.5 %convolution_convert_fusion = bf16[256,1152]{1,0:T(8,128)(2,1)} fusion(bf16[256,768]{1,0:T(8,128)(2,1)S(1)} %get-tuple-element.51.raw, bf16[1152,768]{1,0:T(8,128)(2,1)S(1)} %copy-done), kind=kOutput, calls=%fused_computation.5 | convolution fusion | flops 453279744 | bytes 2752512 | tf_op jit(solution)/shard_map/dot_general | solution.py:236
  91.1 14.7 %all-to-all-done = bf16[16,224,128]{2,1,0:T(8,128)(2,1)S(1)} async-done(((bf16[16,224,128]{2,1,0:T(8,128)(2,1)}), bf16[16,224,128]{2,1,0:T(8,128)(2,1)S(1)}, u32[]{:S(2)}, u32[]{:S(2)}) %all-to-all-start) | async-done | bytes 917536 | tf_op jit(solution)/shard_map/all_to_all | solution.py:239
  105.7 0.1 convert_reduce_fusion
  105.9 0.1 fusion.20
  106.2 19.6 %all_to_all.10 = bf16[16,18,96]{2,1,0:T(8,128)(2,1)S(1)} all-to-all(bf16[16,18,96]{2,1,0:T(8,128)(2,1)S(1)} %copy.10), channel_id=1, replica_groups=mesh['y'=4,'zl'=8,'c'=2,'x'=4,'zh'=2] {'zl','zh'}, dimensions={0} | all-to-all | bytes 110592 | tf_op jit(solution)/shard_map/all_to_all | solution.py:250
  125.8 0.6 broadcast_multiply_fusion
  (25 shorter events, 0.3 us)
Async XLA Ops:
  0.6 18.2 %copy-start.1 = (bf16[256,1152]{1,0:T(8,128)(2,1)S(1)}, bf16[256,1152]{1,0:T(8,128)(2,1)}, u32[]{:S(2)}) copy-start(bf16[256,1152]{1,0:T(8,128)(2,1)} %feats.2) | copy-start | bytes 1769476
  4.0 30.5 %collective-permute-start = (bf16[128,768]{1,0:T(8,128)(2,1)}, bf16[128,768]{1,0:T(8,128)(2,1)S(1)}, u32[]{:S(2)}, u32[]{:S(2)}) collective-permute-start(bf16[128,768]{1,0:T(8,128)(2,1)} %get-tuple-element.28), channel_id=1, source_target_pairs={{0,1},{1,0},{2,3},{3,2},{4,5},{5,4},{6,7},{7,6},{8,9},{9,8},{10,11... | collective-permute-start | bytes 589832 | tf_op jit(solution)/shard_map/ppermute | solution.py:182
  20.3 1.5 %copy-start.2 = (bf16[256,768]{1,0:T(8,128)(2,1)S(1)}, bf16[256,768]{1,0:T(8,128)(2,1)}, u32[]{:S(2)}) copy-start(bf16[256,768]{1,0:T(8,128)(2,1)} %get-tuple-element.35.b0) | copy-start | bytes 1179652
  20.3 12.3 %copy-start.3 = (bf16[128,768]{1,0:T(8,128)(2,1)S(1)}, bf16[128,768]{1,0:T(8,128)(2,1)}, u32[]{:S(2)}) copy-start(bf16[128,768]{1,0:T(8,128)(2,1)} %get-tuple-element.41) | copy-start | bytes 589828
  20.3 14.2 %copy-start = (bf16[1152,768]{1,0:T(8,128)(2,1)S(1)}, bf16[1152,768]{1,0:T(8,128)(2,1)}, u32[]{:S(2)}) copy-start(bf16[1152,768]{1,0:T(8,128)(2,1)} %head.3) | copy-start | bytes 5308420
  21.7 14.2 %collective-permute-start.1 = (bf16[256,768]{1,0:T(8,128)(2,1)S(1)}, bf16[256,768]{1,0:T(8,128)(2,1)S(1)}, u32[]{:S(2)}, u32[]{:S(2)}) collective-permute-start(bf16[256,768]{1,0:T(8,128)(2,1)S(1)} %copy-done.2), channel_id=1, source_target_pairs={{0,2},{2,4},{4,6},{6,0},{1,3},{3,5},{5,7},{7,1},{8,10},{10,12},{12... | collective-permute-start | bytes 1179656 | tf_op jit(solution)/shard_map/ppermute | solution.py:180
  25.1 19.9 %collective-permute-start.2 = (bf16[256,768]{1,0:T(8,128)(2,1)S(1)}, bf16[256,768]{1,0:T(8,128)(2,1)S(1)}, u32[]{:S(2)}, u32[]{:S(2)}) collective-permute-start(bf16[256,768]{1,0:T(8,128)(2,1)S(1)} %copy-done.2), channel_id=1, source_target_pairs={{0,6},{2,0},{4,2},{6,4},{1,7},{3,1},{5,3},{7,5},{8,14},{10,8},{12,... | collective-permute-start | bytes 1179656 | tf_op jit(solution)/shard_map/ppermute | solution.py:180
  28.8 16.2 %collective-permute-start.3 = (bf16[256,768]{1,0:T(8,128)(2,1)S(1)}, bf16[256,768]{1,0:T(8,128)(2,1)S(1)}, u32[]{:S(2)}, u32[]{:S(2)}) collective-permute-start(bf16[256,768]{1,0:T(8,128)(2,1)S(1)} %copy-done.2), channel_id=1, source_target_pairs={{0,4},{2,6},{4,0},{6,2},{1,5},{3,7},{5,1},{7,3},{8,12},{10,14},{12... | collective-permute-start | bytes 1179656 | tf_op jit(solution)/shard_map/ppermute | solution.py:180
  32.5 27.7 %collective-permute-start.7 = (bf16[128,768]{1,0:T(8,128)(2,1)S(1)}, bf16[128,768]{1,0:T(8,128)(2,1)S(1)}, u32[]{:S(2)}, u32[]{:S(2)}) collective-permute-start(bf16[128,768]{1,0:T(8,128)(2,1)S(1)} %copy-done.3), channel_id=1, source_target_pairs={{0,1},{1,0},{2,3},{3,2},{4,5},{5,4},{6,7},{7,6},{8,9},{9,8},{10,11... | collective-permute-start | bytes 589832 | tf_op jit(solution)/shard_map/ppermute | solution.py:200
  45.0 22.1 %collective-permute-start.4 = (bf16[128,768]{1,0:T(8,128)(2,1)S(1)}, bf16[128,768]{1,0:T(8,128)(2,1)S(1)}, u32[]{:S(2)}, u32[]{:S(2)}) collective-permute-start(bf16[128,768]{1,0:T(8,128)(2,1)S(1)} %collective-permute-done.b0), channel_id=1, source_target_pairs={{0,2},{2,4},{4,6},{6,0},{1,3},{3,5},{5,7},{7,1},{8,10},{10,12},{12... | collective-permute-start | bytes 589832 | tf_op jit(solution)/shard_map/ppermute | solution.py:180
  49.8 25.2 %collective-permute-start.5 = (bf16[128,768]{1,0:T(8,128)(2,1)S(1)}, bf16[128,768]{1,0:T(8,128)(2,1)S(1)}, u32[]{:S(2)}, u32[]{:S(2)}) collective-permute-start(bf16[128,768]{1,0:T(8,128)(2,1)S(1)} %collective-permute-done.b0), channel_id=1, source_target_pairs={{0,6},{2,0},{4,2},{6,4},{1,7},{3,1},{5,3},{7,5},{8,14},{10,8},{12,... | collective-permute-start | bytes 589832 | tf_op jit(solution)/shard_map/ppermute | solution.py:180
  52.5 22.5 %collective-permute-start.6 = (bf16[128,768]{1,0:T(8,128)(2,1)S(1)}, bf16[128,768]{1,0:T(8,128)(2,1)S(1)}, u32[]{:S(2)}, u32[]{:S(2)}) collective-permute-start(bf16[128,768]{1,0:T(8,128)(2,1)S(1)} %collective-permute-done.b0), channel_id=1, source_target_pairs={{0,4},{2,6},{4,0},{6,2},{1,5},{3,7},{5,1},{7,3},{8,12},{10,14},{12... | collective-permute-start | bytes 589832 | tf_op jit(solution)/shard_map/ppermute | solution.py:180
  60.2 15.8 %collective-permute-start.10 = (bf16[128,768]{1,0:T(8,128)(2,1)S(1)}, bf16[128,768]{1,0:T(8,128)(2,1)S(1)}, u32[]{:S(2)}, u32[]{:S(2)}) collective-permute-start(bf16[128,768]{1,0:T(8,128)(2,1)S(1)} %collective-permute-done.7.b0), channel_id=1, source_target_pairs={{0,4},{2,6},{4,0},{6,2},{1,5},{3,7},{5,1},{7,3},{8,12},{10,14},{12... | collective-permute-start | bytes 589832 | tf_op jit(solution)/shard_map/ppermute | solution.py:180
  65.0 11.0 %collective-permute-start.8 = (bf16[128,768]{1,0:T(8,128)(2,1)S(1)}, bf16[128,768]{1,0:T(8,128)(2,1)S(1)}, u32[]{:S(2)}, u32[]{:S(2)}) collective-permute-start(bf16[128,768]{1,0:T(8,128)(2,1)S(1)} %collective-permute-done.7.b0), channel_id=1, source_target_pairs={{0,2},{2,4},{4,6},{6,0},{1,3},{3,5},{5,7},{7,1},{8,10},{10,12},{12... | collective-permute-start | bytes 589832 | tf_op jit(solution)/shard_map/ppermute | solution.py:180
  67.2 8.8 %collective-permute-start.9 = (bf16[128,768]{1,0:T(8,128)(2,1)S(1)}, bf16[128,768]{1,0:T(8,128)(2,1)S(1)}, u32[]{:S(2)}, u32[]{:S(2)}) collective-permute-start(bf16[128,768]{1,0:T(8,128)(2,1)S(1)} %collective-permute-done.7.b0), channel_id=1, source_target_pairs={{0,6},{2,0},{4,2},{6,4},{1,7},{3,1},{5,3},{7,5},{8,14},{10,8},{12,... | collective-permute-start | bytes 589832 | tf_op jit(solution)/shard_map/ppermute | solution.py:180
  77.1 4.0 %collective-permute-start.11 = (bf16[448,768]{1,0:T(8,128)(2,1)S(1)}, bf16[448,768]{1,0:T(8,128)(2,1)S(1)}, u32[]{:S(2)}, u32[]{:S(2)}) collective-permute-start(bf16[448,768]{1,0:T(8,128)(2,1)S(1)} %get-tuple-element.46), channel_id=1, source_target_pairs={{0,8},{8,0},{1,9},{9,1},{2,10},{10,2},{3,11},{11,3},{4,12},{12,4},... | collective-permute-start | bytes 2064392 | tf_op jit(solution)/shard_map/ppermute | solution.py:222
  82.6 23.2 %all-to-all-start = ((bf16[16,224,128]{2,1,0:T(8,128)(2,1)}), bf16[16,224,128]{2,1,0:T(8,128)(2,1)S(1)}, u32[]{:S(2)}, u32[]{:S(2)}) async-start(bf16[16,224,128]{2,1,0:T(8,128)(2,1)} %shard_map.83), calls=%async_computation | async-start | bytes 1835008 | tf_op jit(solution)/shard_map/all_to_all | solution.py:239

commit v10 on v8

--- a/solution.py
+++ b/solution.py
@@ -1,3 +1,5 @@
+import functools
+
 import jax
 import jax.numpy as jnp
 from jax import lax
@@ -136,6 +138,13 @@
                 out[4 * y + x, 144:224, :] = jnp.concatenate([rest, pad], axis=0).astype(BF16)
 
 
+def mean_kernel(devices, parts, out):
+    acc = parts[0].astype(F32)
+    for k in range(1, parts.shape[0]):
+        acc += parts[k].astype(F32)
+    out[...] = acc * (1.0 / devices)
+
+
 def local(
     visual_tower_outputs,
     language_tower_outputs,
@@ -238,7 +247,9 @@
     term = term.reshape(nzl, piece_r, nzh, piece_c).transpose(0, 2, 1, 3)
     term = term.reshape(nzl * nzh, piece_r, piece_c)
     term = lax.all_to_all(term, ("zl", "zh"), 0, 0, tiled=True)
-    head_grad = jnp.sum(term.astype(F32), axis=0) / F32(devices)
+    head_grad = call(
+        functools.partial(mean_kernel, devices), shape(piece_r, piece_c, kind=F32), [VMEM], 1_000_000
+    )(term)
     return (text_grad, head_grad)
 
 

time: 127 us -> 127 us (level)
  no operation moved by 1% of the time
where the time goes in v10:
time: 127 us
  starting transfers between devices  59.1 us (47%)
  waiting for transfers between devices  30.9 us (24%)
  blocking collectives  19.6 us (15%)
  Pallas kernels  10.1 us (8%)
  matrix products  4.35 us (3%)
  between operations  2.26 us (2%)
    ppermute x9, starting transfers between devices, around(): return [lax.ppermute(block, 'x', ring(nx, k)) for k in (1, 3, 2)]  33.5 us
    all_to_all x1, blocking collectives, local(): term = lax.all_to_all(term, ('zl', 'zh'), 0, 0, tiled=True)  19.6 us
    all_to_all x1, waiting for transfers between devices, local(): term = lax.all_to_all(term, ('y', 'x'), 0, 0, tiled=True)  16.2 us
    ppermute x1, starting transfers between devices, local(): first = lax.ppermute(first, 'zh', ring(2, 1))  14.8 us
    ppermute x9, waiting for transfers between devices, around(): return [lax.ppermute(block, 'x', ring(nx, k)) for k in (1, 3, 2)]  9.79 us
    all_to_all x1, starting transfers between devices, local(): term = lax.all_to_all(term, ('y', 'x'), 0, 0, tiled=True)  6.92 us
    ppermute x1, waiting for transfers between devices, local(): second = lax.ppermute(second, 'zh', ring(2, 1))  4.29 us
    pallas_call x1, Pallas kernels, local(): call(video_kernel, [shape(rows, width), shape(part, width), shape(part, w...  3.32 us
  transfers between devices with their start and end apart: 13, of which 5 were waited for; matrix products, arithmetic and copies ran while one was open for 3% of the time, Pallas kernels for 3%

profile of v10, /device:TPU:32, one launch (start us, length us, event | category | flops | bytes accessed | tf_op | source)
XLA Modules:
  0.0 126.6 jit_solution(16401526204722339085)
XLA Ops:
  0.6 3.3 %shard_map.77 = (bf16[256,768]{1,0:T(8,128)(2,1)}, bf16[128,768]{1,0:T(8,128)(2,1)}, bf16[128,768]{1,0:T(8,128)(2,1)}) custom-call(bf16[256,1152]{1,0:T(8,128)(2,1)} %feats.1, bf16[1152,768]{1,0:T(8,128)(2,1)} %head.2), custom_call_target="tpu_custom_call" | custom-call | flops 452984832 | bytes 4000000 | tf_op jit(solution)/shard_map/pallas_call | solution.py:170
  4.0 14.8 %collective-permute-start = (bf16[128,768]{1,0:T(8,128)(2,1)}, bf16[128,768]{1,0:T(8,128)(2,1)S(1)}, u32[]{:S(2)}, u32[]{:S(2)}) collective-permute-start(bf16[128,768]{1,0:T(8,128)(2,1)} %get-tuple-element.24), channel_id=1, source_target_pairs={{0,1},{1,0},{2,3},{3,2},{4,5},{5,4},{6,7},{7,6},{8,9},{9,8},{10,11... | collective-permute-start | bytes 589832 | tf_op jit(solution)/shard_map/ppermute | solution.py:186
  18.9 1.4 %fusion.18.theirs = bf16[576,256]{1,0:T(8,128)(2,1)S(1)} fusion(bf16[256,1152]{1,0:T(8,128)(2,1)S(1)} %copy-done.1, s32[]{:T(128)S(6)} %mul.17, s32[576]{0:T(1024)S(1)} %get-tuple-element.49, s32[576]{0:T(1024)S(1)} %get-tuple-element.50, s32[576]{0:T(1024)S(1)} %get-tuple-element.48, s32[576]{0:T(1024)S(1)} %get-tuple-element.51, ...), kind=kOutput, calls=%fused_computation.23 | convolution fusion | flops 343867392 | bytes 895108 | tf_op jit(solution)/shard_map/dot_general | solution.py:195
  20.3 1.4 %fusion.19.mine = bf16[576,256]{1,0:T(8,128)(2,1)S(1)} fusion(bf16[256,1152]{1,0:T(8,128)(2,1)S(1)} %copy-done.1, s32[]{:T(128)S(6)} %mul.16, s32[576]{0:T(1024)S(1)} %get-tuple-element.49, s32[576]{0:T(1024)S(1)} %get-tuple-element.50, s32[576]{0:T(1024)S(1)} %get-tuple-element.48, s32[576]{0:T(1024)S(1)} %get-tuple-element.51, ...), kind=kOutput, calls=%fused_computation.24 | convolution fusion | flops 343867392 | bytes 895108 | tf_op jit(solution)/shard_map/dot_general | solution.py:195
  21.7 3.4 %collective-permute-start.1 = (bf16[256,768]{1,0:T(8,128)(2,1)S(1)}, bf16[256,768]{1,0:T(8,128)(2,1)S(1)}, u32[]{:S(2)}, u32[]{:S(2)}) collective-permute-start(bf16[256,768]{1,0:T(8,128)(2,1)S(1)} %copy-done.2), channel_id=1, source_target_pairs={{0,2},{2,4},{4,6},{6,0},{1,3},{3,5},{5,7},{7,1},{8,10},{10,12},{12... | collective-permute-start | bytes 1179656 | tf_op jit(solution)/shard_map/ppermute | solution.py:184
  25.1 3.7 %collective-permute-start.2 = (bf16[256,768]{1,0:T(8,128)(2,1)S(1)}, bf16[256,768]{1,0:T(8,128)(2,1)S(1)}, u32[]{:S(2)}, u32[]{:S(2)}) collective-permute-start(bf16[256,768]{1,0:T(8,128)(2,1)S(1)} %copy-done.2), channel_id=1, source_target_pairs={{0,6},{2,0},{4,2},{6,4},{1,7},{3,1},{5,3},{7,5},{8,14},{10,8},{12,... | collective-permute-start | bytes 1179656 | tf_op jit(solution)/shard_map/ppermute | solution.py:184
  28.8 3.7 %collective-permute-start.3 = (bf16[256,768]{1,0:T(8,128)(2,1)S(1)}, bf16[256,768]{1,0:T(8,128)(2,1)S(1)}, u32[]{:S(2)}, u32[]{:S(2)}) collective-permute-start(bf16[256,768]{1,0:T(8,128)(2,1)S(1)} %copy-done.2), channel_id=1, source_target_pairs={{0,4},{2,6},{4,0},{6,2},{1,5},{3,7},{5,1},{7,3},{8,12},{10,14},{12... | collective-permute-start | bytes 1179656 | tf_op jit(solution)/shard_map/ppermute | solution.py:184
  32.5 1.9 %collective-permute-start.7 = (bf16[128,768]{1,0:T(8,128)(2,1)S(1)}, bf16[128,768]{1,0:T(8,128)(2,1)S(1)}, u32[]{:S(2)}, u32[]{:S(2)}) collective-permute-start(bf16[128,768]{1,0:T(8,128)(2,1)S(1)} %copy-done.3), channel_id=1, source_target_pairs={{0,1},{1,0},{2,3},{3,2},{4,5},{5,4},{6,7},{7,6},{8,9},{9,8},{10,11... | collective-permute-start | bytes 589832 | tf_op jit(solution)/shard_map/ppermute | solution.py:204
  34.5 0.8 shard_map.78
  35.3 0.6 collective-permute-done.1.b1
  35.9 9.2 %collective-permute-done.2.b2 = bf16[256,768]{1,0:T(8,128)(2,1)S(1)} collective-permute-done((bf16[256,768]{1,0:T(8,128)(2,1)S(1)}, bf16[256,768]{1,0:T(8,128)(2,1)S(1)}, u32[]{:S(2)}, u32[]{:S(2)}) %collective-permute-start.2) | collective-permute-done | bytes 393248 | tf_op jit(solution)/shard_map/ppermute | solution.py:184
  45.1 4.7 %collective-permute-start.4 = (bf16[128,768]{1,0:T(8,128)(2,1)S(1)}, bf16[128,768]{1,0:T(8,128)(2,1)S(1)}, u32[]{:S(2)}, u32[]{:S(2)}) collective-permute-start(bf16[128,768]{1,0:T(8,128)(2,1)S(1)} %collective-permute-done.b0), channel_id=1, source_target_pairs={{0,2},{2,4},{4,6},{6,0},{1,3},{3,5},{5,7},{7,1},{8,10},{10,12},{12... | collective-permute-start | bytes 589832 | tf_op jit(solution)/shard_map/ppermute | solution.py:184
  49.8 2.8 %collective-permute-start.5 = (bf16[128,768]{1,0:T(8,128)(2,1)S(1)}, bf16[128,768]{1,0:T(8,128)(2,1)S(1)}, u32[]{:S(2)}, u32[]{:S(2)}) collective-permute-start(bf16[128,768]{1,0:T(8,128)(2,1)S(1)} %collective-permute-done.b0), channel_id=1, source_target_pairs={{0,6},{2,0},{4,2},{6,4},{1,7},{3,1},{5,3},{7,5},{8,14},{10,8},{12,... | collective-permute-start | bytes 589832 | tf_op jit(solution)/shard_map/ppermute | solution.py:184
  52.5 3.4 %collective-permute-start.6 = (bf16[128,768]{1,0:T(8,128)(2,1)S(1)}, bf16[128,768]{1,0:T(8,128)(2,1)S(1)}, u32[]{:S(2)}, u32[]{:S(2)}) collective-permute-start(bf16[128,768]{1,0:T(8,128)(2,1)S(1)} %collective-permute-done.b0), channel_id=1, source_target_pairs={{0,4},{2,6},{4,0},{6,2},{1,5},{3,7},{5,1},{7,3},{8,12},{10,14},{12... | collective-permute-start | bytes 589832 | tf_op jit(solution)/shard_map/ppermute | solution.py:184
  55.9 4.3 %collective-permute-done.7.b0 = bf16[128,768]{1,0:T(8,128)(2,1)S(1)} collective-permute-done((bf16[128,768]{1,0:T(8,128)(2,1)S(1)}, bf16[128,768]{1,0:T(8,128)(2,1)S(1)}, u32[]{:S(2)}, u32[]{:S(2)}) %collective-permute-start.7) | collective-permute-done | bytes 196640 | tf_op jit(solution)/shard_map/ppermute | solution.py:204
  60.2 4.8 %collective-permute-start.10 = (bf16[128,768]{1,0:T(8,128)(2,1)S(1)}, bf16[128,768]{1,0:T(8,128)(2,1)S(1)}, u32[]{:S(2)}, u32[]{:S(2)}) collective-permute-start(bf16[128,768]{1,0:T(8,128)(2,1)S(1)} %collective-permute-done.7.b0), channel_id=1, source_target_pairs={{0,4},{2,6},{4,0},{6,2},{1,5},{3,7},{5,1},{7,3},{8,12},{10,14},{12... | collective-permute-start | bytes 589832 | tf_op jit(solution)/shard_map/ppermute | solution.py:184
  65.0 2.1 %collective-permute-start.8 = (bf16[128,768]{1,0:T(8,128)(2,1)S(1)}, bf16[128,768]{1,0:T(8,128)(2,1)S(1)}, u32[]{:S(2)}, u32[]{:S(2)}) collective-permute-start(bf16[128,768]{1,0:T(8,128)(2,1)S(1)} %collective-permute-done.7.b0), channel_id=1, source_target_pairs={{0,2},{2,4},{4,6},{6,0},{1,3},{3,5},{5,7},{7,1},{8,10},{10,12},{12... | collective-permute-start | bytes 589832 | tf_op jit(solution)/shard_map/ppermute | solution.py:184
  67.2 4.9 %collective-permute-start.9 = (bf16[128,768]{1,0:T(8,128)(2,1)S(1)}, bf16[128,768]{1,0:T(8,128)(2,1)S(1)}, u32[]{:S(2)}, u32[]{:S(2)}) collective-permute-start(bf16[128,768]{1,0:T(8,128)(2,1)S(1)} %collective-permute-done.7.b0), channel_id=1, source_target_pairs={{0,6},{2,0},{4,2},{6,4},{1,7},{3,1},{5,3},{7,5},{8,14},{10,8},{12,... | collective-permute-start | bytes 589832 | tf_op jit(solution)/shard_map/ppermute | solution.py:184
  73.4 1.6 %shard_map.79.total = f32[256,768]{1,0:T(8,128)S(1)} custom-call(f32[1]{0:T(128)S(6)} %copy.9.sharp, f32[1]{0:T(128)S(6)} %copy.10.offset, bf16[256,768]{1,0:T(8,128)(2,1)S(1)} %get-tuple-element.32.emb, bf16[256,768]{1,0:T(8,128)(2,1)S(1)} %copy-done.2, bf16[256,768]{1,0:T(8,128)(2,1)S(1)} %collective-permute-done.1.b1, ...), custom_call_target="tpu_custom_call" | custom-call | flops 805306368 | bytes 4000000 | tf_op jit(solution)/shard_map/pallas_call | solution.py:213
  75.0 1.0 shard_map.80.total
  76.0 1.1 shard_map.81
  77.2 1.9 %collective-permute-start.11 = (bf16[448,768]{1,0:T(8,128)(2,1)S(1)}, bf16[448,768]{1,0:T(8,128)(2,1)S(1)}, u32[]{:S(2)}, u32[]{:S(2)}) collective-permute-start(bf16[448,768]{1,0:T(8,128)(2,1)S(1)} %get-tuple-element.41), channel_id=1, source_target_pairs={{0,8},{8,0},{1,9},{9,1},{2,10},{10,2},{3,11},{11,3},{4,12},{12,4},... | collective-permute-start | bytes 2064392 | tf_op jit(solution)/shard_map/ppermute | solution.py:226
  79.1 1.5 %convolution_convert_fusion = bf16[256,1152]{1,0:T(8,128)(2,1)} fusion(bf16[256,768]{1,0:T(8,128)(2,1)S(1)} %get-tuple-element.42.raw, bf16[1152,768]{1,0:T(8,128)(2,1)S(1)} %copy-done), kind=kOutput, calls=%fused_computation.5 | convolution fusion | flops 453279744 | bytes 2752512 | tf_op jit(solution)/shard_map/dot_general | solution.py:227
  80.6 0.6 collective-permute-done.11.other
  81.2 1.6 %shard_map.82 = bf16[16,224,128]{2,1,0:T(8,128)(2,1)} custom-call(bf16[576,256]{1,0:T(8,128)(2,1)S(1)} %fusion.19.mine, bf16[256,768]{1,0:T(8,128)(2,1)S(1)} %get-tuple-element.42.raw, bf16[448,768]{1,0:T(8,128)(2,1)S(1)} %collective-permute-done.11.other), custom_call_target="tpu_custom_call" | custom-call | flops 452984832 | bytes 4000000 | tf_op jit(solution)/shard_map/pallas_call | solution.py:232
  82.8 6.9 %all-to-all-start = ((bf16[16,224,128]{2,1,0:T(8,128)(2,1)}), bf16[16,224,128]{2,1,0:T(8,128)(2,1)S(1)}, u32[]{:S(2)}, u32[]{:S(2)}) async-start(bf16[16,224,128]{2,1,0:T(8,128)(2,1)} %shard_map.82), calls=%async_computation | async-start | bytes 1835008 | tf_op jit(solution)/shard_map/all_to_all | solution.py:239
  89.8 16.2 %all-to-all-done = bf16[16,224,128]{2,1,0:T(8,128)(2,1)S(1)} async-done(((bf16[16,224,128]{2,1,0:T(8,128)(2,1)}), bf16[16,224,128]{2,1,0:T(8,128)(2,1)S(1)}, u32[]{:S(2)}, u32[]{:S(2)}) %all-to-all-start) | async-done | bytes 917536 | tf_op jit(solution)/shard_map/all_to_all | solution.py:239
  106.0 0.1 convert_reduce_fusion
  106.2 0.1 fusion.20
  106.3 0.1 convert_element_type.26
  106.4 19.6 %all_to_all.10.parts = bf16[16,18,96]{2,1,0:T(8,128)(2,1)S(1)} all-to-all(bf16[16,18,96]{2,1,0:T(8,128)(2,1)S(1)} %bitcast.6), channel_id=1, replica_groups=mesh['y'=4,'zl'=8,'c'=2,'x'=4,'zh'=2] {'zl','zh'}, dimensions={0} | all-to-all | bytes 110592 | tf_op jit(solution)/shard_map/all_to_all | solution.py:249
  126.0 0.6 shard_map.83
  (22 shorter events, 0.2 us)
Async XLA Ops:
  0.6 18.2 %copy-start.1 = (bf16[256,1152]{1,0:T(8,128)(2,1)S(1)}, bf16[256,1152]{1,0:T(8,128)(2,1)}, u32[]{:S(2)}) copy-start(bf16[256,1152]{1,0:T(8,128)(2,1)} %feats.2) | copy-start | bytes 1769476
  4.0 30.5 %collective-permute-start = (bf16[128,768]{1,0:T(8,128)(2,1)}, bf16[128,768]{1,0:T(8,128)(2,1)S(1)}, u32[]{:S(2)}, u32[]{:S(2)}) collective-permute-start(bf16[128,768]{1,0:T(8,128)(2,1)} %get-tuple-element.24), channel_id=1, source_target_pairs={{0,1},{1,0},{2,3},{3,2},{4,5},{5,4},{6,7},{7,6},{8,9},{9,8},{10,11... | collective-permute-start | bytes 589832 | tf_op jit(solution)/shard_map/ppermute | solution.py:186
  20.3 1.5 %copy-start.2 = (bf16[256,768]{1,0:T(8,128)(2,1)S(1)}, bf16[256,768]{1,0:T(8,128)(2,1)}, u32[]{:S(2)}) copy-start(bf16[256,768]{1,0:T(8,128)(2,1)} %get-tuple-element.31.b0) | copy-start | bytes 1179652
  20.3 12.3 %copy-start.3 = (bf16[128,768]{1,0:T(8,128)(2,1)S(1)}, bf16[128,768]{1,0:T(8,128)(2,1)}, u32[]{:S(2)}) copy-start(bf16[128,768]{1,0:T(8,128)(2,1)} %get-tuple-element.37) | copy-start | bytes 589828
  20.3 14.2 %copy-start = (bf16[1152,768]{1,0:T(8,128)(2,1)S(1)}, bf16[1152,768]{1,0:T(8,128)(2,1)}, u32[]{:S(2)}) copy-start(bf16[1152,768]{1,0:T(8,128)(2,1)} %head.3) | copy-start | bytes 5308420
  21.7 14.2 %collective-permute-start.1 = (bf16[256,768]{1,0:T(8,128)(2,1)S(1)}, bf16[256,768]{1,0:T(8,128)(2,1)S(1)}, u32[]{:S(2)}, u32[]{:S(2)}) collective-permute-start(bf16[256,768]{1,0:T(8,128)(2,1)S(1)} %copy-done.2), channel_id=1, source_target_pairs={{0,2},{2,4},{4,6},{6,0},{1,3},{3,5},{5,7},{7,1},{8,10},{10,12},{12... | collective-permute-start | bytes 1179656 | tf_op jit(solution)/shard_map/ppermute | solution.py:184
  25.1 19.9 %collective-permute-start.2 = (bf16[256,768]{1,0:T(8,128)(2,1)S(1)}, bf16[256,768]{1,0:T(8,128)(2,1)S(1)}, u32[]{:S(2)}, u32[]{:S(2)}) collective-permute-start(bf16[256,768]{1,0:T(8,128)(2,1)S(1)} %copy-done.2), channel_id=1, source_target_pairs={{0,6},{2,0},{4,2},{6,4},{1,7},{3,1},{5,3},{7,5},{8,14},{10,8},{12,... | collective-permute-start | bytes 1179656 | tf_op jit(solution)/shard_map/ppermute | solution.py:184
  28.8 16.2 %collective-permute-start.3 = (bf16[256,768]{1,0:T(8,128)(2,1)S(1)}, bf16[256,768]{1,0:T(8,128)(2,1)S(1)}, u32[]{:S(2)}, u32[]{:S(2)}) collective-permute-start(bf16[256,768]{1,0:T(8,128)(2,1)S(1)} %copy-done.2), channel_id=1, source_target_pairs={{0,4},{2,6},{4,0},{6,2},{1,5},{3,7},{5,1},{7,3},{8,12},{10,14},{12... | collective-permute-start | bytes 1179656 | tf_op jit(solution)/shard_map/ppermute | solution.py:184
  32.5 27.7 %collective-permute-start.7 = (bf16[128,768]{1,0:T(8,128)(2,1)S(1)}, bf16[128,768]{1,0:T(8,128)(2,1)S(1)}, u32[]{:S(2)}, u32[]{:S(2)}) collective-permute-start(bf16[128,768]{1,0:T(8,128)(2,1)S(1)} %copy-done.3), channel_id=1, source_target_pairs={{0,1},{1,0},{2,3},{3,2},{4,5},{5,4},{6,7},{7,6},{8,9},{9,8},{10,11... | collective-permute-start | bytes 589832 | tf_op jit(solution)/shard_map/ppermute | solution.py:204
  45.1 22.1 %collective-permute-start.4 = (bf16[128,768]{1,0:T(8,128)(2,1)S(1)}, bf16[128,768]{1,0:T(8,128)(2,1)S(1)}, u32[]{:S(2)}, u32[]{:S(2)}) collective-permute-start(bf16[128,768]{1,0:T(8,128)(2,1)S(1)} %collective-permute-done.b0), channel_id=1, source_target_pairs={{0,2},{2,4},{4,6},{6,0},{1,3},{3,5},{5,7},{7,1},{8,10},{10,12},{12... | collective-permute-start | bytes 589832 | tf_op jit(solution)/shard_map/ppermute | solution.py:184
  49.8 25.2 %collective-permute-start.5 = (bf16[128,768]{1,0:T(8,128)(2,1)S(1)}, bf16[128,768]{1,0:T(8,128)(2,1)S(1)}, u32[]{:S(2)}, u32[]{:S(2)}) collective-permute-start(bf16[128,768]{1,0:T(8,128)(2,1)S(1)} %collective-permute-done.b0), channel_id=1, source_target_pairs={{0,6},{2,0},{4,2},{6,4},{1,7},{3,1},{5,3},{7,5},{8,14},{10,8},{12,... | collective-permute-start | bytes 589832 | tf_op jit(solution)/shard_map/ppermute | solution.py:184
  52.5 22.5 %collective-permute-start.6 = (bf16[128,768]{1,0:T(8,128)(2,1)S(1)}, bf16[128,768]{1,0:T(8,128)(2,1)S(1)}, u32[]{:S(2)}, u32[]{:S(2)}) collective-permute-start(bf16[128,768]{1,0:T(8,128)(2,1)S(1)} %collective-permute-done.b0), channel_id=1, source_target_pairs={{0,4},{2,6},{4,0},{6,2},{1,5},{3,7},{5,1},{7,3},{8,12},{10,14},{12... | collective-permute-start | bytes 589832 | tf_op jit(solution)/shard_map/ppermute | solution.py:184
  60.2 15.8 %collective-permute-start.10 = (bf16[128,768]{1,0:T(8,128)(2,1)S(1)}, bf16[128,768]{1,0:T(8,128)(2,1)S(1)}, u32[]{:S(2)}, u32[]{:S(2)}) collective-permute-start(bf16[128,768]{1,0:T(8,128)(2,1)S(1)} %collective-permute-done.7.b0), channel_id=1, source_target_pairs={{0,4},{2,6},{4,0},{6,2},{1,5},{3,7},{5,1},{7,3},{8,12},{10,14},{12... | collective-permute-start | bytes 589832 | tf_op jit(solution)/shard_map/ppermute | solution.py:184
  65.0 11.0 %collective-permute-start.8 = (bf16[128,768]{1,0:T(8,128)(2,1)S(1)}, bf16[128,768]{1,0:T(8,128)(2,1)S(1)}, u32[]{:S(2)}, u32[]{:S(2)}) collective-permute-start(bf16[128,768]{1,0:T(8,128)(2,1)S(1)} %collective-permute-done.7.b0), channel_id=1, source_target_pairs={{0,2},{2,4},{4,6},{6,0},{1,3},{3,5},{5,7},{7,1},{8,10},{10,12},{12... | collective-permute-start | bytes 589832 | tf_op jit(solution)/shard_map/ppermute | solution.py:184
  67.2 8.9 %collective-permute-start.9 = (bf16[128,768]{1,0:T(8,128)(2,1)S(1)}, bf16[128,768]{1,0:T(8,128)(2,1)S(1)}, u32[]{:S(2)}, u32[]{:S(2)}) collective-permute-start(bf16[128,768]{1,0:T(8,128)(2,1)S(1)} %collective-permute-done.7.b0), channel_id=1, source_target_pairs={{0,6},{2,0},{4,2},{6,4},{1,7},{3,1},{5,3},{7,5},{8,14},{10,8},{12,... | collective-permute-start | bytes 589832 | tf_op jit(solution)/shard_map/ppermute | solution.py:184
  77.2 4.0 %collective-permute-start.11 = (bf16[448,768]{1,0:T(8,128)(2,1)S(1)}, bf16[448,768]{1,0:T(8,128)(2,1)S(1)}, u32[]{:S(2)}, u32[]{:S(2)}) collective-permute-start(bf16[448,768]{1,0:T(8,128)(2,1)S(1)} %get-tuple-element.41), channel_id=1, source_target_pairs={{0,8},{8,0},{1,9},{9,1},{2,10},{10,2},{3,11},{11,3},{4,12},{12,4},... | collective-permute-start | bytes 2064392 | tf_op jit(solution)/shard_map/ppermute | solution.py:226
  82.8 23.1 %all-to-all-start = ((bf16[16,224,128]{2,1,0:T(8,128)(2,1)}), bf16[16,224,128]{2,1,0:T(8,128)(2,1)S(1)}, u32[]{:S(2)}, u32[]{:S(2)}) async-start(bf16[16,224,128]{2,1,0:T(8,128)(2,1)} %shard_map.82), calls=%async_computation | async-start | bytes 1835008 | tf_op jit(solution)/shard_map/all_to_all | solution.py:239
